TPU v7x, 32 devices: a whole 2x2x4 slice. The times are simulated.
32 devices in a mesh: gz: 4 (over y, core), ta: 8 (over z, x).
Axes of the slice: x: 2, y: 2, z: 4, core: 2. Of those that a mesh axis runs over, the one named last changes fastest.
Arguments:
- volume: bfloat16 [24, 24, 40, 3072], P('gz', None, None, 'ta'), may hold values from -6 to 6
- sketch_matrix: bfloat16 [3072, 256], P('ta'), may hold values from -0.875 to 0.875
- brain_voxels: int32 [14336], P('gz'), may hold values from 0 to 5759, as said below
Outputs:
- sketch: float32 [14336, 256], P(('gz', 'ta'))
Inputs may be any that keep to these rules, and one draw needn't show every extreme that they name: `brain_voxels`: each slab's 3584 entries are distinct and increasing; the first is 0 and the last 5759.
All inputs are finite; a program needn't handle non-finite values.
Results may differ from a plain program's by a relative error of at most 0.0003.
Values may be sent and summed in bfloat16 or wider, within the bound.
No kernel may reach another device: no remote copies, remote signals or barrier semaphores. Data moves between devices by JAX's collectives and lax.ppermute only.
A program may use at most 64 MiB of HBM per device.

v0:
```python
import math

import jax
import jax.numpy as jnp
from jax import lax
from jax.sharding import PartitionSpec as P


def with_halo(shard, sides, width):
    for axis, dim in sides:
        peers, length = (lax.axis_size(axis), shard.shape[dim])
        up = [(i, (i + 1) % peers) for i in range(peers - 1)]
        down = [(j, i) for i, j in up]
        last = lax.slice_in_dim(shard, length - width, length, axis=dim)
        initial = lax.slice_in_dim(shard, 0, width, axis=dim)
        before = lax.ppermute(last, axis, up)
        after = lax.ppermute(initial, axis, down)
        shard = jnp.concatenate([before, shard, after], axis=dim)
    return shard


def kernel_taps():
    sigma = 3.0 / (2.0 * math.sqrt(2.0 * math.log(2.0)))
    raw_taps = [math.exp(-0.5 * (shift_k - 2) ** 2 / sigma**2) for shift_k in range(5)]
    summed = sum(raw_taps)
    return [value_k / summed for value_k in raw_taps]


def smooth_along(source, axis_num, kernel):
    extent = source.shape[axis_num]
    widths = [(0, 0)] * source.ndim
    widths[axis_num] = (2, 2)
    padded = jnp.pad(source, widths)
    summed = jnp.zeros_like(source)
    for shift_k in range(5):
        summed = summed + kernel[shift_k] * lax.slice_in_dim(
            padded, shift_k, shift_k + extent, axis=axis_num
        )
    return summed


def smooth_planes(padded, planes, kernel):
    summed = kernel[0] * padded[0:planes].astype(jnp.float32)
    for shift_k in range(1, 5):
        summed = summed + kernel[shift_k] * padded[shift_k : shift_k + planes].astype(jnp.float32)
    return summed


def shards(volume, sketch_matrix, brain_voxels):
    kernel = kernel_taps()
    planes, width_x, width_y, time_local = volume.shape
    slab_cells = planes * width_x * width_y
    weights = sketch_matrix.astype(jnp.float32)
    padded = with_halo(volume, (("gz", 0),), 2)
    signal = smooth_planes(padded, planes, kernel)
    signal = smooth_along(signal, 1, kernel)
    signal = smooth_along(signal, 2, kernel)
    picked = signal.reshape(slab_cells, time_local)[brain_voxels]
    return lax.psum_scatter(
        jnp.dot(
            picked, weights, precision=lax.Precision.HIGHEST, preferred_element_type=jnp.float32
        ),
        "ta",
        scatter_dimension=0,
        tiled=True,
    )


def solution(mesh):
    in_specs = (P("gz", None, None, "ta"), P("ta", None), P("gz"))
    out_specs = P(("gz", "ta"), None)
    return jax.shard_map(shards, mesh=mesh, in_specs=in_specs, out_specs=out_specs, check_vma=False)
```

profile of v0, /device:TPU:0, one launch (start us, length us, event | category | flops | bytes accessed | tf_op | source)
XLA Modules:
  0.0 163.0 jit_solution(7560657344698756646)
XLA Ops:
  6.5 0.0 copy-start
  6.5 0.0 reduce-scatter.2.cloned.1.call-start
  6.5 0.0 copy-start.1
  6.5 2.3 %fusion.16 = (bf16[2,24,40,384]{3,2,1,0:T(8,128)(2,1)S(1)}, bf16[2,24,40,384]{3,2,1,0:T(8,128)(2,1)S(1)}) fusion(bf16[6,24,40,384]{3,2,1,0:T(8,128)(2,1)} %param.3), kind=kLoop, calls=%fused_computation.32 | loop fusion | bytes 5898240 | tf_op jit(solution)/shard_map/slice | solution.py:14
  8.8 2.6 %collective-permute-start = (bf16[2,24,40,384]{3,2,1,0:T(8,128)(2,1)S(1)}, bf16[2,24,40,384]{3,2,1,0:T(8,128)(2,1)S(1)}, u32[]{:S(2)}, u32[]{:S(2)}) collective-permute-start(bf16[2,24,40,384]{3,2,1,0:T(8,128)(2,1)S(1)} %get-tuple-element.7), channel_id=1, source_target_pairs={{0,8},{8,16},{16,24},{1,9},{9,17},{17,25},{2,10},{10,18},{18,26},{... | collective-permute-start | bytes 4423688 | tf_op jit(solution)/shard_map/ppermute | solution.py:16
  11.4 1.3 collective-permute-start.1
  12.7 0.7 compare_select_fusion
  13.4 0.8 collective-permute-done
  14.2 1.3 constant_dynamic-update-slice_fusion.1
  15.5 0.0 copy-done.1
  15.5 2.9 %constant_dynamic-update-slice_fusion = (bf16[8,24,40,384]{3,2,1,0:T(8,128)(2,1)}, bf16[8,24,40,384]{3,2,1,0:T(8,128)(2,1)S(1)}) fusion(bf16[8,24,40,384]{3,2,1,0:T(8,128)(2,1)} %constant_dynamic-update-slice_fusion.1, bf16[6,24,40,384]{3,2,1,0:T(8,128)(2,1)S(1)} %copy-done.1), kind=kLoop, calls=%fused_computation.28 | loop fusion | bytes 13271040 | tf_op jit(solution)/shard_map/concatenate | solution.py:18
  18.3 0.3 collective-permute-done.1
  18.6 0.3 constant_dynamic-update-slice_fusion.2
  18.9 6.3 %multiply_add_fusion = f32[6,24,40,384]{3,2,1,0:T(8,128)S(1)} fusion(bf16[6,24,40,384]{3,2,1,0:T(8,128)(2,1)S(1)} %copy-done.1, bf16[8,24,40,384]{3,2,1,0:T(8,128)(2,1)S(1)} %constant_dynamic-update-slice_fusion.2, bf16[8,24,40,384]{3,2,1,0:T(8,128)(2,1)} %get-tuple-element.5), kind=kLoop, calls=%fused_computation.25 | loop fusion | flops 30965760 | bytes 30965760 | tf_op jit(solution)/shard_map/add | solution.py:45
  25.2 3.6 %fusion.4 = f32[6,24,40,384]{3,2,1,0:T(8,128)S(1)} fusion(f32[6,24,40,384]{3,2,1,0:T(8,128)S(1)} %multiply_add_fusion), kind=kLoop, calls=%fused_computation.13 | loop fusion | flops 19906560 | bytes 17694720 | tf_op jit(solution)/shard_map/add | solution.py:36
  28.8 6.8 %fusion.12 = f32[6,24,40,384]{3,2,1,0:T(8,128)} fusion(f32[6,24,40,384]{3,2,1,0:T(8,128)S(1)} %fusion.4), kind=kLoop, calls=%fused_computation.21 | loop fusion | flops 19906560 | bytes 17694720 | tf_op jit(solution)/shard_map/add | solution.py:36
  35.6 14.2 %gather_fusion = f32[3584,384]{1,0:T(8,128)} fusion(f32[5760,384]{1,0:T(8,128)} %bitcast.3, s32[4096]{0:T(1024)S(1)} %pad_clamp_fusion), kind=kCustom, calls=%fused_computation | custom fusion | bytes 11024384 | tf_op jit(solution)/shard_map/gather | solution.py:58
  49.8 0.0 copy-done
  49.8 7.5 %fusion.17 = f32[3584,256]{1,0:T(8,128)} fusion(f32[3584,384]{1,0:T(8,128)} %gather_fusion, bf16[384,256]{1,0:T(8,128)(2,1)S(1)} %copy-done), kind=kOutput, calls=%fused_computation.33 | convolution fusion | flops 4227858432 | bytes 9371648 | tf_op jit(solution)/shard_map/dot_general | solution.py:60
  57.3 0.0 reduce-scatter.2.cloned.1.call-update
  57.4 98.8 %reduce-scatter.2.cloned.1.call-done = f32[448,256]{1,0:T(8,128)} async-done(((f32[3584,256]{1,0:T(8,128)}), f32[448,256]{1,0:T(8,128)}) %reduce-scatter.2.cloned.1.call-update) | async-done | bytes 458768 | tf_op jit(solution)/shard_map/reduce_scatter | solution.py:59
  (1 shorter events, 0.0 us)
Async XLA Ops:
  6.5 43.3 %copy-start = (bf16[384,256]{1,0:T(8,128)(2,1)S(1)}, bf16[384,256]{1,0:T(8,128)(2,1)}, u32[]{:S(2)}) copy-start(bf16[384,256]{1,0:T(8,128)(2,1)} %param.4) | copy-start | bytes 589828
  6.5 149.6 %reduce-scatter.2.cloned.1.call-start = ((), (), s32[]{:S(2)}) async-start(), calls=%async_computation.1 | async-start | bytes 4128768 | tf_op jit(solution)/shard_map/reduce_scatter | solution.py:59
  6.5 8.9 %copy-start.1 = (bf16[6,24,40,384]{3,2,1,0:T(8,128)(2,1)S(1)}, bf16[6,24,40,384]{3,2,1,0:T(8,128)(2,1)}, u32[]{:S(2)}) copy-start(bf16[6,24,40,384]{3,2,1,0:T(8,128)(2,1)} %param.3) | copy-start | bytes 13271044
  8.8 5.4 %collective-permute-start = (bf16[2,24,40,384]{3,2,1,0:T(8,128)(2,1)S(1)}, bf16[2,24,40,384]{3,2,1,0:T(8,128)(2,1)S(1)}, u32[]{:S(2)}, u32[]{:S(2)}) collective-permute-start(bf16[2,24,40,384]{3,2,1,0:T(8,128)(2,1)S(1)} %get-tuple-element.7), channel_id=1, source_target_pairs={{0,8},{8,16},{16,24},{1,9},{9,17},{17,25},{2,10},{10,18},{18,26},{... | collective-permute-start | bytes 4423688 | tf_op jit(solution)/shard_map/ppermute | solution.py:16
  11.4 7.2 %collective-permute-start.1 = (bf16[2,24,40,384]{3,2,1,0:T(8,128)(2,1)S(1)}, bf16[2,24,40,384]{3,2,1,0:T(8,128)(2,1)S(1)}, u32[]{:S(2)}, u32[]{:S(2)}) collective-permute-start(bf16[2,24,40,384]{3,2,1,0:T(8,128)(2,1)S(1)} %get-tuple-element.8), channel_id=1, source_target_pairs={{8,0},{16,8},{24,16},{9,1},{17,9},{25,17},{10,2},{18,10},{26,18},{... | collective-permute-start | bytes 4423688 | tf_op jit(solution)/shard_map/ppermute | solution.py:17
Sparse Core Ops, SparseCore 0:
  57.5 98.6 reduce-scatter.1
where the time goes:
time: 163 us
  waiting for transfers between devices  99.9 us (61%)
  local copies, waits for them, and re-layouts  20.9 us (13%)
  other arithmetic  17.4 us (11%)
  between operations  13.4 us (8%)
  matrix products  7.48 us (5%)
  starting transfers between devices  3.88 us (2%)
    reduce_scatter x1, waiting for transfers between devices, shards(): lax.psum_scatter(jnp.dot(picked, weights, precision=lax.Precision.HIGHEST...  98.8 us
    gather x1, local copies, waits for them, and re-layouts, shards(): picked = signal.reshape(slab_cells, time_local)[brain_voxels]  14.2 us
    add x2, other arithmetic, smooth_along(): summed + kernel[shift_k] * lax.slice_in_dim(padded, shift_k, shift_k + ex...  10.4 us
    dot_general x1, matrix products, shards(): jnp.dot(picked, weights, precision=lax.Precision.HIGHEST, preferred_eleme...  7.48 us
    add x1, other arithmetic, smooth_planes(): summed + kernel[shift_k] * padded[shift_k:shift_k + planes].astype(jnp.fl...  6.33 us
  transfers between devices with their start and end apart: 3, of which 3 were waited for; matrix products, arithmetic and copies ran while one was open for 3% of the time, Pallas kernels for 0%

commit v1 on v0

v1 whole, which is shorter than its diff:
```python
import functools
import math

import jax
import jax.numpy as jnp
from jax import lax
from jax.experimental import pallas as pl
from jax.experimental.pallas import tpu as pltpu
from jax.sharding import PartitionSpec as P

LANES = 128
LEVELS = 32766.0
STEPS = 128.0
VMEM = pltpu.CompilerParams(vmem_limit_bytes=24 * 1024 * 1024)
F32 = jnp.float32
I16 = jnp.int16


def kernel_taps():
    sigma = 3.0 / (2.0 * math.sqrt(2.0 * math.log(2.0)))
    raw_taps = [math.exp(-0.5 * (shift_k - 2) ** 2 / sigma**2) for shift_k in range(5)]
    summed = sum(raw_taps)
    return [value_k / summed for value_k in raw_taps]


def pack_block(values, out, row):
    rows, cols = values.shape
    half = rows // 2
    codes = []
    for part in range(2):
        v = values[part * half : (part + 1) * half].reshape(half // 8, 8, cols)
        top = jnp.maximum(jnp.max(jnp.abs(v), axis=0), 1e-30)
        code = jnp.ceil(jnp.log2(top) * STEPS) + 1.0
        inverse = jnp.exp2(code * (-1.0 / STEPS)) * LEVELS
        q = jnp.round(v * inverse[None]).astype(jnp.int32)
        codes.append(code.astype(jnp.int32))
        out[row + part * half : row + (part + 1) * half, :] = q.reshape(half, cols).astype(I16)
    out[row + rows : row + rows + 16, :] = jnp.concatenate(codes, axis=0).astype(I16)


def unpack_scales(block, rows):
    codes = block[rows : rows + 16, :].astype(jnp.int32).astype(F32)
    return jnp.exp2(codes * (1.0 / STEPS)) * (1.0 / LEVELS)


def unpack_half(block, rows, part, scales):
    half = rows // 2
    q = block[part * half : (part + 1) * half, :].astype(jnp.int32).astype(F32)
    q = q.reshape(half // 8, 8, q.shape[-1]) * scales[part * 8 : part * 8 + 8][None]
    return q.reshape(half, q.shape[-1])


def edge_kernel(planes, cells, chunks, v_hbm, w_ref, *refs):
    outs, (buf, sem) = refs[: 2 * chunks], refs[2 * chunks :]
    odd = lax.axis_index("gz") % 2
    far = (planes - 2) * odd
    near = (planes - 2) * (1 - odd)
    copies = []
    for i, plane in enumerate((far, far + 1, near, near + 1)):
        rows = pl.ds(pl.multiple_of(plane * cells, cells), cells)
        copies.append(pltpu.make_async_copy(v_hbm.at[rows, :], buf.at[i], sem.at[i]))
        copies[-1].start()
    for i in range(4):
        copies[i].wait()
        product = jnp.dot(buf[i], w_ref[...], preferred_element_type=F32)
        for c in range(chunks):
            pack_block(
                product[:, c * LANES : (c + 1) * LANES],
                outs[2 * c + i // 2].at[i % 2],
                0,
            )


def slab_kernel(
    taps, shape, tile, share, chunk, v_hbm, w_ref, halo_ref, near_ref, bv_ref, first_ref,
    send_ref, keep_ref, buf, prod, pad, picked, sem,
):
    planes, width_x, width_y = shape
    cells = width_x * width_y
    blocks = send_ref.shape[0]
    window = tile + 8
    _, t1, t2 = taps[2], taps[1], taps[0]
    t0 = taps[2]
    copies = []
    for p in range(planes):
        rows = pl.ds(p * cells, cells)
        copies.append(pltpu.make_async_copy(v_hbm.at[rows, :], buf.at[p], sem.at[p]))
        copies[-1].start()
    odd = lax.axis_index("gz") % 2
    for ref, base in ((halo_ref, (planes + 2) * odd), (near_ref, (planes + 2) * (1 - odd))):
        for i in range(2):
            block = ref.at[i]
            scales = unpack_scales(block, cells)
            for part in range(2):
                half = cells // 2
                prod[base + i, part * half : (part + 1) * half, :] = unpack_half(
                    block, cells, part, scales
                )
    picked[...] = jnp.zeros_like(picked)
    pad[...] = jnp.zeros_like(pad)
    w = w_ref[:, chunk * LANES : (chunk + 1) * LANES]
    for p in range(planes):
        copies[p].wait()
        prod[p + 2] = jnp.dot(buf[p], w, preferred_element_type=F32)

    stride = width_y + 8
    per_tile = tile // width_y
    lane = lax.broadcasted_iota(jnp.int32, (window, LANES), 1)

    def plane_step(p, carry):
        def row(x):
            at = [prod[p + k, x * width_y : (x + 1) * width_y, :] for k in range(5)]
            return t0 * at[2] + t1 * (at[1] + at[3]) + t2 * (at[0] + at[4])

        zero = jnp.zeros((width_y, LANES), F32)
        win = [zero, zero, row(0), row(1)]
        for x in range(width_x):
            win.append(row(x + 2) if x + 2 < width_x else zero)
            value = t0 * win[2] + t1 * (win[1] + win[3]) + t2 * (win[0] + win[4])
            pad[8 + x * stride : 8 + x * stride + width_y, :] = value
            win = win[1:]
        for t in range(width_x // per_tile):
            rows = []
            for x in range(t * per_tile, (t + 1) * per_tile):
                at = [pad[6 + k + x * stride : 6 + k + x * stride + width_y, :] for k in range(5)]
                rows.append(t0 * at[2] + t1 * (at[1] + at[3]) + t2 * (at[0] + at[4]))
            value = jnp.concatenate(rows, axis=0)
            high = value.astype(jnp.bfloat16)
            low = (value - high.astype(F32)).astype(jnp.bfloat16)
            number = p * (width_x // per_tile) + t
            start = pl.multiple_of((first_ref[number] // 8) * 8, 8)
            voxel = bv_ref[pl.ds(start, window), :] - number * tile
            hits = []
            for left in range(0, tile, LANES):
                right = min(tile - left, LANES)
                hit = jnp.where(voxel == lane + left, 1.0, 0.0)
                hits.append(hit[:, :right].astype(jnp.bfloat16))
            choose = jnp.concatenate(hits, axis=1)
            both = jnp.concatenate([high, low], axis=1)
            out = jnp.dot(choose, both, preferred_element_type=F32)
            picked[pl.ds(start, window), :] += out[:, :LANES] + out[:, LANES:]
        return carry

    lax.fori_loop(0, planes, plane_step, 0)
    mine = lax.axis_index("ta") % 2
    for k in range(blocks):
        theirs_at = pl.multiple_of((2 * k + 1 - mine) * share, 8)
        mine_at = pl.multiple_of((2 * k + mine) * share, 8)
        pack_block(picked[pl.ds(theirs_at, share), :], send_ref.at[k], 0)
        keep_ref[k] = picked[pl.ds(mine_at, share), :]


def middle_kernel(share, got_ref, keep_ref, own_ref, *refs):
    msgs = refs
    blocks = got_ref.shape[0]
    z = lax.axis_index("ta") // 2

    def total(k):
        block = got_ref.at[k]
        scales = unpack_scales(block, share)
        rest = jnp.concatenate([unpack_half(block, share, part, scales) for part in range(2)], axis=0)
        return keep_ref[k] + rest

    own_ref[...] = total(z)
    for d in range(1, blocks):
        pack_block(total(z ^ d), msgs[d - 1], 0)


def last_kernel(share, chunks, blocks, *refs):
    out_ref = refs[-1]
    half = share // 2
    for c in range(chunks):
        own, msgs = refs[c * blocks], refs[c * blocks + 1 : (c + 1) * blocks]
        scales = [unpack_scales(m, share) for m in msgs]
        for part in range(2):
            rows = slice(part * half, (part + 1) * half)
            value = own[rows, :]
            for m, s in zip(msgs, scales):
                value = value + unpack_half(m, share, part, s)
            out_ref[rows, c * LANES : (c + 1) * LANES] = value


def shards(volume, sketch_matrix, brain_voxels):
    taps = kernel_taps()
    planes, width_x, width_y, time_local = volume.shape
    cells = width_x * width_y
    slab = planes * cells
    rank = sketch_matrix.shape[1]
    chunks = rank // LANES
    picks = brain_voxels.shape[0]
    n_gz, n_ta = lax.axis_size("gz"), lax.axis_size("ta")
    share = picks // n_ta
    blocks = n_ta // 2
    tile = 6 * width_y
    window = tile + 8
    tiles = slab // tile
    vmem = pl.BlockSpec(memory_space=pltpu.VMEM)
    smem = pl.BlockSpec(memory_space=pltpu.SMEM)
    hbm = pl.BlockSpec(memory_space=pl.ANY)
    flat = volume.reshape(slab, time_local)

    edge = pl.pallas_call(
        functools.partial(edge_kernel, planes, cells, chunks),
        out_shape=[jax.ShapeDtypeStruct((2, cells + 16, LANES), I16)] * (2 * chunks),
        in_specs=[hbm, vmem],
        out_specs=[vmem] * (2 * chunks),
        scratch_shapes=[
            pltpu.VMEM((4, cells, time_local), jnp.bfloat16),
            pltpu.SemaphoreType.DMA((4,)),
        ],
        compiler_params=VMEM,
        cost_estimate=pl.CostEstimate(
            flops=8 * cells * time_local * rank,
            bytes_accessed=8 * cells * (time_local + rank),
            transcendentals=0,
        ),
        name="edge_products",
    )(flat, sketch_matrix)

    even_pairs = [(i, i ^ 1) for i in range(n_gz)]
    odd_pairs = [(i, i + 1) for i in range(1, n_gz - 1, 2)]
    odd_pairs = odd_pairs + [(j, i) for i, j in odd_pairs]
    side = [(i, i ^ 1) for i in range(n_ta)]

    first = jnp.sum(
        brain_voxels[None, :] < (jnp.arange(tiles, dtype=jnp.int32) * tile)[:, None],
        axis=1,
        dtype=jnp.int32,
    )
    wide = jnp.broadcast_to(
        jnp.pad(brain_voxels, (0, window), constant_values=-1)[:, None], (picks + window, LANES)
    )

    results = []
    for c in range(chunks):
        halo = lax.ppermute(edge[2 * c], "gz", odd_pairs)
        near = lax.ppermute(edge[2 * c + 1], "gz", even_pairs)
        send, keep = pl.pallas_call(
            functools.partial(
                slab_kernel, taps, (planes, width_x, width_y), tile, share, c
            ),
            out_shape=[
                jax.ShapeDtypeStruct((blocks, share + 16, LANES), I16),
                jax.ShapeDtypeStruct((blocks, share, LANES), F32),
            ],
            in_specs=[hbm, vmem, vmem, vmem, vmem, smem],
            out_specs=[vmem, vmem],
            scratch_shapes=[
                pltpu.VMEM((planes, cells, time_local), jnp.bfloat16),
                pltpu.VMEM((planes + 4, cells, LANES), F32),
                pltpu.VMEM((width_x * (width_y + 8) + 8, LANES), F32),
                pltpu.VMEM((picks + window, LANES), F32),
                pltpu.SemaphoreType.DMA((planes,)),
            ],
            compiler_params=VMEM,
            cost_estimate=pl.CostEstimate(
                flops=2 * slab * LANES * (time_local + 2 * window),
                bytes_accessed=2 * slab * time_local + 2 * picks * LANES * 4,
                transcendentals=0,
            ),
            name="slab_rows",
        )(flat, sketch_matrix, halo, near, wide, first)
        got = lax.ppermute(send, "ta", side)
        mids = pl.pallas_call(
            functools.partial(middle_kernel, share),
            out_shape=[jax.ShapeDtypeStruct((share, LANES), F32)]
            + [jax.ShapeDtypeStruct((share + 16, LANES), I16)] * (blocks - 1),
            in_specs=[vmem, vmem],
            out_specs=[vmem] * blocks,
            compiler_params=VMEM,
            cost_estimate=pl.CostEstimate(
                flops=4 * picks * LANES, bytes_accessed=5 * picks * LANES, transcendentals=0
            ),
            name="middle_sums",
        )(got, keep)
        results.append(mids[0])
        for d in range(1, blocks):
            pairs = [(i, i ^ (2 * d)) for i in range(n_ta)]
            results.append(lax.ppermute(mids[d], "ta", pairs))

    return pl.pallas_call(
        functools.partial(last_kernel, share, chunks, blocks),
        out_shape=jax.ShapeDtypeStruct((share, rank), F32),
        in_specs=[vmem] * (chunks * blocks),
        out_specs=vmem,
        compiler_params=VMEM,
        name="last_sums",
    )(*results)


def solution(mesh):
    in_specs = (P("gz", None, None, "ta"), P("ta", None), P("gz"))
    out_specs = P(("gz", "ta"), None)
    return jax.shard_map(shards, mesh=mesh, in_specs=in_specs, out_specs=out_specs, check_vma=False)
```

time: 163 us -> 63.1 us (0.39)
  the two profiles are of different devices: /device:TPU:0 before, /device:TPU:1 now
where the time goes in v1:
time: 63.1 us; the launch traced here: 62.9 us
  Pallas kernels  25.7 us (41%)
  waiting for transfers between devices  17.4 us (28%)
  starting transfers between devices  15.7 us (25%)
  local copies, waits for them, and re-layouts  3.75 us (6%)
    pallas_call x2, Pallas kernels, shards(): pl.pallas_call(functools.partial(slab_kernel, taps, (planes, width_x, wid...  20 us
    ppermute x6, waiting for transfers between devices, shards(): results.append(lax.ppermute(mids[d], 'ta', pairs))  7.79 us
    ppermute x6, starting transfers between devices, shards(): results.append(lax.ppermute(mids[d], 'ta', pairs))  7.53 us
    ppermute x2, starting transfers between devices, shards(): halo = lax.ppermute(edge[2 * c], 'gz', odd_pairs)  6.46 us
    ppermute x2, waiting for transfers between devices, shards(): got = lax.ppermute(send, 'ta', side)  5.39 us
    ppermute x2, waiting for transfers between devices, shards(): halo = lax.ppermute(edge[2 * c], 'gz', odd_pairs)  4.25 us
    pallas_call x1, Pallas kernels, shards(): pl.pallas_call(functools.partial(edge_kernel, planes, cells, chunks), out...  4.22 us
    unnamed x6, local copies, waits for them, and re-layouts  3.18 us
  transfers between devices with their start and end apart: 12, of which 4 were waited for; matrix products, arithmetic and copies ran while one was open for 1% of the time, Pallas kernels for 33%

profile of v1, /device:TPU:1, one launch (start us, length us, event | category | flops | bytes accessed | tf_op | source)
XLA Modules:
  0.0 62.9 jit_solution(10826674786912863515)
XLA Ops:
  0.0 2.3 %copy-done = bf16[6,24,40,384]{3,2,1,0:T(8,128)(2,1)S(1)} copy-done((bf16[6,24,40,384]{3,2,1,0:T(8,128)(2,1)S(1)}, bf16[6,24,40,384]{3,2,1,0:T(8,128)(2,1)}, u32[]{:S(2)}) %copy-start) | copy-done | bytes 4423704
  2.3 0.9 %copy-done.1 = bf16[384,256]{1,0:T(8,128)(2,1)S(1)} copy-done((bf16[384,256]{1,0:T(8,128)(2,1)S(1)}, bf16[384,256]{1,0:T(8,128)(2,1)}, u32[]{:S(2)}) %copy-start.1) | copy-done | bytes 196632
  3.2 4.2 %edge_products.1 = (s16[2,976,128]{2,1,0:T(8,128)(2,1)S(1)}, s16[2,976,128]{2,1,0:T(8,128)(2,1)S(1)}, s16[2,976,128]{2,1,0:T(8,128)(2,1)S(1)}, s16[2,976,128]{2,1,0:T(8,128)(2,1)S(1)}) custom-call(bf16[5760,384]{1,0:T(8,128)(2,1)S(1)} %bitcast.1, bf16[384,256]{1,0:T(8,128)(2,1)S(1)} %copy-done.1), custom_call_target="tpu_custom_call" | custom-call | flops 754974720 | bytes 4915200 | tf_op jit(solution)/shard_map/edge_products/pallas_call | solution.py:202
  7.4 4.5 %collective-permute-start = (s16[2,976,128]{2,1,0:T(8,128)(2,1)S(1)}, s16[2,976,128]{2,1,0:T(8,128)(2,1)S(1)}, u32[]{:S(2)}, u32[]{:S(2)}) collective-permute-start(s16[2,976,128]{2,1,0:T(8,128)(2,1)S(1)} %get-tuple-element.21), channel_id=1, source_target_pairs={{8,16},{16,8},{9,17},{17,9},{10,18},{18,10},{11,19},{19,11},{12,20... | collective-permute-start | bytes 1499144 | tf_op jit(solution)/shard_map/ppermute | solution.py:236
  12.0 1.9 %collective-permute-start.6 = (s16[2,976,128]{2,1,0:T(8,128)(2,1)S(1)}, s16[2,976,128]{2,1,0:T(8,128)(2,1)S(1)}, u32[]{:S(2)}, u32[]{:S(2)}) collective-permute-start(s16[2,976,128]{2,1,0:T(8,128)(2,1)S(1)} %get-tuple-element.29), channel_id=1, source_target_pairs={{8,16},{16,8},{9,17},{17,9},{10,18},{18,10},{11,19},{19,11},{12,20... | collective-permute-start | bytes 1499144 | tf_op jit(solution)/shard_map/ppermute | solution.py:236
  14.0 0.1 collective-permute-start.7
  14.1 0.2 convert_reduce_fusion.first_ref
  14.3 4.2 %collective-permute-done.halo_ref = s16[2,976,128]{2,1,0:T(8,128)(2,1)S(1)} collective-permute-done((s16[2,976,128]{2,1,0:T(8,128)(2,1)S(1)}, s16[2,976,128]{2,1,0:T(8,128)(2,1)S(1)}, u32[]{:S(2)}, u32[]{:S(2)}) %collective-permute-start) | collective-permute-done | bytes 499744 | tf_op jit(solution)/shard_map/ppermute | solution.py:236
  18.6 0.6 broadcast_in_dim.2.bv_ref
  19.1 10.0 %slab_rows.2 = (s16[4,464,128]{2,1,0:T(8,128)(2,1)S(1)}, f32[4,448,128]{2,1,0:T(8,128)S(1)}) custom-call(bf16[5760,384]{1,0:T(8,128)(2,1)S(1)} %bitcast.2, bf16[384,256]{1,0:T(8,128)(2,1)S(1)} %copy-done.1, s16[2,976,128]{2,1,0:T(8,128)(2,1)S(1)} %collective-permute-done.halo_ref, s16[2,976,128]{2,1,0:T(8,128)(2,1)S(1)} %collective-permute-done.1.near_ref, ...), custom_call_target="tpu_custom_call" | custom-call | flops 1297612800 | bytes 8093696 | tf_op jit(solution)/shard_map/slab_rows/pallas_call | solution.py:238
  29.1 1.3 %collective-permute-start.2 = (s16[4,464,128]{2,1,0:T(8,128)(2,1)S(1)}, s16[4,464,128]{2,1,0:T(8,128)(2,1)S(1)}, u32[]{:S(2)}, u32[]{:S(2)}) collective-permute-start(s16[4,464,128]{2,1,0:T(8,128)(2,1)S(1)} %get-tuple-element.23), channel_id=1, source_target_pairs={{0,1},{1,0},{2,3},{3,2},{4,5},{5,4},{6,7},{7,6},{8,9},{9,8},{10,11... | collective-permute-start | bytes 1425416 | tf_op jit(solution)/shard_map/ppermute | solution.py:263
  30.4 10.0 %slab_rows.3 = (s16[4,464,128]{2,1,0:T(8,128)(2,1)S(1)}, f32[4,448,128]{2,1,0:T(8,128)S(1)}) custom-call(bf16[5760,384]{1,0:T(8,128)(2,1)S(1)} %bitcast.3, bf16[384,256]{1,0:T(8,128)(2,1)S(1)} %copy-done.1, s16[2,976,128]{2,1,0:T(8,128)(2,1)S(1)} %collective-permute-done.6.halo_ref, s16[2,976,128]{2,1,0:T(8,128)(2,1)S(1)} %collective-permute-done.7.near_ref, ...), custom_call_target="tpu_custom_call" | custom-call | flops 1297612800 | bytes 8093696 | tf_op jit(solution)/shard_map/slab_rows/pallas_call | solution.py:238
  40.4 0.3 collective-permute-start.8
  40.7 0.3 middle_sums.2
  41.0 1.4 %collective-permute-start.3 = (s16[464,128]{1,0:T(8,128)(2,1)S(1)}, s16[464,128]{1,0:T(8,128)(2,1)S(1)}, u32[]{:S(2)}, u32[]{:S(2)}) collective-permute-start(s16[464,128]{1,0:T(8,128)(2,1)S(1)} %get-tuple-element.26), channel_id=1, source_target_pairs={{0,2},{1,3},{2,0},{3,1},{4,6},{5,7},{6,4},{7,5},{8,10},{9,11},{10,... | collective-permute-start | bytes 356360 | tf_op jit(solution)/shard_map/ppermute | solution.py:279
  42.4 2.3 %collective-permute-start.4 = (s16[464,128]{1,0:T(8,128)(2,1)S(1)}, s16[464,128]{1,0:T(8,128)(2,1)S(1)}, u32[]{:S(2)}, u32[]{:S(2)}) collective-permute-start(s16[464,128]{1,0:T(8,128)(2,1)S(1)} %get-tuple-element.27), channel_id=1, source_target_pairs={{0,4},{1,5},{2,6},{3,7},{4,0},{5,1},{6,2},{7,3},{8,12},{9,13},{10,... | collective-permute-start | bytes 356360 | tf_op jit(solution)/shard_map/ppermute | solution.py:279
  44.7 5.4 %collective-permute-done.8.got_ref = s16[4,464,128]{2,1,0:T(8,128)(2,1)S(1)} collective-permute-done((s16[4,464,128]{2,1,0:T(8,128)(2,1)S(1)}, s16[4,464,128]{2,1,0:T(8,128)(2,1)S(1)}, u32[]{:S(2)}, u32[]{:S(2)}) %collective-permute-start.8) | collective-permute-done | bytes 475168 | tf_op jit(solution)/shard_map/ppermute | solution.py:263
  50.1 0.3 middle_sums.3
  50.3 1.6 %collective-permute-start.9 = (s16[464,128]{1,0:T(8,128)(2,1)S(1)}, s16[464,128]{1,0:T(8,128)(2,1)S(1)}, u32[]{:S(2)}, u32[]{:S(2)}) collective-permute-start(s16[464,128]{1,0:T(8,128)(2,1)S(1)} %get-tuple-element.34), channel_id=1, source_target_pairs={{0,2},{1,3},{2,0},{3,1},{4,6},{5,7},{6,4},{7,5},{8,10},{9,11},{10,... | collective-permute-start | bytes 356360 | tf_op jit(solution)/shard_map/ppermute | solution.py:279
  52.0 2.0 %collective-permute-start.10 = (s16[464,128]{1,0:T(8,128)(2,1)S(1)}, s16[464,128]{1,0:T(8,128)(2,1)S(1)}, u32[]{:S(2)}, u32[]{:S(2)}) collective-permute-start(s16[464,128]{1,0:T(8,128)(2,1)S(1)} %get-tuple-element.35), channel_id=1, source_target_pairs={{0,4},{1,5},{2,6},{3,7},{4,0},{5,1},{6,2},{7,3},{8,12},{9,13},{10,... | collective-permute-start | bytes 356360 | tf_op jit(solution)/shard_map/ppermute | solution.py:279
  54.0 0.2 collective-permute-start.11
  54.2 1.2 %collective-permute-done.9.refs_5_ = s16[464,128]{1,0:T(8,128)(2,1)S(1)} collective-permute-done((s16[464,128]{1,0:T(8,128)(2,1)S(1)}, s16[464,128]{1,0:T(8,128)(2,1)S(1)}, u32[]{:S(2)}, u32[]{:S(2)}) %collective-permute-start.9) | collective-permute-done | bytes 118816 | tf_op jit(solution)/shard_map/ppermute | solution.py:279
  55.4 6.6 %collective-permute-done.10.refs_6_ = s16[464,128]{1,0:T(8,128)(2,1)S(1)} collective-permute-done((s16[464,128]{1,0:T(8,128)(2,1)S(1)}, s16[464,128]{1,0:T(8,128)(2,1)S(1)}, u32[]{:S(2)}, u32[]{:S(2)}) %collective-permute-start.10) | collective-permute-done | bytes 118816 | tf_op jit(solution)/shard_map/ppermute | solution.py:279
  62.0 1.0 %last_sums.1 = f32[448,256]{1,0:T(8,128)} custom-call(f32[448,128]{1,0:T(8,128)S(1)} %get-tuple-element.25.refs_0_, s16[464,128]{1,0:T(8,128)(2,1)S(1)} %collective-permute-done.3.refs_1_, s16[464,128]{1,0:T(8,128)(2,1)S(1)} %collective-permute-done.4.refs_2_, s16[464,128]{1,0:T(8,128)(2,1)S(1)} %collective-permute-done.5.refs_3_, ...), custom_call_target="tpu_custom_call" | custom-call | tf_op jit(solution)/shard_map/last_sums/pallas_call | solution.py:281
  (16 shorter events, 0.1 us)
Async XLA Ops:
  0.0 2.3 %copy-start = (bf16[6,24,40,384]{3,2,1,0:T(8,128)(2,1)S(1)}, bf16[6,24,40,384]{3,2,1,0:T(8,128)(2,1)}, u32[]{:S(2)}) copy-start(bf16[6,24,40,384]{3,2,1,0:T(8,128)(2,1)} %param.3) | copy-start | bytes 13271044
  2.3 0.9 %copy-start.1 = (bf16[384,256]{1,0:T(8,128)(2,1)S(1)}, bf16[384,256]{1,0:T(8,128)(2,1)}, u32[]{:S(2)}) copy-start(bf16[384,256]{1,0:T(8,128)(2,1)} %w_ref.5) | copy-start | bytes 589828
  3.2 10.9 %copy-start.2 = (s32[3584]{0:T(1024)S(1)}, s32[3584]{0:T(1024)}, u32[]{:S(2)}) copy-start(s32[3584]{0:T(1024)} %param.5) | copy-start | bytes 43012
  7.4 11.1 %collective-permute-start = (s16[2,976,128]{2,1,0:T(8,128)(2,1)S(1)}, s16[2,976,128]{2,1,0:T(8,128)(2,1)S(1)}, u32[]{:S(2)}, u32[]{:S(2)}) collective-permute-start(s16[2,976,128]{2,1,0:T(8,128)(2,1)S(1)} %get-tuple-element.21), channel_id=1, source_target_pairs={{8,16},{16,8},{9,17},{17,9},{10,18},{18,10},{11,19},{19,11},{12,20... | collective-permute-start | bytes 1499144 | tf_op jit(solution)/shard_map/ppermute | solution.py:236
  12.0 6.6 %collective-permute-start.1 = (s16[2,976,128]{2,1,0:T(8,128)(2,1)S(1)}, s16[2,976,128]{2,1,0:T(8,128)(2,1)S(1)}, u32[]{:S(2)}, u32[]{:S(2)}) collective-permute-start(s16[2,976,128]{2,1,0:T(8,128)(2,1)S(1)} %get-tuple-element.22), channel_id=1, source_target_pairs={{0,8},{8,0},{16,24},{24,16},{1,9},{9,1},{17,25},{25,17},{2,10},{10... | collective-permute-start | bytes 1499144 | tf_op jit(solution)/shard_map/ppermute | solution.py:237
  12.0 18.4 %collective-permute-start.6 = (s16[2,976,128]{2,1,0:T(8,128)(2,1)S(1)}, s16[2,976,128]{2,1,0:T(8,128)(2,1)S(1)}, u32[]{:S(2)}, u32[]{:S(2)}) collective-permute-start(s16[2,976,128]{2,1,0:T(8,128)(2,1)S(1)} %get-tuple-element.29), channel_id=1, source_target_pairs={{8,16},{16,8},{9,17},{17,9},{10,18},{18,10},{11,19},{19,11},{12,20... | collective-permute-start | bytes 1499144 | tf_op jit(solution)/shard_map/ppermute | solution.py:236
  14.0 16.4 %collective-permute-start.7 = (s16[2,976,128]{2,1,0:T(8,128)(2,1)S(1)}, s16[2,976,128]{2,1,0:T(8,128)(2,1)S(1)}, u32[]{:S(2)}, u32[]{:S(2)}) collective-permute-start(s16[2,976,128]{2,1,0:T(8,128)(2,1)S(1)} %get-tuple-element.30), channel_id=1, source_target_pairs={{0,8},{8,0},{16,24},{24,16},{1,9},{9,1},{17,25},{25,17},{2,10},{10... | collective-permute-start | bytes 1499144 | tf_op jit(solution)/shard_map/ppermute | solution.py:237
  29.1 11.6 %collective-permute-start.2 = (s16[4,464,128]{2,1,0:T(8,128)(2,1)S(1)}, s16[4,464,128]{2,1,0:T(8,128)(2,1)S(1)}, u32[]{:S(2)}, u32[]{:S(2)}) collective-permute-start(s16[4,464,128]{2,1,0:T(8,128)(2,1)S(1)} %get-tuple-element.23), channel_id=1, source_target_pairs={{0,1},{1,0},{2,3},{3,2},{4,5},{5,4},{6,7},{7,6},{8,9},{9,8},{10,11... | collective-permute-start | bytes 1425416 | tf_op jit(solution)/shard_map/ppermute | solution.py:263
  40.4 9.6 %collective-permute-start.8 = (s16[4,464,128]{2,1,0:T(8,128)(2,1)S(1)}, s16[4,464,128]{2,1,0:T(8,128)(2,1)S(1)}, u32[]{:S(2)}, u32[]{:S(2)}) collective-permute-start(s16[4,464,128]{2,1,0:T(8,128)(2,1)S(1)} %get-tuple-element.31), channel_id=1, source_target_pairs={{0,1},{1,0},{2,3},{3,2},{4,5},{5,4},{6,7},{7,6},{8,9},{9,8},{10,11... | collective-permute-start | bytes 1425416 | tf_op jit(solution)/shard_map/ppermute | solution.py:263
  41.0 13.0 %collective-permute-start.3 = (s16[464,128]{1,0:T(8,128)(2,1)S(1)}, s16[464,128]{1,0:T(8,128)(2,1)S(1)}, u32[]{:S(2)}, u32[]{:S(2)}) collective-permute-start(s16[464,128]{1,0:T(8,128)(2,1)S(1)} %get-tuple-element.26), channel_id=1, source_target_pairs={{0,2},{1,3},{2,0},{3,1},{4,6},{5,7},{6,4},{7,5},{8,10},{9,11},{10,... | collective-permute-start | bytes 356360 | tf_op jit(solution)/shard_map/ppermute | solution.py:279
  42.4 11.8 %collective-permute-start.4 = (s16[464,128]{1,0:T(8,128)(2,1)S(1)}, s16[464,128]{1,0:T(8,128)(2,1)S(1)}, u32[]{:S(2)}, u32[]{:S(2)}) collective-permute-start(s16[464,128]{1,0:T(8,128)(2,1)S(1)} %get-tuple-element.27), channel_id=1, source_target_pairs={{0,4},{1,5},{2,6},{3,7},{4,0},{5,1},{6,2},{7,3},{8,12},{9,13},{10,... | collective-permute-start | bytes 356360 | tf_op jit(solution)/shard_map/ppermute | solution.py:279
  44.7 9.5 %collective-permute-start.5 = (s16[464,128]{1,0:T(8,128)(2,1)S(1)}, s16[464,128]{1,0:T(8,128)(2,1)S(1)}, u32[]{:S(2)}, u32[]{:S(2)}) collective-permute-start(s16[464,128]{1,0:T(8,128)(2,1)S(1)} %get-tuple-element.28), channel_id=1, source_target_pairs={{0,6},{1,7},{2,4},{3,5},{4,2},{5,3},{6,0},{7,1},{8,14},{9,15},{10,... | collective-permute-start | bytes 356360 | tf_op jit(solution)/shard_map/ppermute | solution.py:279
  50.3 5.0 %collective-permute-start.9 = (s16[464,128]{1,0:T(8,128)(2,1)S(1)}, s16[464,128]{1,0:T(8,128)(2,1)S(1)}, u32[]{:S(2)}, u32[]{:S(2)}) collective-permute-start(s16[464,128]{1,0:T(8,128)(2,1)S(1)} %get-tuple-element.34), channel_id=1, source_target_pairs={{0,2},{1,3},{2,0},{3,1},{4,6},{5,7},{6,4},{7,5},{8,10},{9,11},{10,... | collective-permute-start | bytes 356360 | tf_op jit(solution)/shard_map/ppermute | solution.py:279
  52.0 10.0 %collective-permute-start.10 = (s16[464,128]{1,0:T(8,128)(2,1)S(1)}, s16[464,128]{1,0:T(8,128)(2,1)S(1)}, u32[]{:S(2)}, u32[]{:S(2)}) collective-permute-start(s16[464,128]{1,0:T(8,128)(2,1)S(1)} %get-tuple-element.35), channel_id=1, source_target_pairs={{0,4},{1,5},{2,6},{3,7},{4,0},{5,1},{6,2},{7,3},{8,12},{9,13},{10,... | collective-permute-start | bytes 356360 | tf_op jit(solution)/shard_map/ppermute | solution.py:279
  54.0 8.0 %collective-permute-start.11 = (s16[464,128]{1,0:T(8,128)(2,1)S(1)}, s16[464,128]{1,0:T(8,128)(2,1)S(1)}, u32[]{:S(2)}, u32[]{:S(2)}) collective-permute-start(s16[464,128]{1,0:T(8,128)(2,1)S(1)} %get-tuple-element.36), channel_id=1, source_target_pairs={{0,6},{1,7},{2,4},{3,5},{4,2},{5,3},{6,0},{7,1},{8,14},{9,15},{10,... | collective-permute-start | bytes 356360 | tf_op jit(solution)/shard_map/ppermute | solution.py:279

commit v2 on v1

v2 whole, which is shorter than its diff:
```python
import functools
import math

import jax
import jax.numpy as jnp
from jax import lax
from jax.experimental import pallas as pl
from jax.experimental.pallas import tpu as pltpu
from jax.sharding import PartitionSpec as P

LANES = 128
LEVELS = 32766.0
STEPS = 128.0
VMEM = pltpu.CompilerParams(vmem_limit_bytes=24 * 1024 * 1024)
F32 = jnp.float32
I16 = jnp.int16


def kernel_taps():
    sigma = 3.0 / (2.0 * math.sqrt(2.0 * math.log(2.0)))
    raw_taps = [math.exp(-0.5 * (shift_k - 2) ** 2 / sigma**2) for shift_k in range(5)]
    summed = sum(raw_taps)
    return [value_k / summed for value_k in raw_taps]


def pack_block(values, out, row):
    rows, cols = values.shape
    half = rows // 2
    codes = []
    for part in range(2):
        v = values[part * half : (part + 1) * half].reshape(half // 8, 8, cols)
        top = jnp.maximum(jnp.max(jnp.abs(v), axis=0), 1e-30)
        code = jnp.ceil(jnp.log2(top) * STEPS) + 1.0
        inverse = jnp.exp2(code * (-1.0 / STEPS)) * LEVELS
        q = jnp.round(v * inverse[None]).astype(jnp.int32)
        codes.append(code.astype(jnp.int32))
        out[row + part * half : row + (part + 1) * half, :] = q.reshape(half, cols).astype(I16)
    out[row + rows : row + rows + 16, :] = jnp.concatenate(codes, axis=0).astype(I16)


def unpack_scales(block, rows):
    codes = block[rows : rows + 16, :].astype(jnp.int32).astype(F32)
    return jnp.exp2(codes * (1.0 / STEPS)) * (1.0 / LEVELS)


def unpack_half(block, rows, part, scales):
    half = rows // 2
    q = block[part * half : (part + 1) * half, :].astype(jnp.int32).astype(F32)
    q = q.reshape(half // 8, 8, q.shape[-1]) * scales[part * 8 : part * 8 + 8][None]
    return q.reshape(half, q.shape[-1])


def product_kernel(first, cells, chunks, v_hbm, w_hbm, *refs):
    starts = first(lax.axis_index("gz") % 2)
    scratch = refs[-4:]
    buf, wbuf, sem, wsem = scratch
    refs = refs[:-4]
    msgs, prods = refs[-2 * chunks : -chunks], refs[-chunks:]
    load_w = pltpu.make_async_copy(w_hbm, wbuf, wsem.at[0])
    load_w.start()
    copies, planes = [], []
    for pair, start in enumerate(starts):
        for i in range(2):
            plane = start + i
            rows = pl.ds(pl.multiple_of(plane * cells, cells), cells)
            number = 2 * pair + i
            copies.append(pltpu.make_async_copy(v_hbm.at[rows, :], buf.at[number], sem.at[number]))
            copies[-1].start()
            planes.append(plane)
    load_w.wait()
    for i, plane in enumerate(planes):
        copies[i].wait()
        product = jnp.dot(buf[i], wbuf[...], preferred_element_type=F32)
        for c in range(chunks):
            part = product[:, c * LANES : (c + 1) * LANES]
            prods[c][plane] = part
            if i < 2:
                pack_block(part, msgs[c].at[i], 0)


def slab_kernel(
    ratios, shape, tile, share, prod, halo_ref, near_ref, bv_ref, first_ref,
    send_ref, keep_ref, ext, pad, picked,
):
    planes, width_x, width_y = shape
    cells = width_x * width_y
    blocks = send_ref.shape[0]
    window = tile + 8
    r1, r2 = ratios
    odd = lax.axis_index("gz") % 2
    half = cells // 2
    for ref, base in ((halo_ref, 2 * odd), (near_ref, 2 * (1 - odd))):
        for i in range(2):
            block = ref.at[i]
            scales = unpack_scales(block, cells)
            for part in range(2):
                ext[base + i, part * half : (part + 1) * half, :] = unpack_half(
                    block, cells, part, scales
                )
    stride = width_y + 8
    for side in range(2):
        for x in range(width_x + 1):
            pad[side, x * stride : x * stride + 8, :] = jnp.zeros((8, LANES), F32)
    picked[0:8, :] = jnp.zeros((8, LANES), F32)
    per_tile = tile // width_y
    lane = lax.broadcasted_iota(jnp.int32, (window, LANES), 1)

    def blur(at):
        return at[2] + r1 * (at[1] + at[3]) + r2 * (at[0] + at[4])

    def source(p, rows):
        if p < 0:
            return ext[p + 2, rows, :]
        if p >= planes:
            return ext[p - planes + 2, rows, :]
        return prod[p, rows, :]

    for p in range(planes):
        side = p % 2

        def row(x):
            rows = slice(x * width_y, (x + 1) * width_y)
            return blur([source(p + k - 2, rows) for k in range(5)])

        zero = jnp.zeros((width_y, LANES), F32)
        win = [zero, zero, row(0), row(1)]
        for x in range(width_x):
            win.append(row(x + 2) if x + 2 < width_x else zero)
            pad[side, 8 + x * stride : 8 + x * stride + width_y, :] = blur(win)
            win = win[1:]
        found = []
        for t in range(width_x // per_tile):
            rows = []
            for x in range(t * per_tile, (t + 1) * per_tile):
                base = 6 + x * stride
                rows.append(blur([pad[side, base + k : base + k + width_y, :] for k in range(5)]))
            value = jnp.concatenate(rows, axis=0)
            high = value.astype(jnp.bfloat16)
            low = (value - high.astype(F32)).astype(jnp.bfloat16)
            number = p * (width_x // per_tile) + t
            start = pl.multiple_of((first_ref[number] // 8) * 8, 8)
            voxel = bv_ref[pl.ds(start, window), :]
            hits = []
            for left in range(0, tile, LANES):
                right = min(tile - left, LANES)
                hit = jnp.where(voxel == lane + (left + number * tile), 1.0, 0.0)
                hits.append(hit[:, :right].astype(jnp.bfloat16))
            choose = jnp.concatenate(hits, axis=1)
            both = jnp.concatenate([high, low], axis=1)
            out = jnp.dot(choose, both, preferred_element_type=F32)
            found.append((start, out[:, :LANES] + out[:, LANES:]))
        for start, out in found:
            picked[pl.ds(start, 8), :] += out[:8]
            picked[pl.ds(pl.multiple_of(start + 8, 8), window - 8), :] = out[8:]

    mine = lax.axis_index("ta") % 2
    for k in range(blocks):
        theirs_at = pl.multiple_of((2 * k + 1 - mine) * share, 8)
        mine_at = pl.multiple_of((2 * k + mine) * share, 8)
        pack_block(picked[pl.ds(theirs_at, share), :], send_ref.at[k], 0)
        keep_ref[k] = picked[pl.ds(mine_at, share), :]


def middle_kernel(share, got_ref, keep_ref, own_ref, *refs):
    msgs = refs
    blocks = got_ref.shape[0]
    z = lax.axis_index("ta") // 2

    def total(k):
        block = got_ref.at[k]
        scales = unpack_scales(block, share)
        rest = jnp.concatenate([unpack_half(block, share, part, scales) for part in range(2)], axis=0)
        return keep_ref[k] + rest

    own_ref[...] = total(z)
    for d in range(1, blocks):
        pack_block(total(z ^ d), msgs[d - 1], 0)


def last_kernel(scale, share, chunks, blocks, *refs):
    out_ref = refs[-1]
    half = share // 2
    for c in range(chunks):
        own, msgs = refs[c * blocks], refs[c * blocks + 1 : (c + 1) * blocks]
        scales = [unpack_scales(m, share) for m in msgs]
        for part in range(2):
            rows = slice(part * half, (part + 1) * half)
            value = own[rows, :]
            for m, s in zip(msgs, scales):
                value = value + unpack_half(m, share, part, s)
            out_ref[rows, c * LANES : (c + 1) * LANES] = value * scale


def shards(volume, sketch_matrix, brain_voxels):
    taps = kernel_taps()
    ratios = (taps[1] / taps[2], taps[0] / taps[2])
    planes, width_x, width_y, time_local = volume.shape
    cells = width_x * width_y
    slab = planes * cells
    rank = sketch_matrix.shape[1]
    chunks = rank // LANES
    picks = brain_voxels.shape[0]
    n_gz, n_ta = lax.axis_size("gz"), lax.axis_size("ta")
    share = picks // n_ta
    blocks = n_ta // 2
    tile = 6 * width_y
    window = tile + 8
    tiles = slab // tile
    vmem = pl.BlockSpec(memory_space=pltpu.VMEM)
    smem = pl.BlockSpec(memory_space=pltpu.SMEM)
    hbm = pl.BlockSpec(memory_space=pltpu.HBM)
    flat = volume.reshape(slab, time_local)

    def products(first, pairs, held):
        names = [jax.ShapeDtypeStruct((2, cells + 16, LANES), I16)] * chunks
        names += [jax.ShapeDtypeStruct((planes, cells, LANES), F32)] * chunks
        out = pl.pallas_call(
            functools.partial(product_kernel, first, cells, chunks),
            out_shape=names,
            in_specs=[hbm, hbm] + [hbm] * len(held),
            out_specs=[vmem] * (2 * chunks),
            input_output_aliases={2 + i: chunks + i for i in range(len(held))},
            scratch_shapes=[
                pltpu.VMEM((2 * pairs, cells, time_local), jnp.bfloat16),
                pltpu.VMEM((time_local, rank), jnp.bfloat16),
                pltpu.SemaphoreType.DMA((2 * pairs,)),
                pltpu.SemaphoreType.DMA((1,)),
            ],
            compiler_params=VMEM,
            cost_estimate=pl.CostEstimate(
                flops=4 * pairs * cells * time_local * rank,
                bytes_accessed=4 * pairs * cells * time_local,
                transcendentals=0,
            ),
        )(pltpu.with_memory_space_constraint(flat, pltpu.HBM), pltpu.with_memory_space_constraint(sketch_matrix, pltpu.HBM), *held)
        return out[:chunks], out[chunks:]

    far, prods = products(lambda odd: [(planes - 2) * odd], 1, [])
    middle = list(range(2, planes - 2, 2))
    near, prods = products(lambda odd: [(planes - 2) * (1 - odd)] + middle, 1 + len(middle), prods)

    even_pairs = [(i, i ^ 1) for i in range(n_gz)]
    odd_pairs = [(i, i + 1) for i in range(1, n_gz - 1, 2)]
    odd_pairs = odd_pairs + [(j, i) for i, j in odd_pairs]
    side = [(i, i ^ 1) for i in range(n_ta)]

    first = jnp.sum(
        brain_voxels[None, :] < (jnp.arange(tiles, dtype=jnp.int32) * tile)[:, None],
        axis=1,
        dtype=jnp.int32,
    )
    wide = jnp.broadcast_to(
        jnp.pad(brain_voxels, (0, window), constant_values=-1)[:, None], (picks + window, LANES)
    )

    results = []
    for c in range(chunks):
        halo = lax.ppermute(far[c], "gz", odd_pairs)
        beside = lax.ppermute(near[c], "gz", even_pairs)
        send, keep = pl.pallas_call(
            functools.partial(slab_kernel, ratios, (planes, width_x, width_y), tile, share),
            out_shape=[
                jax.ShapeDtypeStruct((blocks, share + 16, LANES), I16),
                jax.ShapeDtypeStruct((blocks, share, LANES), F32),
            ],
            in_specs=[vmem, vmem, vmem, vmem, smem],
            out_specs=[vmem, vmem],
            scratch_shapes=[
                pltpu.VMEM((4, cells, LANES), F32),
                pltpu.VMEM((2, width_x * (width_y + 8) + 8, LANES), F32),
                pltpu.VMEM((picks + window, LANES), F32),
            ],
            compiler_params=VMEM,
            cost_estimate=pl.CostEstimate(
                flops=4 * slab * LANES * window,
                bytes_accessed=4 * slab * LANES + 8 * picks * LANES,
                transcendentals=0,
            ),
            name="slab_rows",
        )(prods[c], halo, beside, wide, first)
        got = lax.ppermute(send, "ta", side)
        mids = pl.pallas_call(
            functools.partial(middle_kernel, share),
            out_shape=[jax.ShapeDtypeStruct((share, LANES), F32)]
            + [jax.ShapeDtypeStruct((share + 16, LANES), I16)] * (blocks - 1),
            in_specs=[vmem, vmem],
            out_specs=[vmem] * blocks,
            compiler_params=VMEM,
            cost_estimate=pl.CostEstimate(
                flops=4 * picks * LANES, bytes_accessed=5 * picks * LANES, transcendentals=0
            ),
            name="middle_sums",
        )(got, keep)
        results.append(mids[0])
        for d in range(1, blocks):
            pairs = [(i, i ^ (2 * d)) for i in range(n_ta)]
            results.append(lax.ppermute(mids[d], "ta", pairs))

    return pl.pallas_call(
        functools.partial(last_kernel, taps[2] ** 3, share, chunks, blocks),
        out_shape=jax.ShapeDtypeStruct((share, rank), F32),
        in_specs=[vmem] * (chunks * blocks),
        out_specs=vmem,
        compiler_params=VMEM,
        name="last_sums",
    )(*results)


def solution(mesh):
    in_specs = (P("gz", None, None, "ta"), P("ta", None), P("gz"))
    out_specs = P(("gz", "ta"), None)
    return jax.shard_map(shards, mesh=mesh, in_specs=in_specs, out_specs=out_specs, check_vma=False)
```

time: 63.1 us -> 56.3 us (0.89)
  the two profiles are of different devices: /device:TPU:1 before, /device:TPU:28 now
where the time goes in v2:
time: 56.3 us; the launch traced here: 56.1 us
  waiting for transfers between devices  25.1 us (45%)
  Pallas kernels  17.7 us (31%)
  starting transfers between devices  12.4 us (22%)
  local copies, waits for them, and re-layouts  0.57 us (1%)
    ppermute x6, waiting for transfers between devices, shards(): results.append(lax.ppermute(mids[d], 'ta', pairs))  13.7 us
    pallas_call x2, Pallas kernels, shards(): pl.pallas_call(functools.partial(slab_kernel, ratios, (planes, width_x, w...  9.36 us
    ppermute x2, waiting for transfers between devices, shards(): got = lax.ppermute(send, 'ta', side)  7.26 us
    pallas_call x2, Pallas kernels, products(): pl.pallas_call(functools.partial(product_kernel, first, cells, chunks), o...  6.8 us
    ppermute x2, starting transfers between devices, shards(): halo = lax.ppermute(far[c], 'gz', odd_pairs)  5.74 us
    ppermute x6, starting transfers between devices, shards(): results.append(lax.ppermute(mids[d], 'ta', pairs))  4.4 us
    ppermute x2, waiting for transfers between devices, shards(): halo = lax.ppermute(far[c], 'gz', odd_pairs)  4.14 us
    ppermute x2, starting transfers between devices, shards(): got = lax.ppermute(send, 'ta', side)  2.16 us
  transfers between devices with their start and end apart: 12, of which 6 were waited for; matrix products, arithmetic and copies ran while one was open for 1% of the time, Pallas kernels for 18%

profile of v2, /device:TPU:28, one launch (start us, length us, event | category | flops | bytes accessed | tf_op | source)
XLA Modules:
  0.0 56.1 jit_solution(16633471337123607089)
XLA Ops:
  0.0 2.7 %shard_map.37 = (s16[2,976,128]{2,1,0:T(8,128)(2,1)S(1)}, s16[2,976,128]{2,1,0:T(8,128)(2,1)S(1)}, f32[6,960,128]{2,1,0:T(8,128)S(1)}, f32[6,960,128]{2,1,0:T(8,128)S(1)}) custom-call(bf16[5760,384]{1,0:T(8,128)(2,1)} %bitcast.1, bf16[384,256]{1,0:T(8,128)(2,1)} %w_hbm.3), custom_call_target="tpu_custom_call" | custom-call | flops 377487360 | bytes 1474560 | tf_op jit(solution)/shard_map/pallas_call | solution.py:217
  2.7 4.1 %shard_map.38 = (s16[2,976,128]{2,1,0:T(8,128)(2,1)S(1)}, s16[2,976,128]{2,1,0:T(8,128)(2,1)S(1)}, f32[6,960,128]{2,1,0:T(8,128)S(1)}, f32[6,960,128]{2,1,0:T(8,128)S(1)}) custom-call(bf16[5760,384]{1,0:T(8,128)(2,1)} %bitcast.2, bf16[384,256]{1,0:T(8,128)(2,1)} %w_hbm.3, ...), custom_call_target="tpu_custom_call", output_to_operand_aliasing={{2}: (2, {}), {3}: (3, {})} | custom-call | flops 754974720 | bytes 2949120 | tf_op jit(solution)/shard_map/pallas_call | solution.py:217
  6.9 2.5 %collective-permute-start.6 = (s16[2,976,128]{2,1,0:T(8,128)(2,1)S(1)}, s16[2,976,128]{2,1,0:T(8,128)(2,1)S(1)}, u32[]{:S(2)}, u32[]{:S(2)}) collective-permute-start(s16[2,976,128]{2,1,0:T(8,128)(2,1)S(1)} %get-tuple-element.37), channel_id=1, source_target_pairs={{8,16},{16,8},{9,17},{17,9},{10,18},{18,10},{11,19},{19,11},{12,20... | collective-permute-start | bytes 1499144 | tf_op jit(solution)/shard_map/ppermute | solution.py:258
  9.5 3.2 %collective-permute-start = (s16[2,976,128]{2,1,0:T(8,128)(2,1)S(1)}, s16[2,976,128]{2,1,0:T(8,128)(2,1)S(1)}, u32[]{:S(2)}, u32[]{:S(2)}) collective-permute-start(s16[2,976,128]{2,1,0:T(8,128)(2,1)S(1)} %get-tuple-element.28), channel_id=1, source_target_pairs={{8,16},{16,8},{9,17},{17,9},{10,18},{18,10},{11,19},{19,11},{12,20... | collective-permute-start | bytes 1499144 | tf_op jit(solution)/shard_map/ppermute | solution.py:258
  12.8 0.2 convert_reduce_fusion.first_ref
  13.0 4.1 %collective-permute-done.6.halo_ref = s16[2,976,128]{2,1,0:T(8,128)(2,1)S(1)} collective-permute-done((s16[2,976,128]{2,1,0:T(8,128)(2,1)S(1)}, s16[2,976,128]{2,1,0:T(8,128)(2,1)S(1)}, u32[]{:S(2)}, u32[]{:S(2)}) %collective-permute-start.6) | collective-permute-done | bytes 499744 | tf_op jit(solution)/shard_map/ppermute | solution.py:258
  17.1 0.6 broadcast_in_dim.2.bv_ref
  17.7 4.7 %slab_rows.3 = (s16[4,464,128]{2,1,0:T(8,128)(2,1)S(1)}, f32[4,448,128]{2,1,0:T(8,128)S(1)}) custom-call(f32[6,960,128]{2,1,0:T(8,128)S(1)} %get-tuple-element.36.prod, s16[2,976,128]{2,1,0:T(8,128)(2,1)S(1)} %collective-permute-done.6.halo_ref, s16[2,976,128]{2,1,0:T(8,128)(2,1)S(1)} %collective-permute-done.7.near_ref, ...), custom_call_target="tpu_custom_call" | custom-call | flops 731381760 | bytes 6619136 | tf_op jit(solution)/shard_map/slab_rows/pallas_call | solution.py:260
  22.4 1.6 %collective-permute-start.8 = (s16[4,464,128]{2,1,0:T(8,128)(2,1)S(1)}, s16[4,464,128]{2,1,0:T(8,128)(2,1)S(1)}, u32[]{:S(2)}, u32[]{:S(2)}) collective-permute-start(s16[4,464,128]{2,1,0:T(8,128)(2,1)S(1)} %get-tuple-element.39), channel_id=1, source_target_pairs={{0,1},{1,0},{2,3},{3,2},{4,5},{5,4},{6,7},{7,6},{8,9},{9,8},{10,11... | collective-permute-start | bytes 1425416 | tf_op jit(solution)/shard_map/ppermute | solution.py:281
  24.0 4.7 %slab_rows.2 = (s16[4,464,128]{2,1,0:T(8,128)(2,1)S(1)}, f32[4,448,128]{2,1,0:T(8,128)S(1)}) custom-call(f32[6,960,128]{2,1,0:T(8,128)S(1)} %get-tuple-element.27.prod, s16[2,976,128]{2,1,0:T(8,128)(2,1)S(1)} %collective-permute-done.halo_ref, s16[2,976,128]{2,1,0:T(8,128)(2,1)S(1)} %collective-permute-done.1.near_ref, ...), custom_call_target="tpu_custom_call" | custom-call | flops 731381760 | bytes 6619136 | tf_op jit(solution)/shard_map/slab_rows/pallas_call | solution.py:260
  28.6 0.6 %collective-permute-start.2 = (s16[4,464,128]{2,1,0:T(8,128)(2,1)S(1)}, s16[4,464,128]{2,1,0:T(8,128)(2,1)S(1)}, u32[]{:S(2)}, u32[]{:S(2)}) collective-permute-start(s16[4,464,128]{2,1,0:T(8,128)(2,1)S(1)} %get-tuple-element.30), channel_id=1, source_target_pairs={{0,1},{1,0},{2,3},{3,2},{4,5},{5,4},{6,7},{7,6},{8,9},{9,8},{10,11... | collective-permute-start | bytes 1425416 | tf_op jit(solution)/shard_map/ppermute | solution.py:281
  29.3 6.0 %collective-permute-done.8.got_ref = s16[4,464,128]{2,1,0:T(8,128)(2,1)S(1)} collective-permute-done((s16[4,464,128]{2,1,0:T(8,128)(2,1)S(1)}, s16[4,464,128]{2,1,0:T(8,128)(2,1)S(1)}, u32[]{:S(2)}, u32[]{:S(2)}) %collective-permute-start.8) | collective-permute-done | bytes 475168 | tf_op jit(solution)/shard_map/ppermute | solution.py:281
  35.2 0.3 middle_sums.3
  35.5 0.4 collective-permute-start.10
  35.9 2.5 %collective-permute-start.11 = (s16[464,128]{1,0:T(8,128)(2,1)S(1)}, s16[464,128]{1,0:T(8,128)(2,1)S(1)}, u32[]{:S(2)}, u32[]{:S(2)}) collective-permute-start(s16[464,128]{1,0:T(8,128)(2,1)S(1)} %get-tuple-element.44), channel_id=1, source_target_pairs={{0,6},{1,7},{2,4},{3,5},{4,2},{5,3},{6,0},{7,1},{8,14},{9,15},{10,... | collective-permute-start | bytes 356360 | tf_op jit(solution)/shard_map/ppermute | solution.py:297
  38.4 0.7 %collective-permute-start.9 = (s16[464,128]{1,0:T(8,128)(2,1)S(1)}, s16[464,128]{1,0:T(8,128)(2,1)S(1)}, u32[]{:S(2)}, u32[]{:S(2)}) collective-permute-start(s16[464,128]{1,0:T(8,128)(2,1)S(1)} %get-tuple-element.42), channel_id=1, source_target_pairs={{0,2},{1,3},{2,0},{3,1},{4,6},{5,7},{6,4},{7,5},{8,10},{9,11},{10,... | collective-permute-start | bytes 356360 | tf_op jit(solution)/shard_map/ppermute | solution.py:297
  39.1 1.3 %collective-permute-done.2.got_ref = s16[4,464,128]{2,1,0:T(8,128)(2,1)S(1)} collective-permute-done((s16[4,464,128]{2,1,0:T(8,128)(2,1)S(1)}, s16[4,464,128]{2,1,0:T(8,128)(2,1)S(1)}, u32[]{:S(2)}, u32[]{:S(2)}) %collective-permute-start.2) | collective-permute-done | bytes 475168 | tf_op jit(solution)/shard_map/ppermute | solution.py:281
  40.3 0.3 middle_sums.2
  40.6 0.5 collective-permute-start.3
  41.1 0.3 collective-permute-start.4
  41.5 7.1 %collective-permute-done.10.refs_6_ = s16[464,128]{1,0:T(8,128)(2,1)S(1)} collective-permute-done((s16[464,128]{1,0:T(8,128)(2,1)S(1)}, s16[464,128]{1,0:T(8,128)(2,1)S(1)}, u32[]{:S(2)}, u32[]{:S(2)}) %collective-permute-start.10) | collective-permute-done | bytes 118816 | tf_op jit(solution)/shard_map/ppermute | solution.py:297
  48.5 2.7 %collective-permute-done.4.refs_2_ = s16[464,128]{1,0:T(8,128)(2,1)S(1)} collective-permute-done((s16[464,128]{1,0:T(8,128)(2,1)S(1)}, s16[464,128]{1,0:T(8,128)(2,1)S(1)}, u32[]{:S(2)}, u32[]{:S(2)}) %collective-permute-start.4) | collective-permute-done | bytes 118816 | tf_op jit(solution)/shard_map/ppermute | solution.py:297
  51.2 3.9 %collective-permute-done.5.refs_3_ = s16[464,128]{1,0:T(8,128)(2,1)S(1)} collective-permute-done((s16[464,128]{1,0:T(8,128)(2,1)S(1)}, s16[464,128]{1,0:T(8,128)(2,1)S(1)}, u32[]{:S(2)}, u32[]{:S(2)}) %collective-permute-start.5) | collective-permute-done | bytes 118816 | tf_op jit(solution)/shard_map/ppermute | solution.py:297
  55.2 1.0 %last_sums.1 = f32[448,256]{1,0:T(8,128)} custom-call(f32[448,128]{1,0:T(8,128)S(1)} %get-tuple-element.32.refs_0_, s16[464,128]{1,0:T(8,128)(2,1)S(1)} %collective-permute-done.3.refs_1_, s16[464,128]{1,0:T(8,128)(2,1)S(1)} %collective-permute-done.4.refs_2_, s16[464,128]{1,0:T(8,128)(2,1)S(1)} %collective-permute-done.5.refs_3_, ...), custom_call_target="tpu_custom_call" | custom-call | tf_op jit(solution)/shard_map/last_sums/pallas_call | solution.py:299
  (13 shorter events, 0.2 us)
Async XLA Ops:
  2.7 10.0 %copy-start = (s32[3584]{0:T(1024)S(1)}, s32[3584]{0:T(1024)}, u32[]{:S(2)}) copy-start(s32[3584]{0:T(1024)} %param.5) | copy-start | bytes 43012
  6.8 6.2 %collective-permute-start.7 = (s16[2,976,128]{2,1,0:T(8,128)(2,1)S(1)}, s16[2,976,128]{2,1,0:T(8,128)(2,1)S(1)}, u32[]{:S(2)}, u32[]{:S(2)}) collective-permute-start(s16[2,976,128]{2,1,0:T(8,128)(2,1)S(1)} %get-tuple-element.38), channel_id=1, source_target_pairs={{0,8},{8,0},{16,24},{24,16},{1,9},{9,1},{17,25},{25,17},{2,10},{10... | collective-permute-start | bytes 1499144 | tf_op jit(solution)/shard_map/ppermute | solution.py:259
  6.9 10.2 %collective-permute-start.6 = (s16[2,976,128]{2,1,0:T(8,128)(2,1)S(1)}, s16[2,976,128]{2,1,0:T(8,128)(2,1)S(1)}, u32[]{:S(2)}, u32[]{:S(2)}) collective-permute-start(s16[2,976,128]{2,1,0:T(8,128)(2,1)S(1)} %get-tuple-element.37), channel_id=1, source_target_pairs={{8,16},{16,8},{9,17},{17,9},{10,18},{18,10},{11,19},{19,11},{12,20... | collective-permute-start | bytes 1499144 | tf_op jit(solution)/shard_map/ppermute | solution.py:258
  9.4 14.5 %collective-permute-start.1 = (s16[2,976,128]{2,1,0:T(8,128)(2,1)S(1)}, s16[2,976,128]{2,1,0:T(8,128)(2,1)S(1)}, u32[]{:S(2)}, u32[]{:S(2)}) collective-permute-start(s16[2,976,128]{2,1,0:T(8,128)(2,1)S(1)} %get-tuple-element.29), channel_id=1, source_target_pairs={{0,8},{8,0},{16,24},{24,16},{1,9},{9,1},{17,25},{25,17},{2,10},{10... | collective-permute-start | bytes 1499144 | tf_op jit(solution)/shard_map/ppermute | solution.py:259
  9.5 14.5 %collective-permute-start = (s16[2,976,128]{2,1,0:T(8,128)(2,1)S(1)}, s16[2,976,128]{2,1,0:T(8,128)(2,1)S(1)}, u32[]{:S(2)}, u32[]{:S(2)}) collective-permute-start(s16[2,976,128]{2,1,0:T(8,128)(2,1)S(1)} %get-tuple-element.28), channel_id=1, source_target_pairs={{8,16},{16,8},{9,17},{17,9},{10,18},{18,10},{11,19},{19,11},{12,20... | collective-permute-start | bytes 1499144 | tf_op jit(solution)/shard_map/ppermute | solution.py:258
  22.4 12.8 %collective-permute-start.8 = (s16[4,464,128]{2,1,0:T(8,128)(2,1)S(1)}, s16[4,464,128]{2,1,0:T(8,128)(2,1)S(1)}, u32[]{:S(2)}, u32[]{:S(2)}) collective-permute-start(s16[4,464,128]{2,1,0:T(8,128)(2,1)S(1)} %get-tuple-element.39), channel_id=1, source_target_pairs={{0,1},{1,0},{2,3},{3,2},{4,5},{5,4},{6,7},{7,6},{8,9},{9,8},{10,11... | collective-permute-start | bytes 1425416 | tf_op jit(solution)/shard_map/ppermute | solution.py:281
  28.6 11.7 %collective-permute-start.2 = (s16[4,464,128]{2,1,0:T(8,128)(2,1)S(1)}, s16[4,464,128]{2,1,0:T(8,128)(2,1)S(1)}, u32[]{:S(2)}, u32[]{:S(2)}) collective-permute-start(s16[4,464,128]{2,1,0:T(8,128)(2,1)S(1)} %get-tuple-element.30), channel_id=1, source_target_pairs={{0,1},{1,0},{2,3},{3,2},{4,5},{5,4},{6,7},{7,6},{8,9},{9,8},{10,11... | collective-permute-start | bytes 1425416 | tf_op jit(solution)/shard_map/ppermute | solution.py:281
  35.5 13.0 %collective-permute-start.10 = (s16[464,128]{1,0:T(8,128)(2,1)S(1)}, s16[464,128]{1,0:T(8,128)(2,1)S(1)}, u32[]{:S(2)}, u32[]{:S(2)}) collective-permute-start(s16[464,128]{1,0:T(8,128)(2,1)S(1)} %get-tuple-element.43), channel_id=1, source_target_pairs={{0,4},{1,5},{2,6},{3,7},{4,0},{5,1},{6,2},{7,3},{8,12},{9,13},{10,... | collective-permute-start | bytes 356360 | tf_op jit(solution)/shard_map/ppermute | solution.py:297
  35.9 12.6 %collective-permute-start.11 = (s16[464,128]{1,0:T(8,128)(2,1)S(1)}, s16[464,128]{1,0:T(8,128)(2,1)S(1)}, u32[]{:S(2)}, u32[]{:S(2)}) collective-permute-start(s16[464,128]{1,0:T(8,128)(2,1)S(1)} %get-tuple-element.44), channel_id=1, source_target_pairs={{0,6},{1,7},{2,4},{3,5},{4,2},{5,3},{6,0},{7,1},{8,14},{9,15},{10,... | collective-permute-start | bytes 356360 | tf_op jit(solution)/shard_map/ppermute | solution.py:297
  38.4 10.1 %collective-permute-start.9 = (s16[464,128]{1,0:T(8,128)(2,1)S(1)}, s16[464,128]{1,0:T(8,128)(2,1)S(1)}, u32[]{:S(2)}, u32[]{:S(2)}) collective-permute-start(s16[464,128]{1,0:T(8,128)(2,1)S(1)} %get-tuple-element.42), channel_id=1, source_target_pairs={{0,2},{1,3},{2,0},{3,1},{4,6},{5,7},{6,4},{7,5},{8,10},{9,11},{10,... | collective-permute-start | bytes 356360 | tf_op jit(solution)/shard_map/ppermute | solution.py:297
  40.6 7.9 %collective-permute-start.3 = (s16[464,128]{1,0:T(8,128)(2,1)S(1)}, s16[464,128]{1,0:T(8,128)(2,1)S(1)}, u32[]{:S(2)}, u32[]{:S(2)}) collective-permute-start(s16[464,128]{1,0:T(8,128)(2,1)S(1)} %get-tuple-element.33), channel_id=1, source_target_pairs={{0,2},{1,3},{2,0},{3,1},{4,6},{5,7},{6,4},{7,5},{8,10},{9,11},{10,... | collective-permute-start | bytes 356360 | tf_op jit(solution)/shard_map/ppermute | solution.py:297
  41.1 10.1 %collective-permute-start.4 = (s16[464,128]{1,0:T(8,128)(2,1)S(1)}, s16[464,128]{1,0:T(8,128)(2,1)S(1)}, u32[]{:S(2)}, u32[]{:S(2)}) collective-permute-start(s16[464,128]{1,0:T(8,128)(2,1)S(1)} %get-tuple-element.34), channel_id=1, source_target_pairs={{0,4},{1,5},{2,6},{3,7},{4,0},{5,1},{6,2},{7,3},{8,12},{9,13},{10,... | collective-permute-start | bytes 356360 | tf_op jit(solution)/shard_map/ppermute | solution.py:297
  48.5 6.6 %collective-permute-start.5 = (s16[464,128]{1,0:T(8,128)(2,1)S(1)}, s16[464,128]{1,0:T(8,128)(2,1)S(1)}, u32[]{:S(2)}, u32[]{:S(2)}) collective-permute-start(s16[464,128]{1,0:T(8,128)(2,1)S(1)} %get-tuple-element.35), channel_id=1, source_target_pairs={{0,6},{1,7},{2,4},{3,5},{4,2},{5,3},{6,0},{7,1},{8,14},{9,15},{10,... | collective-permute-start | bytes 356360 | tf_op jit(solution)/shard_map/ppermute | solution.py:297

commit v3 on v2

v3 whole, which is shorter than its diff:
```python
import functools
import math

import jax
import jax.numpy as jnp
from jax import lax
from jax.experimental import pallas as pl
from jax.experimental.pallas import tpu as pltpu
from jax.sharding import PartitionSpec as P

LANES = 128
LEVELS = 32766.0
STEPS = 128.0
FAR_PARTS, NEAR_PARTS = 4, 2
VMEM = pltpu.CompilerParams(vmem_limit_bytes=24 * 1024 * 1024)
F32 = jnp.float32
I16 = jnp.int16


def kernel_taps():
    sigma = 3.0 / (2.0 * math.sqrt(2.0 * math.log(2.0)))
    raw_taps = [math.exp(-0.5 * (shift_k - 2) ** 2 / sigma**2) for shift_k in range(5)]
    summed = sum(raw_taps)
    return [value_k / summed for value_k in raw_taps]


def pack_block(values, out, parts=2):
    rows, cols = values.shape
    size = rows // parts
    codes = []
    for part in range(parts):
        v = values[part * size : (part + 1) * size].reshape(size // 8, 8, cols)
        top = jnp.maximum(jnp.max(jnp.abs(v), axis=0), 1e-30)
        code = jnp.ceil(jnp.log2(top) * STEPS) + 1.0
        inverse = jnp.exp2(code * (-1.0 / STEPS)) * LEVELS
        q = jnp.round(v * inverse[None]).astype(jnp.int32)
        codes.append(code.astype(jnp.int32))
        out[part * size : (part + 1) * size, :] = q.reshape(size, cols).astype(I16)
    out[rows : rows + 8 * parts, :] = jnp.concatenate(codes, axis=0).astype(I16)


def unpack_scales(block, rows, parts=2):
    codes = block[rows : rows + 8 * parts, :].astype(jnp.int32).astype(F32)
    return jnp.exp2(codes * (1.0 / STEPS)) * (1.0 / LEVELS)


def unpack_part(block, rows, part, scales, parts=2):
    size = rows // parts
    q = block[part * size : (part + 1) * size, :].astype(jnp.int32).astype(F32)
    q = q.reshape(size // 8, 8, q.shape[-1]) * scales[part * 8 : part * 8 + 8][None]
    return q.reshape(size, q.shape[-1])


def product_kernel(plan, cells, chunks, v_hbm, w_hbm, *refs):
    outs, (buf, wbuf, sem) = refs[:-3], refs[-3:]
    planes, packs = plan(lax.axis_index("gz") % 2)
    msgs, prods = outs[-chunks - len(packs) : -chunks], outs[-chunks:]
    load = pltpu.make_async_copy(w_hbm, wbuf, sem.at[len(planes)])
    load.start()
    copies = []
    for i, plane in enumerate(planes):
        rows = pl.ds(pl.multiple_of(plane * cells, cells), cells)
        copies.append(pltpu.make_async_copy(v_hbm.at[rows, :], buf.at[i], sem.at[i]))
        copies[-1].start()
    load.wait()
    for i, plane in enumerate(planes):
        copies[i].wait()
        product = jnp.dot(buf[i], wbuf[...], preferred_element_type=F32)
        for c in range(chunks):
            prods[c][plane] = product[:, c * LANES : (c + 1) * LANES]
    for msg, (c, plane, parts) in zip(msgs, packs):
        for i in range(2):
            pack_block(prods[c][plane + i], msg.at[i], parts)


def slab_kernel(
    ratios, shape, tile, share, halves, prod, halo_ref, near_ref, bv_ref, first_ref, *refs
):
    planes, width_x, width_y = shape
    cells = width_x * width_y
    sends, keeps, (ext, pad, picked) = refs[:2], refs[2:4], refs[4:]
    window = tile + 8
    r1, r2 = ratios
    odd = lax.axis_index("gz") % 2
    g, last = lax.axis_index("gz"), lax.axis_size("gz") - 1
    inside = jnp.where((g == 0) | (g == last), 0.0, 1.0)
    for ref, base, parts, factor in (
        (halo_ref, 2 * odd, FAR_PARTS, inside),
        (near_ref, 2 * (1 - odd), NEAR_PARTS, 1.0),
    ):
        size = cells // parts
        for i in range(2):
            block = ref.at[i]
            scales = unpack_scales(block, cells, parts) * factor
            for part in range(parts):
                ext[base + i, part * size : (part + 1) * size, :] = unpack_part(
                    block, cells, part, scales, parts
                )
    stride = width_y + 8
    for side in range(2):
        for x in range(width_x + 1):
            pad[side, x * stride : x * stride + 8, :] = jnp.zeros((8, LANES), F32)
    picked[0:8, :] = jnp.zeros((8, LANES), F32)
    per_tile = tile // width_y
    lane = lax.broadcasted_iota(jnp.int32, (window, LANES), 1)

    def blur(at):
        return at[2] + r1 * (at[1] + at[3]) + r2 * (at[0] + at[4])

    def source(p, rows):
        if p < 0:
            return ext[p + 2, rows, :]
        if p >= planes:
            return ext[p - planes + 2, rows, :]
        return prod[p, rows, :]

    for p in range(planes):
        side = p % 2

        def row(x):
            rows = slice(x * width_y, (x + 1) * width_y)
            return blur([source(p + k - 2, rows) for k in range(5)])

        zero = jnp.zeros((width_y, LANES), F32)
        win = [zero, zero, row(0), row(1)]
        for x in range(width_x):
            win.append(row(x + 2) if x + 2 < width_x else zero)
            pad[side, 8 + x * stride : 8 + x * stride + width_y, :] = blur(win)
            win = win[1:]
        found = []
        for t in range(width_x // per_tile):
            rows = []
            for x in range(t * per_tile, (t + 1) * per_tile):
                base = 6 + x * stride
                rows.append(blur([pad[side, base + k : base + k + width_y, :] for k in range(5)]))
            value = jnp.concatenate(rows, axis=0)
            high = value.astype(jnp.bfloat16)
            low = (value - high.astype(F32)).astype(jnp.bfloat16)
            number = p * (width_x // per_tile) + t
            start = pl.multiple_of((first_ref[number] // 8) * 8, 8)
            voxel = bv_ref[pl.ds(start, window), :]
            hits = []
            for left in range(0, tile, LANES):
                right = min(tile - left, LANES)
                hit = jnp.where(voxel == lane + (left + number * tile), 1.0, 0.0)
                hits.append(hit[:, :right].astype(jnp.bfloat16))
            choose = jnp.concatenate(hits, axis=1)
            both = jnp.concatenate([high, low], axis=1)
            out = jnp.dot(choose, both, preferred_element_type=F32)
            found.append((start, out[:, :LANES] + out[:, LANES:]))
        for start, out in found:
            picked[pl.ds(start, 8), :] += out[:8]
            picked[pl.ds(pl.multiple_of(start + 8, 8), window - 8), :] = out[8:]

    mine = lax.axis_index("ta") % 2
    z = lax.axis_index("ta") // 2
    for send, keep, half in zip(sends, keeps, halves):
        for k, d in enumerate(half):
            theirs_at = pl.multiple_of((2 * (z ^ d) + 1 - mine) * share, 8)
            mine_at = pl.multiple_of((2 * (z ^ d) + mine) * share, 8)
            pack_block(picked[pl.ds(theirs_at, share), :], send.at[k])
            keep[k] = picked[pl.ds(mine_at, share), :]


def unpack_block(block, rows):
    scales = unpack_scales(block, rows)
    return jnp.concatenate([unpack_part(block, rows, part, scales) for part in range(2)], axis=0)


def pass_kernel(share, got_ref, keep_ref, out_ref):
    for k in range(got_ref.shape[0]):
        pack_block(keep_ref[k] + unpack_block(got_ref.at[k], share), out_ref.at[k])


def join_kernel(share, got_ref, keep_ref, near_ref, keep_out, *send_out):
    count = got_ref.shape[0]
    for k in range(count):
        total = keep_ref[k] + unpack_block(got_ref.at[k], share)
        total = total + unpack_block(near_ref.at[k], share)
        if k % 2:
            pack_block(total, send_out[0].at[k // 2])
        else:
            keep_out[k // 2] = total


def fold_kernel(share, got_ref, keep_ref, keep_out, *send_out):
    for k in range(got_ref.shape[0]):
        total = keep_ref[k] + unpack_block(got_ref.at[k], share)
        if k % 2:
            pack_block(total, send_out[0].at[k // 2])
        else:
            keep_out[k // 2] = total


def last_kernel(scale, share, chunks, *refs):
    out_ref = refs[-1]
    for c in range(chunks):
        own, got = refs[2 * c : 2 * c + 2]
        value = own[0] + unpack_block(got.at[0], share)
        out_ref[:, c * LANES : (c + 1) * LANES] = value * scale


def shards(volume, sketch_matrix, brain_voxels):
    taps = kernel_taps()
    ratios = (taps[1] / taps[2], taps[0] / taps[2])
    planes, width_x, width_y, time_local = volume.shape
    cells = width_x * width_y
    slab = planes * cells
    rank = sketch_matrix.shape[1]
    chunks = rank // LANES
    picks = brain_voxels.shape[0]
    n_gz, n_ta = lax.axis_size("gz"), lax.axis_size("ta")
    share = picks // n_ta
    blocks = n_ta // 2
    tile = 6 * width_y
    window = tile + 8
    tiles = slab // tile
    vmem = pl.BlockSpec(memory_space=pltpu.VMEM)
    smem = pl.BlockSpec(memory_space=pltpu.SMEM)
    hbm = pl.BlockSpec(memory_space=pltpu.HBM)
    flat = volume.reshape(slab, time_local)

    def products(plan, count, which, held):
        shapes = []
        for c in which:
            for parts in (FAR_PARTS, NEAR_PARTS):
                shapes.append(jax.ShapeDtypeStruct((2, cells + 8 * parts, LANES), I16))
        messages = len(shapes)
        shapes += [jax.ShapeDtypeStruct((planes, cells, LANES), F32)] * chunks
        out = pl.pallas_call(
            functools.partial(product_kernel, plan, cells, chunks),
            out_shape=shapes,
            in_specs=[hbm, hbm] + [vmem] * len(held),
            out_specs=[vmem] * len(shapes),
            input_output_aliases={2 + i: messages + i for i in range(len(held))},
            scratch_shapes=[
                pltpu.VMEM((count, cells, time_local), jnp.bfloat16),
                pltpu.VMEM((time_local, rank), jnp.bfloat16),
                pltpu.SemaphoreType.DMA((count + 1,)),
            ],
            compiler_params=VMEM,
            cost_estimate=pl.CostEstimate(
                flops=2 * count * cells * time_local * rank,
                bytes_accessed=2 * count * cells * time_local,
                transcendentals=0,
            ),
            name="middle_products" if held else "edge_products",
        )(
            pltpu.with_memory_space_constraint(flat, pltpu.HBM),
            pltpu.with_memory_space_constraint(sketch_matrix, pltpu.HBM),
            *held,
        )
        return out[:messages], out[messages:]

    def packs_of(which, odd):
        top = planes - 2
        return [
            (c, plane, parts)
            for c in which
            for plane, parts in ((top * odd, FAR_PARTS), (top * (1 - odd), NEAR_PARTS))
        ]

    def edge_plan(odd):
        far, near = (planes - 2) * odd, (planes - 2) * (1 - odd)
        return [far, far + 1, near, near + 1], packs_of([0], odd)

    def middle_plan(odd):
        return list(range(2, planes - 2)), packs_of(range(1, chunks), odd)

    first_messages, prods = products(edge_plan, 4, [0], [])
    prods, brain_voxels = lax.optimization_barrier((prods, brain_voxels))
    first = jnp.sum(
        brain_voxels[None, :] < (jnp.arange(tiles, dtype=jnp.int32) * tile)[:, None],
        axis=1,
        dtype=jnp.int32,
    )
    wide = jnp.broadcast_to(
        jnp.pad(brain_voxels, (0, window), constant_values=-1)[:, None], (picks + window, LANES)
    )
    prods, wide, first = lax.optimization_barrier((prods, wide, first))
    later_messages, prods = products(middle_plan, planes - 4, range(1, chunks), prods)
    messages = list(first_messages) + list(later_messages)

    even_pairs = [(i, i ^ 1) for i in range(n_gz)]
    odd_pairs = []
    for i in range(n_gz):
        for j in range(n_ta):
            partner = (i, j ^ 2) if i in (0, n_gz - 1) else (i + 1 if i % 2 else i - 1, j)
            odd_pairs.append((i * n_ta + j, partner[0] * n_ta + partner[1]))

    halves = (range(1, blocks, 2), range(0, blocks, 2))

    def sums(kernel, count, args, name, keeps):
        shapes = [jax.ShapeDtypeStruct((count - count // 2, share, LANES), F32)] * keeps
        sent = count // 2 if keeps else count
        if sent:
            shapes.append(jax.ShapeDtypeStruct((sent, share + 16, LANES), I16))
        return pl.pallas_call(
            functools.partial(kernel, share),
            out_shape=shapes,
            in_specs=[vmem] * len(args),
            out_specs=[vmem] * len(shapes),
            compiler_params=VMEM,
            cost_estimate=pl.CostEstimate(
                flops=4 * count * share * LANES,
                bytes_accessed=8 * count * share * LANES,
                transcendentals=0,
            ),
            name=name,
        )(*args)

    def across(value, mask):
        return lax.ppermute(value, "ta", [(i, i ^ mask) for i in range(n_ta)])

    results = []
    for c in range(chunks):
        near = lax.ppermute(messages[2 * c + 1], "gz", even_pairs)
        far = lax.ppermute(messages[2 * c], ("gz", "ta"), odd_pairs)
        rows = pl.pallas_call(
            functools.partial(
                slab_kernel, ratios, (planes, width_x, width_y), tile, share, halves
            ),
            out_shape=[
                jax.ShapeDtypeStruct((len(half), share + 16, LANES), I16) for half in halves
            ]
            + [jax.ShapeDtypeStruct((len(half), share, LANES), F32) for half in halves],
            in_specs=[vmem, vmem, vmem, vmem, smem],
            out_specs=[vmem] * 4,
            scratch_shapes=[
                pltpu.VMEM((4, cells, LANES), F32),
                pltpu.VMEM((2, width_x * (width_y + 8) + 8, LANES), F32),
                pltpu.VMEM((picks + window, LANES), F32),
            ],
            compiler_params=VMEM,
            cost_estimate=pl.CostEstimate(
                flops=4 * slab * LANES * window,
                bytes_accessed=4 * slab * LANES + 8 * picks * LANES,
                transcendentals=0,
            ),
            name="slab_rows",
        )(prods[c], far, near, wide, first)
        near_rows, kept_rows, near_keep, kept_keep = rows
        side_near, side_kept = across(near_rows, 1), across(kept_rows, 1)
        (out,) = sums(pass_kernel, blocks // 2, (side_near, near_keep), "pass_sums", 0)
        near_got = across(out, 2)
        count, mask = blocks // 2, 4
        keep, out = sums(join_kernel, count, (side_kept, kept_keep, near_got), "join_sums", 1)
        while count > 2:
            count //= 2
            keep, out = sums(fold_kernel, count, (across(out, mask), keep), "fold_sums", 1)
            mask *= 2
        results += [keep, across(out, mask)]

    return pl.pallas_call(
        functools.partial(last_kernel, taps[2] ** 3, share, chunks),
        out_shape=jax.ShapeDtypeStruct((share, rank), F32),
        in_specs=[vmem] * (2 * chunks),
        out_specs=vmem,
        compiler_params=VMEM,
        name="last_sums",
    )(*results)


def solution(mesh):
    in_specs = (P("gz", None, None, "ta"), P("ta", None), P("gz"))
    out_specs = P(("gz", "ta"), None)
    return jax.shard_map(shards, mesh=mesh, in_specs=in_specs, out_specs=out_specs, check_vma=False)
```

time: 56.3 us -> 52.8 us (0.938)
  the two profiles are of different devices: /device:TPU:28 before, /device:TPU:0 now
where the time goes in v3:
time: 52.8 us; the launch traced here: 52.6 us
  Pallas kernels  17.8 us (34%)
  starting transfers between devices  17.2 us (33%)
  waiting for transfers between devices  16.8 us (32%)
  local copies, waits for them, and re-layouts  0.57 us (1%)
    ppermute x8, starting transfers between devices, across(): return lax.ppermute(value, 'ta', [(i, i ^ mask) for i in range(n_ta)])  13.8 us
    ppermute x8, waiting for transfers between devices, across(): return lax.ppermute(value, 'ta', [(i, i ^ mask) for i in range(n_ta)])  13.7 us
    pallas_call x2, Pallas kernels, shards(): pl.pallas_call(functools.partial(slab_kernel, ratios, (planes, width_x, w...  9.31 us
    pallas_call x2, Pallas kernels, products(): pl.pallas_call(functools.partial(product_kernel, plan, cells, chunks), ou...  6.95 us
    ppermute x2, waiting for transfers between devices, shards(): far = lax.ppermute(messages[2 * c], ('gz', 'ta'), odd_pairs)  3.13 us
    ppermute x2, starting transfers between devices, shards(): far = lax.ppermute(messages[2 * c], ('gz', 'ta'), odd_pairs)  2.74 us
  transfers between devices with their start and end apart: 12, of which 6 were waited for; matrix products, arithmetic and copies ran while one was open for 1% of the time, Pallas kernels for 24%

profile of v3, /device:TPU:0, one launch (start us, length us, event | category | flops | bytes accessed | tf_op | source)
XLA Modules:
  0.0 52.6 jit_solution(16369270874599410037)
XLA Ops:
  0.0 4.1 %edge_products.1 = (s16[2,992,128]{2,1,0:T(8,128)(2,1)S(1)}, s16[2,976,128]{2,1,0:T(8,128)(2,1)S(1)}, f32[6,960,128]{2,1,0:T(8,128)S(1)}, f32[6,960,128]{2,1,0:T(8,128)S(1)}) custom-call(bf16[5760,384]{1,0:T(8,128)(2,1)} %bitcast.1, bf16[384,256]{1,0:T(8,128)(2,1)} %w_hbm.3), custom_call_target="tpu_custom_call" | custom-call | flops 754974720 | bytes 2949120 | tf_op jit(solution)/shard_map/edge_products/pallas_call | solution.py:230
  4.1 0.5 collective-permute-start.1
  4.6 2.7 %collective-permute-start = (s16[2,992,128]{2,1,0:T(8,128)(2,1)S(1)}, s16[2,992,128]{2,1,0:T(8,128)(2,1)S(1)}, u32[]{:S(2)}, u32[]{:S(2)}) collective-permute-start(s16[2,992,128]{2,1,0:T(8,128)(2,1)S(1)} %get-tuple-element.40), channel_id=1, source_target_pairs={{0,2},{1,3},{2,0},{3,1},{4,6},{5,7},{6,4},{7,5},{8,16},{9,17},{10,... | collective-permute-start | bytes 1523720 | tf_op jit(solution)/shard_map/ppermute | solution.py:318
  7.3 0.2 convert_reduce_fusion.first_ref
  7.5 0.6 %broadcast_in_dim.2.bv_ref = s32[3832,128]{1,0:T(8,128)S(1)} broadcast(s32[3832]{0:T(1024)S(1)} %pad.4), dimensions={0} | broadcast | bytes 1977312 | tf_op jit(solution)/shard_map/broadcast_in_dim | solution.py:277
  8.1 2.8 %middle_products.1 = (s16[2,992,128]{2,1,0:T(8,128)(2,1)S(1)}, s16[2,976,128]{2,1,0:T(8,128)(2,1)S(1)}, f32[6,960,128]{2,1,0:T(8,128)S(1)}, f32[6,960,128]{2,1,0:T(8,128)S(1)}) custom-call(bf16[5760,384]{1,0:T(8,128)(2,1)} %bitcast.2, bf16[384,256]{1,0:T(8,128)(2,1)} %w_hbm.3, ...), custom_call_target="tpu_custom_call", output_to_operand_aliasing={{2}: (2, {}), {3}: (3, {})} | custom-call | flops 377487360 | bytes 1474560 | tf_op jit(solution)/shard_map/middle_products/pallas_call | solution.py:230
  11.1 3.1 %collective-permute-done.halo_ref = s16[2,992,128]{2,1,0:T(8,128)(2,1)S(1)} collective-permute-done((s16[2,992,128]{2,1,0:T(8,128)(2,1)S(1)}, s16[2,992,128]{2,1,0:T(8,128)(2,1)S(1)}, u32[]{:S(2)}, u32[]{:S(2)}) %collective-permute-start) | collective-permute-done | bytes 507936 | tf_op jit(solution)/shard_map/ppermute | solution.py:318
  14.3 4.7 %slab_rows.2 = (s16[2,464,128]{2,1,0:T(8,128)(2,1)S(1)}, s16[2,464,128]{2,1,0:T(8,128)(2,1)S(1)}, f32[2,448,128]{2,1,0:T(8,128)S(1)}, f32[2,448,128]{2,1,0:T(8,128)S(1)}) custom-call(f32[6,960,128]{2,1,0:T(8,128)S(1)} %get-tuple-element.39.prod, s16[2,992,128]{2,1,0:T(8,128)(2,1)S(1)} %collective-permute-done.halo_ref, ...), custom_call_target="tpu_custom_call" | custom-call | flops 731381760 | bytes 6619136 | tf_op jit(solution)/shard_map/slab_rows/pallas_call | solution.py:319
  18.9 2.0 %collective-permute-start.3 = (s16[2,464,128]{2,1,0:T(8,128)(2,1)S(1)}, s16[2,464,128]{2,1,0:T(8,128)(2,1)S(1)}, u32[]{:S(2)}, u32[]{:S(2)}) collective-permute-start(s16[2,464,128]{2,1,0:T(8,128)(2,1)S(1)} %get-tuple-element.46), channel_id=1, source_target_pairs={{0,1},{1,0},{2,3},{3,2},{4,5},{5,4},{6,7},{7,6},{8,9},{9,8},{10,11... | collective-permute-start | bytes 712712 | tf_op jit(solution)/shard_map/ppermute | solution.py:313
  20.9 4.7 %slab_rows.3 = (s16[2,464,128]{2,1,0:T(8,128)(2,1)S(1)}, s16[2,464,128]{2,1,0:T(8,128)(2,1)S(1)}, f32[2,448,128]{2,1,0:T(8,128)S(1)}, f32[2,448,128]{2,1,0:T(8,128)S(1)}) custom-call(f32[6,960,128]{2,1,0:T(8,128)S(1)} %get-tuple-element.50.prod, s16[2,992,128]{2,1,0:T(8,128)(2,1)S(1)} %collective-permute-done.6.halo_ref, ...), custom_call_target="tpu_custom_call" | custom-call | flops 731381760 | bytes 6619136 | tf_op jit(solution)/shard_map/slab_rows/pallas_call | solution.py:319
  25.6 0.8 %collective-permute-start.9 = (s16[2,464,128]{2,1,0:T(8,128)(2,1)S(1)}, s16[2,464,128]{2,1,0:T(8,128)(2,1)S(1)}, u32[]{:S(2)}, u32[]{:S(2)}) collective-permute-start(s16[2,464,128]{2,1,0:T(8,128)(2,1)S(1)} %get-tuple-element.55), channel_id=1, source_target_pairs={{0,1},{1,0},{2,3},{3,2},{4,5},{5,4},{6,7},{7,6},{8,9},{9,8},{10,11... | collective-permute-start | bytes 712712 | tf_op jit(solution)/shard_map/ppermute | solution.py:313
  26.4 1.3 %collective-permute-start.2 = (s16[2,464,128]{2,1,0:T(8,128)(2,1)S(1)}, s16[2,464,128]{2,1,0:T(8,128)(2,1)S(1)}, u32[]{:S(2)}, u32[]{:S(2)}) collective-permute-start(s16[2,464,128]{2,1,0:T(8,128)(2,1)S(1)} %get-tuple-element.44), channel_id=1, source_target_pairs={{0,1},{1,0},{2,3},{3,2},{4,5},{5,4},{6,7},{7,6},{8,9},{9,8},{10,11... | collective-permute-start | bytes 712712 | tf_op jit(solution)/shard_map/ppermute | solution.py:313
  27.9 1.6 %collective-permute-start.4 = (s16[2,464,128]{2,1,0:T(8,128)(2,1)S(1)}, s16[2,464,128]{2,1,0:T(8,128)(2,1)S(1)}, u32[]{:S(2)}, u32[]{:S(2)}) collective-permute-start(s16[2,464,128]{2,1,0:T(8,128)(2,1)S(1)} %pass_sums.2), channel_id=1, source_target_pairs={{0,2},{1,3},{2,0},{3,1},{4,6},{5,7},{6,4},{7,5},{8,10},{9,11},{10,... | collective-permute-start | bytes 712712 | tf_op jit(solution)/shard_map/ppermute | solution.py:313
  29.5 1.1 %collective-permute-start.8 = (s16[2,464,128]{2,1,0:T(8,128)(2,1)S(1)}, s16[2,464,128]{2,1,0:T(8,128)(2,1)S(1)}, u32[]{:S(2)}, u32[]{:S(2)}) collective-permute-start(s16[2,464,128]{2,1,0:T(8,128)(2,1)S(1)} %get-tuple-element.53), channel_id=1, source_target_pairs={{0,1},{1,0},{2,3},{3,2},{4,5},{5,4},{6,7},{7,6},{8,9},{9,8},{10,11... | collective-permute-start | bytes 712712 | tf_op jit(solution)/shard_map/ppermute | solution.py:313
  30.6 3.7 %collective-permute-done.9.got_ref = s16[2,464,128]{2,1,0:T(8,128)(2,1)S(1)} collective-permute-done((s16[2,464,128]{2,1,0:T(8,128)(2,1)S(1)}, s16[2,464,128]{2,1,0:T(8,128)(2,1)S(1)}, u32[]{:S(2)}, u32[]{:S(2)}) %collective-permute-start.9) | collective-permute-done | bytes 237600 | tf_op jit(solution)/shard_map/ppermute | solution.py:313
  34.5 1.6 %collective-permute-start.10 = (s16[2,464,128]{2,1,0:T(8,128)(2,1)S(1)}, s16[2,464,128]{2,1,0:T(8,128)(2,1)S(1)}, u32[]{:S(2)}, u32[]{:S(2)}) collective-permute-start(s16[2,464,128]{2,1,0:T(8,128)(2,1)S(1)} %pass_sums.3), channel_id=1, source_target_pairs={{0,2},{1,3},{2,0},{3,1},{4,6},{5,7},{6,4},{7,5},{8,10},{9,11},{10,... | collective-permute-start | bytes 712712 | tf_op jit(solution)/shard_map/ppermute | solution.py:313
  36.1 3.3 %collective-permute-done.2.got_ref = s16[2,464,128]{2,1,0:T(8,128)(2,1)S(1)} collective-permute-done((s16[2,464,128]{2,1,0:T(8,128)(2,1)S(1)}, s16[2,464,128]{2,1,0:T(8,128)(2,1)S(1)}, u32[]{:S(2)}, u32[]{:S(2)}) %collective-permute-start.2) | collective-permute-done | bytes 237600 | tf_op jit(solution)/shard_map/ppermute | solution.py:313
  39.6 2.7 %collective-permute-start.5 = (s16[1,464,128]{2,1,0:T(8,128)(2,1)S(1)}, s16[1,464,128]{2,1,0:T(8,128)(2,1)S(1)}, u32[]{:S(2)}, u32[]{:S(2)}) collective-permute-start(s16[1,464,128]{2,1,0:T(8,128)(2,1)S(1)} %get-tuple-element.49), channel_id=1, source_target_pairs={{0,4},{1,5},{2,6},{3,7},{4,0},{5,1},{6,2},{7,3},{8,12},{9,13},{10,... | collective-permute-start | bytes 356360 | tf_op jit(solution)/shard_map/ppermute | solution.py:313
  42.3 1.2 %collective-permute-done.8.got_ref = s16[2,464,128]{2,1,0:T(8,128)(2,1)S(1)} collective-permute-done((s16[2,464,128]{2,1,0:T(8,128)(2,1)S(1)}, s16[2,464,128]{2,1,0:T(8,128)(2,1)S(1)}, u32[]{:S(2)}, u32[]{:S(2)}) %collective-permute-start.8) | collective-permute-done | bytes 237600 | tf_op jit(solution)/shard_map/ppermute | solution.py:313
  43.5 0.2 join_sums.3
  43.7 2.7 %collective-permute-start.11 = (s16[1,464,128]{2,1,0:T(8,128)(2,1)S(1)}, s16[1,464,128]{2,1,0:T(8,128)(2,1)S(1)}, u32[]{:S(2)}, u32[]{:S(2)}) collective-permute-start(s16[1,464,128]{2,1,0:T(8,128)(2,1)S(1)} %get-tuple-element.58), channel_id=1, source_target_pairs={{0,4},{1,5},{2,6},{3,7},{4,0},{5,1},{6,2},{7,3},{8,12},{9,13},{10,... | collective-permute-start | bytes 356360 | tf_op jit(solution)/shard_map/ppermute | solution.py:313
  46.3 0.5 collective-permute-done.5.refs_1_
  46.8 5.0 %collective-permute-done.11.refs_3_ = s16[1,464,128]{2,1,0:T(8,128)(2,1)S(1)} collective-permute-done((s16[1,464,128]{2,1,0:T(8,128)(2,1)S(1)}, s16[1,464,128]{2,1,0:T(8,128)(2,1)S(1)}, u32[]{:S(2)}, u32[]{:S(2)}) %collective-permute-start.11) | collective-permute-done | bytes 118816 | tf_op jit(solution)/shard_map/ppermute | solution.py:313
  51.8 0.8 %last_sums.1 = f32[448,256]{1,0:T(8,128)} custom-call(f32[1,448,128]{2,1,0:T(8,128)S(1)} %get-tuple-element.48.refs_0_, s16[1,464,128]{2,1,0:T(8,128)(2,1)S(1)} %collective-permute-done.5.refs_1_, f32[1,448,128]{2,1,0:T(8,128)S(1)} %get-tuple-element.57.refs_2_, s16[1,464,128]{2,1,0:T(8,128)(2,1)S(1)} %collective-permute-done.11.refs_3_), custom_call_target="tpu_custom_call" | custom-call | tf_op jit(solution)/shard_map/last_sums/pallas_call | solution.py:354
  (15 shorter events, 0.7 us)
Async XLA Ops:
  0.0 7.3 %copy-start = (s32[3584]{0:T(1024)S(1)}, s32[3584]{0:T(1024)}, u32[]{:S(2)}) copy-start(s32[3584]{0:T(1024)} %param.5) | copy-start | bytes 43012
  4.1 7.0 %collective-permute-start.1 = (s16[2,976,128]{2,1,0:T(8,128)(2,1)S(1)}, s16[2,976,128]{2,1,0:T(8,128)(2,1)S(1)}, u32[]{:S(2)}, u32[]{:S(2)}) collective-permute-start(s16[2,976,128]{2,1,0:T(8,128)(2,1)S(1)} %get-tuple-element.41), channel_id=1, source_target_pairs={{0,8},{8,0},{16,24},{24,16},{1,9},{9,1},{17,25},{25,17},{2,10},{10... | collective-permute-start | bytes 1499144 | tf_op jit(solution)/shard_map/ppermute | solution.py:317
  4.6 9.6 %collective-permute-start = (s16[2,992,128]{2,1,0:T(8,128)(2,1)S(1)}, s16[2,992,128]{2,1,0:T(8,128)(2,1)S(1)}, u32[]{:S(2)}, u32[]{:S(2)}) collective-permute-start(s16[2,992,128]{2,1,0:T(8,128)(2,1)S(1)} %get-tuple-element.40), channel_id=1, source_target_pairs={{0,2},{1,3},{2,0},{3,1},{4,6},{5,7},{6,4},{7,5},{8,16},{9,17},{10,... | collective-permute-start | bytes 1523720 | tf_op jit(solution)/shard_map/ppermute | solution.py:318
  10.9 10.0 %collective-permute-start.6 = (s16[2,992,128]{2,1,0:T(8,128)(2,1)S(1)}, s16[2,992,128]{2,1,0:T(8,128)(2,1)S(1)}, u32[]{:S(2)}, u32[]{:S(2)}) collective-permute-start(s16[2,992,128]{2,1,0:T(8,128)(2,1)S(1)} %get-tuple-element.51), channel_id=1, source_target_pairs={{0,2},{1,3},{2,0},{3,1},{4,6},{5,7},{6,4},{7,5},{8,16},{9,17},{10,... | collective-permute-start | bytes 1523720 | tf_op jit(solution)/shard_map/ppermute | solution.py:318
  11.0 9.9 %collective-permute-start.7 = (s16[2,976,128]{2,1,0:T(8,128)(2,1)S(1)}, s16[2,976,128]{2,1,0:T(8,128)(2,1)S(1)}, u32[]{:S(2)}, u32[]{:S(2)}) collective-permute-start(s16[2,976,128]{2,1,0:T(8,128)(2,1)S(1)} %get-tuple-element.52), channel_id=1, source_target_pairs={{0,8},{8,0},{16,24},{24,16},{1,9},{9,1},{17,25},{25,17},{2,10},{10... | collective-permute-start | bytes 1499144 | tf_op jit(solution)/shard_map/ppermute | solution.py:317
  18.9 8.8 %collective-permute-start.3 = (s16[2,464,128]{2,1,0:T(8,128)(2,1)S(1)}, s16[2,464,128]{2,1,0:T(8,128)(2,1)S(1)}, u32[]{:S(2)}, u32[]{:S(2)}) collective-permute-start(s16[2,464,128]{2,1,0:T(8,128)(2,1)S(1)} %get-tuple-element.46), channel_id=1, source_target_pairs={{0,1},{1,0},{2,3},{3,2},{4,5},{5,4},{6,7},{7,6},{8,9},{9,8},{10,11... | collective-permute-start | bytes 712712 | tf_op jit(solution)/shard_map/ppermute | solution.py:313
  25.6 8.7 %collective-permute-start.9 = (s16[2,464,128]{2,1,0:T(8,128)(2,1)S(1)}, s16[2,464,128]{2,1,0:T(8,128)(2,1)S(1)}, u32[]{:S(2)}, u32[]{:S(2)}) collective-permute-start(s16[2,464,128]{2,1,0:T(8,128)(2,1)S(1)} %get-tuple-element.55), channel_id=1, source_target_pairs={{0,1},{1,0},{2,3},{3,2},{4,5},{5,4},{6,7},{7,6},{8,9},{9,8},{10,11... | collective-permute-start | bytes 712712 | tf_op jit(solution)/shard_map/ppermute | solution.py:313
  26.4 13.0 %collective-permute-start.2 = (s16[2,464,128]{2,1,0:T(8,128)(2,1)S(1)}, s16[2,464,128]{2,1,0:T(8,128)(2,1)S(1)}, u32[]{:S(2)}, u32[]{:S(2)}) collective-permute-start(s16[2,464,128]{2,1,0:T(8,128)(2,1)S(1)} %get-tuple-element.44), channel_id=1, source_target_pairs={{0,1},{1,0},{2,3},{3,2},{4,5},{5,4},{6,7},{7,6},{8,9},{9,8},{10,11... | collective-permute-start | bytes 712712 | tf_op jit(solution)/shard_map/ppermute | solution.py:313
  27.9 11.6 %collective-permute-start.4 = (s16[2,464,128]{2,1,0:T(8,128)(2,1)S(1)}, s16[2,464,128]{2,1,0:T(8,128)(2,1)S(1)}, u32[]{:S(2)}, u32[]{:S(2)}) collective-permute-start(s16[2,464,128]{2,1,0:T(8,128)(2,1)S(1)} %pass_sums.2), channel_id=1, source_target_pairs={{0,2},{1,3},{2,0},{3,1},{4,6},{5,7},{6,4},{7,5},{8,10},{9,11},{10,... | collective-permute-start | bytes 712712 | tf_op jit(solution)/shard_map/ppermute | solution.py:313
  29.5 14.0 %collective-permute-start.8 = (s16[2,464,128]{2,1,0:T(8,128)(2,1)S(1)}, s16[2,464,128]{2,1,0:T(8,128)(2,1)S(1)}, u32[]{:S(2)}, u32[]{:S(2)}) collective-permute-start(s16[2,464,128]{2,1,0:T(8,128)(2,1)S(1)} %get-tuple-element.53), channel_id=1, source_target_pairs={{0,1},{1,0},{2,3},{3,2},{4,5},{5,4},{6,7},{7,6},{8,9},{9,8},{10,11... | collective-permute-start | bytes 712712 | tf_op jit(solution)/shard_map/ppermute | solution.py:313
  34.5 9.0 %collective-permute-start.10 = (s16[2,464,128]{2,1,0:T(8,128)(2,1)S(1)}, s16[2,464,128]{2,1,0:T(8,128)(2,1)S(1)}, u32[]{:S(2)}, u32[]{:S(2)}) collective-permute-start(s16[2,464,128]{2,1,0:T(8,128)(2,1)S(1)} %pass_sums.3), channel_id=1, source_target_pairs={{0,2},{1,3},{2,0},{3,1},{4,6},{5,7},{6,4},{7,5},{8,10},{9,11},{10,... | collective-permute-start | bytes 712712 | tf_op jit(solution)/shard_map/ppermute | solution.py:313
  39.6 7.2 %collective-permute-start.5 = (s16[1,464,128]{2,1,0:T(8,128)(2,1)S(1)}, s16[1,464,128]{2,1,0:T(8,128)(2,1)S(1)}, u32[]{:S(2)}, u32[]{:S(2)}) collective-permute-start(s16[1,464,128]{2,1,0:T(8,128)(2,1)S(1)} %get-tuple-element.49), channel_id=1, source_target_pairs={{0,4},{1,5},{2,6},{3,7},{4,0},{5,1},{6,2},{7,3},{8,12},{9,13},{10,... | collective-permute-start | bytes 356360 | tf_op jit(solution)/shard_map/ppermute | solution.py:313
  43.7 8.1 %collective-permute-start.11 = (s16[1,464,128]{2,1,0:T(8,128)(2,1)S(1)}, s16[1,464,128]{2,1,0:T(8,128)(2,1)S(1)}, u32[]{:S(2)}, u32[]{:S(2)}) collective-permute-start(s16[1,464,128]{2,1,0:T(8,128)(2,1)S(1)} %get-tuple-element.58), channel_id=1, source_target_pairs={{0,4},{1,5},{2,6},{3,7},{4,0},{5,1},{6,2},{7,3},{8,12},{9,13},{10,... | collective-permute-start | bytes 356360 | tf_op jit(solution)/shard_map/ppermute | solution.py:313

commit v4 on v3

v4 whole, which is shorter than its diff:
```python
import functools
import math

import jax
import jax.numpy as jnp
from jax import lax
from jax.experimental import pallas as pl
from jax.experimental.pallas import tpu as pltpu
from jax.sharding import PartitionSpec as P

LANES = 128
LEVELS = 32766.0
STEPS = 128.0
FAR_PARTS, NEAR_PARTS = 4, 2
VMEM = pltpu.CompilerParams(vmem_limit_bytes=24 * 1024 * 1024)
COST = pl.CostEstimate(flops=0, bytes_accessed=0, transcendentals=0)
F32 = jnp.float32
I16 = jnp.int16


def kernel_taps():
    sigma = 3.0 / (2.0 * math.sqrt(2.0 * math.log(2.0)))
    raw_taps = [math.exp(-0.5 * (shift_k - 2) ** 2 / sigma**2) for shift_k in range(5)]
    summed = sum(raw_taps)
    return [value_k / summed for value_k in raw_taps]


def pack_block(values, out, parts=2):
    rows, cols = values.shape
    size = rows // parts
    codes = []
    for part in range(parts):
        v = values[part * size : (part + 1) * size].reshape(size // 8, 8, cols)
        top = jnp.maximum(jnp.max(jnp.abs(v), axis=0), 1e-30)
        code = jnp.ceil(jnp.log2(top) * STEPS) + 1.0
        inverse = jnp.exp2(code * (-1.0 / STEPS)) * LEVELS
        q = jnp.round(v * inverse[None]).astype(jnp.int32)
        codes.append(code.astype(jnp.int32))
        out[part * size : (part + 1) * size, :] = q.reshape(size, cols).astype(I16)
    out[rows : rows + 8 * parts, :] = jnp.concatenate(codes, axis=0).astype(I16)


def unpack_scales(block, rows, parts=2):
    codes = block[rows : rows + 8 * parts, :].astype(jnp.int32).astype(F32)
    return jnp.exp2(codes * (1.0 / STEPS)) * (1.0 / LEVELS)


def unpack_part(block, rows, part, scales, parts=2):
    size = rows // parts
    q = block[part * size : (part + 1) * size, :].astype(jnp.int32).astype(F32)
    q = q.reshape(size // 8, 8, q.shape[-1]) * scales[part * 8 : part * 8 + 8][None]
    return q.reshape(size, q.shape[-1])


def product_kernel(plan, pack_first, cells, chunks, v_hbm, w_hbm, *refs):
    outs, (buf, wbuf, sem) = refs[:-3], refs[-3:]
    planes, packs = plan(lax.axis_index("gz") % 2)
    msgs, prods = outs[: len(packs)], outs[len(packs) :]
    load = pltpu.make_async_copy(w_hbm, wbuf, sem.at[len(planes)])
    load.start()
    copies = []
    for i, plane in enumerate(planes):
        rows = pl.ds(pl.multiple_of(plane * cells, cells), cells)
        copies.append(pltpu.make_async_copy(v_hbm.at[rows, :], buf.at[i], sem.at[i]))
        copies[-1].start()

    def pack():
        for msg, (c, plane, parts) in zip(msgs, packs):
            for i in range(2):
                pack_block(prods[c][plane + 2 + i], msg.at[i], parts)

    if pack_first:
        pack()
    load.wait()
    for i, plane in enumerate(planes):
        copies[i].wait()
        product = jnp.dot(buf[i], wbuf[...], preferred_element_type=F32)
        for c in range(chunks):
            prods[c][plane + 2] = product[:, c * LANES : (c + 1) * LANES]
    if not pack_first:
        pack()


def unpack_planes(ref, prod, slot, cells, parts, factor):
    size = cells // parts
    for i in range(2):
        block = ref.at[i]
        scales = unpack_scales(block, cells, parts) * factor
        for part in range(parts):
            prod[slot + i, part * size : (part + 1) * size, :] = unpack_part(
                block, cells, part, scales, parts
            )


def smooth_and_pick(ratios, shape, tile, prod, bv_ref, first_ref, pad, first_plane, count, write):
    width_x, width_y = shape
    window = tile + 8
    r1, r2 = ratios
    stride = width_y + 8
    for side in range(2):
        for x in range(width_x + 1):
            pad[side, x * stride : x * stride + 8, :] = jnp.zeros((8, LANES), F32)
    per_tile = tile // width_y
    tiles = width_x // per_tile
    lane = lax.broadcasted_iota(jnp.int32, (window, LANES), 1)

    def blur(at):
        return at[2] + r1 * (at[1] + at[3]) + r2 * (at[0] + at[4])

    for i in range(count):
        side = i % 2
        p = first_plane + i

        def row(x):
            rows = slice(x * width_y, (x + 1) * width_y)
            return blur([prod[p + k, rows, :] for k in range(5)])

        zero = jnp.zeros((width_y, LANES), F32)
        win = [zero, zero, row(0), row(1)]
        for x in range(width_x):
            win.append(row(x + 2) if x + 2 < width_x else zero)
            pad[side, 8 + x * stride : 8 + x * stride + width_y, :] = blur(win)
            win = win[1:]
        found = []
        for t in range(tiles):
            rows = []
            for x in range(t * per_tile, (t + 1) * per_tile):
                base = 6 + x * stride
                rows.append(blur([pad[side, base + k : base + k + width_y, :] for k in range(5)]))
            value = jnp.concatenate(rows, axis=0)
            high = value.astype(jnp.bfloat16)
            low = (value - high.astype(F32)).astype(jnp.bfloat16)
            number = p * tiles + t
            start = pl.multiple_of((first_ref[number] // 8) * 8, 8)
            voxel = bv_ref[pl.ds(start, window), :]
            hits = []
            for left in range(0, tile, LANES):
                right = min(tile - left, LANES)
                hit = jnp.where(voxel == lane + (left + number * tile), 1.0, 0.0)
                hits.append(hit[:, :right].astype(jnp.bfloat16))
            choose = jnp.concatenate(hits, axis=1)
            both = jnp.concatenate([high, low], axis=1)
            out = jnp.dot(choose, both, preferred_element_type=F32)
            found.append((start, out[:, :LANES] + out[:, LANES:]))
        for start, out in found:
            write(start, out)


def inner_kernel(ratios, shape, planes, tile, near_ref, bv_ref, first_ref, prod, picked, pad):
    odd = lax.axis_index("gz") % 2
    unpack_planes(near_ref, prod, (planes + 2) * (1 - odd), shape[0] * shape[1], NEAR_PARTS, 1.0)
    picked[...] = jnp.zeros_like(picked)

    def write(start, out):
        rest = out.shape[0] - 8
        picked[pl.ds(start, 8), :] += out[:8]
        picked[pl.ds(pl.multiple_of(start + 8, 8), rest), :] = out[8:]

    smooth_and_pick(
        ratios, shape, tile, prod, bv_ref, first_ref, pad, 2 * (1 - odd), planes - 2, write
    )


def middle_inner_kernel(
    ratios, shape, planes, tile, plan, chunks, v_hbm, w_hbm, near_ref, bv_ref, first_ref, *refs
):
    outs, (pad, buf, wbuf, sem) = refs[chunks:-4], refs[-4:]
    picked, msgs, prods = outs[0], outs[1:-chunks], outs[-chunks:]
    cells = shape[0] * shape[1]
    product_kernel(plan, True, cells, chunks, v_hbm, w_hbm, *msgs, *prods, buf, wbuf, sem)
    inner_kernel(
        ratios, shape, planes, tile, near_ref, bv_ref, first_ref, prods[0], picked, pad
    )


def later_inner_kernel(ratios, shape, planes, tile, _, near_ref, bv_ref, first_ref, *refs):
    inner_kernel(ratios, shape, planes, tile, near_ref, bv_ref, first_ref, *refs)


def outer_kernel(
    ratios, shape, planes, tile, share, pieces, carries, *refs
):
    _, far_ref, _, bv_ref, first_ref = refs[:5]
    carried, refs = refs[5 : 5 + carries], refs[5 + carries :]
    prod, picked, refs, pad = refs[0], refs[1], refs[2:-1], refs[-1]
    sends, keeps = refs[: len(pieces)], refs[len(pieces) :]
    g, last = lax.axis_index("gz"), lax.axis_size("gz") - 1
    odd = g % 2
    inside = jnp.where((g == 0) | (g == last), 0.0, 1.0)
    unpack_planes(far_ref, prod, (planes + 2) * odd, shape[0] * shape[1], FAR_PARTS, inside)

    def write(start, out):
        picked[pl.ds(start, out.shape[0]), :] += out

    smooth_and_pick(
        ratios, shape, tile, prod, bv_ref, first_ref, pad, (planes - 2) * odd, 2, write
    )
    mine = lax.axis_index("ta") % 2
    z = lax.axis_index("ta") // 2
    for send, keep, piece in zip(sends, keeps, pieces):
        skip = send.shape[0] - len(piece)
        for k in range(skip):
            send[k] = carried[k][0]
        for k, d in enumerate(piece):
            theirs_at = pl.multiple_of((2 * (z ^ d) + 1 - mine) * share, 8)
            mine_at = pl.multiple_of((2 * (z ^ d) + mine) * share, 8)
            pack_block(picked[pl.ds(theirs_at, share), :], send.at[skip + k])
            keep[k] = picked[pl.ds(mine_at, share), :]


def unpack_block(block, rows):
    scales = unpack_scales(block, rows)
    return jnp.concatenate([unpack_part(block, rows, part, scales) for part in range(2)], axis=0)


def pass_kernel(share, got_ref, keep_ref, out_ref):
    for k in range(got_ref.shape[0]):
        pack_block(keep_ref[k] + unpack_block(got_ref.at[k], share), out_ref.at[k])


def join_kernel(share, got_ref, keep_ref, near_ref, keep_out, *send_out):
    count = got_ref.shape[0]
    for k in range(count):
        total = keep_ref[k] + unpack_block(got_ref.at[k], share)
        total = total + unpack_block(near_ref.at[k], share)
        if k % 2:
            pack_block(total, send_out[0].at[k // 2])
        else:
            keep_out[k // 2] = total


def fold_kernel(share, got_ref, keep_ref, keep_out, *send_out):
    for k in range(got_ref.shape[0]):
        total = keep_ref[k] + unpack_block(got_ref.at[k], share)
        if k % 2:
            pack_block(total, send_out[0].at[k // 2])
        else:
            keep_out[k // 2] = total


def short_join_kernel(share, got_ref, keep_ref, near_ref, *outs):
    for k, out in enumerate(outs):
        total = keep_ref[k] + unpack_block(got_ref.at[k], share)
        if k == 0:
            total = total + unpack_block(near_ref.at[0], share)
        pack_block(total, out.at[0])


def last_kernel(scale, share, chunks, *refs):
    out_ref = refs[-1]
    for c in range(chunks):
        own, got = refs[2 * c : 2 * c + 2]
        value = own[0] + unpack_block(got.at[0], share)
        out_ref[:, c * LANES : (c + 1) * LANES] = value * scale


def short_last_kernel(scale, share, chunks, side_ref, *refs):
    out_ref = refs[-1]
    for c in range(chunks):
        own, near, far = refs[3 * c : 3 * c + 3]
        value = own[0] + unpack_block(side_ref.at[c], share)
        value = value + unpack_block(near.at[0], share) + unpack_block(far.at[0], share)
        out_ref[:, c * LANES : (c + 1) * LANES] = value * scale


def shards(volume, sketch_matrix, brain_voxels):
    taps = kernel_taps()
    ratios = (taps[1] / taps[2], taps[0] / taps[2])
    planes, width_x, width_y, time_local = volume.shape
    cells = width_x * width_y
    slab = planes * cells
    rank = sketch_matrix.shape[1]
    chunks = rank // LANES
    picks = brain_voxels.shape[0]
    n_gz, n_ta = lax.axis_size("gz"), lax.axis_size("ta")
    share = picks // n_ta
    blocks = n_ta // 2
    tile = 6 * width_y
    window = tile + 8
    tiles = slab // tile
    vmem = pl.BlockSpec(memory_space=pltpu.VMEM)
    smem = pl.BlockSpec(memory_space=pltpu.SMEM)
    hbm = pl.BlockSpec(memory_space=pltpu.HBM)
    flat = volume.reshape(slab, time_local)

    def message_shapes(which):
        return [
            jax.ShapeDtypeStruct((2, cells + 8 * parts, LANES), I16)
            for c in which
            for parts in (FAR_PARTS, NEAR_PARTS)
        ]

    def product_scratch(count):
        return [
            pltpu.VMEM((count, cells, time_local), jnp.bfloat16),
            pltpu.VMEM((time_local, rank), jnp.bfloat16),
            pltpu.SemaphoreType.DMA((count + 1,)),
        ]

    def packs_of(which, odd):
        top = planes - 2
        return [
            (c, plane, parts)
            for c in which
            for plane, parts in ((top * odd, FAR_PARTS), (top * (1 - odd), NEAR_PARTS))
        ]

    def edge_plan(odd):
        far, near = (planes - 2) * odd, (planes - 2) * (1 - odd)
        return [far, far + 1, near, near + 1], packs_of([0], odd)

    def middle_plan(odd):
        return list(range(2, planes - 2)), packs_of(range(1, chunks), odd)

    held_shape = jax.ShapeDtypeStruct((planes + 4, cells, LANES), F32)
    picked_shape = jax.ShapeDtypeStruct((picks + window, LANES), F32)
    matrices = (
        pltpu.with_memory_space_constraint(flat, pltpu.HBM),
        pltpu.with_memory_space_constraint(sketch_matrix, pltpu.HBM),
    )
    shapes = message_shapes([0]) + [held_shape] * chunks
    out = pl.pallas_call(
        functools.partial(product_kernel, edge_plan, False, cells, chunks),
        out_shape=shapes,
        in_specs=[hbm, hbm],
        out_specs=[vmem] * len(shapes),
        scratch_shapes=product_scratch(4),
        compiler_params=VMEM,
        cost_estimate=COST,
        name="edge_products",
    )(*matrices)
    messages, prods = list(out[:2]), out[2:]
    prods, brain_voxels = lax.optimization_barrier((prods, brain_voxels))
    first = jnp.sum(
        brain_voxels[None, :] < (jnp.arange(tiles, dtype=jnp.int32) * tile)[:, None],
        axis=1,
        dtype=jnp.int32,
    )
    wide = jnp.broadcast_to(
        jnp.pad(brain_voxels, (0, window), constant_values=-1)[:, None], (picks + window, LANES)
    )

    even_pairs = [(i, i ^ 1) for i in range(n_gz)]
    odd_pairs = []
    for i in range(n_gz):
        for j in range(n_ta):
            partner = (i, j ^ 2) if i in (0, n_gz - 1) else (i + 1 if i % 2 else i - 1, j)
            odd_pairs.append((i * n_ta + j, partner[0] * n_ta + partner[1]))

    pad = pltpu.VMEM((2, width_x * (width_y + 8) + 8, LANES), F32)
    short = blocks == 4

    message_of = lambda count: jax.ShapeDtypeStruct((count, share + 16, LANES), I16)
    kept_of = lambda count: jax.ShapeDtypeStruct((count, share, LANES), F32)

    def sums(kernel, shapes, args, name):
        return pl.pallas_call(
            functools.partial(kernel, share),
            out_shape=shapes,
            in_specs=[vmem] * len(args),
            out_specs=[vmem] * len(shapes),
            compiler_params=VMEM,
            cost_estimate=COST,
            name=name,
        )(*args)

    def across(value, mask):
        return lax.ppermute(value, "ta", [(i, i ^ mask) for i in range(n_ta)])

    results, carried = [], []
    for c in range(chunks):
        near = lax.ppermute(messages[2 * c + 1], "gz", even_pairs)
        far = lax.ppermute(messages[2 * c], ("gz", "ta"), odd_pairs)
        if c == 0:
            shapes = [picked_shape] + message_shapes(range(1, chunks)) + [held_shape] * chunks
            out = pl.pallas_call(
                functools.partial(
                    middle_inner_kernel, ratios, (width_x, width_y), planes, tile,
                    middle_plan, chunks,
                ),
                out_shape=shapes,
                in_specs=[hbm, hbm, vmem, vmem, smem] + [vmem] * chunks,
                out_specs=[vmem] * len(shapes),
                input_output_aliases={5 + i: len(shapes) - chunks + i for i in range(chunks)},
                scratch_shapes=[pad] + product_scratch(planes - 4),
                compiler_params=VMEM,
                cost_estimate=COST,
                name="middle_and_inner_rows",
            )(*matrices, near, wide, first, *prods)
            picked, prods = out[0], list(out[-chunks:])
            messages += out[1:-chunks]
            held = prods[0]
        else:
            held, rows = lax.optimization_barrier((prods[c], rows))
            held, picked = pl.pallas_call(
                functools.partial(later_inner_kernel, ratios, (width_x, width_y), planes, tile),
                out_shape=[held_shape, picked_shape],
                in_specs=[vmem, vmem, vmem, smem],
                out_specs=[vmem] * 2,
                input_output_aliases={0: 0},
                scratch_shapes=[pad],
                compiler_params=VMEM,
                cost_estimate=COST,
                name="inner_rows",
            )(held, near, wide, first)
        if short:
            pieces = ((3,), (2,), (1,), (0,)) if c else ((3,), (2, 1), (0,))
        else:
            pieces = (range(1, blocks, 2), range(0, blocks, 2))
        counts = [len(piece) for piece in pieces]
        ends = carried if c == chunks - 1 else []
        sent = [message_of(count) for count in counts[:-1]] + [message_of(counts[-1] + len(ends))]
        rows = pl.pallas_call(
            functools.partial(
                outer_kernel, ratios, (width_x, width_y), planes, tile, share, pieces, len(ends)
            ),
            out_shape=[held_shape, picked_shape] + sent + [kept_of(count) for count in counts],
            in_specs=[vmem, vmem, vmem, vmem, smem] + [vmem] * len(ends),
            out_specs=[vmem] * (2 + 2 * len(pieces)),
            input_output_aliases={0: 0, 2: 1},
            scratch_shapes=[pad],
            compiler_params=VMEM,
            cost_estimate=COST,
            name="outer_rows",
        )(held, far, picked, wide, first, *ends)[2:]
        sent, kept = rows[: len(pieces)], rows[len(pieces) :]
        one = message_of(1)
        if short:
            side = [across(value, 1) for value in sent[:-1]]
            (out,) = sums(pass_kernel, [one], (side[0], kept[0]), "pass_sums")
            near_got = across(out, 2)
            shapes = [one] * counts[1]
            out = sums(short_join_kernel, shapes, (side[1], kept[1], near_got), "join_sums")
            far_got = across(out[0], 4)
            if len(out) == 1:
                out = [out[0]] + list(sums(pass_kernel, [one], (side[2], kept[2]), "pass_sums"))
            results += [kept[-1], across(out[1], 2), far_got]
            carried.append(sent[-1])
            if c == chunks - 1:
                results = [across(sent[-1], 1)] + results
        else:
            side = [across(value, 1) for value in sent]
            (out,) = sums(pass_kernel, [message_of(counts[0])], (side[0], kept[0]), "pass_sums")
            near_got = across(out, 2)
            count, mask = counts[1], 4
            shapes = [kept_of(count // 2), message_of(count // 2)]
            keep, out = sums(join_kernel, shapes, (side[1], kept[1], near_got), "join_sums")
            while count > 2:
                count //= 2
                shapes = [kept_of(count // 2), message_of(count // 2)]
                keep, out = sums(fold_kernel, shapes, (across(out, mask), keep), "fold_sums")
                mask *= 2
            results += [keep, across(out, mask)]

    return pl.pallas_call(
        functools.partial(
            short_last_kernel if short else last_kernel, taps[2] ** 3, share, chunks
        ),
        out_shape=jax.ShapeDtypeStruct((share, rank), F32),
        in_specs=[vmem] * len(results),
        out_specs=vmem,
        compiler_params=VMEM,
        name="last_sums",
    )(*results)


def solution(mesh):
    in_specs = (P("gz", None, None, "ta"), P("ta", None), P("gz"))
    out_specs = P(("gz", "ta"), None)
    return jax.shard_map(shards, mesh=mesh, in_specs=in_specs, out_specs=out_specs, check_vma=False)
```

time: 52.8 us -> 49 us (0.928)
  waiting for transfers between devices: 16.8 us -> 7.12 us
  starting transfers between devices: 17.2 us -> 19.9 us
  Pallas kernels: 17.8 us -> 19.3 us
  other arithmetic: 0.22 us -> 0.93 us
  local copies, waits for them, and re-layouts: 0.57 us -> 1.28 us
    ppermute x8 -> x12, waiting for transfers between devices: 13.7 us -> 6.08 us  [across(): return lax.ppermute(value, 'ta', [(i, i ^ mask) for i in range(n_ta)])]
    ppermute x8 -> x12, starting transfers between devices: 13.8 us -> 16.5 us  [across(): return lax.ppermute(value, 'ta', [(i, i ^ mask) for i in range(n_ta)])]
    ppermute x2, waiting for transfers between devices: 3.13 us -> 1.04 us  [shards(): far = lax.ppermute(messages[2 * c], ('gz', 'ta'), odd_pairs)]
    pallas_call x5 -> x6, Pallas kernels: 17.1 us -> 18.8 us  [the longest x1 5.69 us: shards(): pl.pallas_call(functools.partial(middle_inner_kernel, ratios, (width_x, w...]
    pad x1, local copies, waits for them, and re-layouts: 0.01 us -> 0.72 us  [shards(): jnp.pad(brain_voxels, (0, window), constant_values=-1)[:, None]]
    reduce_sum x1, other arithmetic: 0.22 us -> 0.93 us  [shards(): jnp.sum(brain_voxels[None, :] < (jnp.arange(tiles, dtype=jnp.int32) * til...]
  transfers between devices with their start and end apart: 12 -> 16, of which waited for: 6 -> 5; matrix products, arithmetic and copies ran while one was open for 1% -> 5% of each run, Pallas kernels for 24% -> 29%
where the time goes in v4:
time: 49 us; the launch traced here: 48.7 us
  starting transfers between devices  19.9 us (41%)
  Pallas kernels  19.3 us (39%)
  waiting for transfers between devices  7.12 us (15%)
  local copies, waits for them, and re-layouts  1.28 us (3%)
  other arithmetic  0.93 us (2%)
    ppermute x12, starting transfers between devices, across(): return lax.ppermute(value, 'ta', [(i, i ^ mask) for i in range(n_ta)])  16.5 us
    ppermute x12, waiting for transfers between devices, across(): return lax.ppermute(value, 'ta', [(i, i ^ mask) for i in range(n_ta)])  6.08 us
    pallas_call x1, Pallas kernels, shards(): pl.pallas_call(functools.partial(middle_inner_kernel, ratios, (width_x, w...  5.69 us
    pallas_call x2, Pallas kernels, shards(): pl.pallas_call(functools.partial(outer_kernel, ratios, (width_x, width_y)...  4.67 us
    pallas_call x1, Pallas kernels, shards(): pl.pallas_call(functools.partial(product_kernel, edge_plan, False, cells,...  4.1 us
    pallas_call x1, Pallas kernels, shards(): pl.pallas_call(functools.partial(later_inner_kernel, ratios, (width_x, wi...  3.34 us
    ppermute x2, starting transfers between devices, shards(): far = lax.ppermute(messages[2 * c], ('gz', 'ta'), odd_pairs)  2.85 us
    ppermute x2, waiting for transfers between devices, shards(): far = lax.ppermute(messages[2 * c], ('gz', 'ta'), odd_pairs)  1.04 us
  transfers between devices with their start and end apart: 16, of which 5 were waited for; matrix products, arithmetic and copies ran while one was open for 5% of the time, Pallas kernels for 29%

profile of v4, /device:TPU:0, one launch (start us, length us, event | category | flops | bytes accessed | tf_op | source)
XLA Modules:
  0.0 48.7 jit_solution(11591507364120543996)
XLA Ops:
  0.0 4.1 %edge_products.1 = (s16[2,992,128]{2,1,0:T(8,128)(2,1)S(1)}, s16[2,976,128]{2,1,0:T(8,128)(2,1)S(1)}, f32[10,960,128]{2,1,0:T(8,128)S(1)}, f32[10,960,128]{2,1,0:T(8,128)S(1)}) custom-call(bf16[5760,384]{1,0:T(8,128)(2,1)} %bitcast.1, bf16[384,256]{1,0:T(8,128)(2,1)} %w_hbm.3), custom_call_target="tpu_custom_call" | custom-call | tf_op jit(solution)/shard_map/edge_products/pallas_call | solution.py:322
  4.6 2.7 %collective-permute-start.1 = (s16[2,992,128]{2,1,0:T(8,128)(2,1)S(1)}, s16[2,992,128]{2,1,0:T(8,128)(2,1)S(1)}, u32[]{:S(2)}, u32[]{:S(2)}) collective-permute-start(s16[2,992,128]{2,1,0:T(8,128)(2,1)S(1)} %get-tuple-element.44), channel_id=1, source_target_pairs={{0,2},{1,3},{2,0},{3,1},{4,6},{5,7},{6,4},{7,5},{8,16},{9,17},{10,... | collective-permute-start | bytes 1523720 | tf_op jit(solution)/shard_map/ppermute | solution.py:373
  7.3 0.7 %pad.4 = s32[3832]{0:T(1024)S(1)} pad(s32[3584]{0:T(1024)} %param.5, s32[]{:T(128)} %constant.0.clone.1), padding=0_248 | pad | bytes 29668 | tf_op jit(solution)/shard_map/jit(_pad)/pad | solution.py:340
  8.0 0.9 %convert_reduce_fusion.first_ref.refs_4_ = s32[24]{0:T(128)S(1)} fusion(s32[3584]{0:T(1024)} %param.5, s32[24]{0:T(128)S(1)} %iota_multiply_fusion), kind=kLoop, calls=%fused_computation | loop fusion | flops 258024 | bytes 14528 | tf_op jit(solution)/shard_map/reduce_sum | solution.py:334
  8.9 0.6 %broadcast_in_dim.2.bv_ref.refs_3_ = s32[3832,128]{1,0:T(8,128)S(1)} broadcast(s32[3832]{0:T(1024)S(1)} %pad.4), dimensions={0} | broadcast | bytes 1977312 | tf_op jit(solution)/shard_map/broadcast_in_dim | solution.py:339
  9.5 5.7 %middle_and_inner_rows.1 = (f32[3832,128]{1,0:T(8,128)S(1)}, s16[2,992,128]{2,1,0:T(8,128)(2,1)S(1)}, s16[2,976,128]{2,1,0:T(8,128)(2,1)S(1)}, f32[10,960,128]{2,1,0:T(8,128)S(1)}, f32[10,960,128]{2,1,0:T(8,128)S(1)}) custom-call(bf16[5760,384]{1,0:T(8,128)(2,1)} %bitcast.2, bf16[384,256]{1,0:T(8,128)(2,1)} %w_hbm.3, ...), custom_call_target="tpu_custom_call", output_to_operand_aliasing={{3}: (5, {}), {4}: (6, {})} | custom-call | tf_op jit(solution)/shard_map/middle_and_inner_rows/pallas_call | solution.py:376
  15.5 2.3 %outer_rows.2 = (f32[10,960,128]{2,1,0:T(8,128)S(1)}, f32[3832,128]{1,0:T(8,128)S(1)}, s16[1,464,128]{2,1,0:T(8,128)(2,1)S(1)}, s16[2,464,128]{2,1,0:T(8,128)(2,...) custom-call(f32[10,960,128]{2,1,0:T(8,128)S(1)} %get-tuple-element.4, ...), custom_call_target="tpu_custom_call", output_to_operand_aliasing={{0}: (0, {}), {1}: (2, {})} | custom-call | tf_op jit(solution)/shard_map/outer_rows/pallas_call | solution.py:413
  17.8 2.0 %collective-permute-start.6 = (s16[1,464,128]{2,1,0:T(8,128)(2,1)S(1)}, s16[1,464,128]{2,1,0:T(8,128)(2,1)S(1)}, u32[]{:S(2)}, u32[]{:S(2)}) collective-permute-start(s16[1,464,128]{2,1,0:T(8,128)(2,1)S(1)} %get-tuple-element.46), channel_id=1, source_target_pairs={{0,1},{1,0},{2,3},{3,2},{4,5},{5,4},{6,7},{7,6},{8,9},{9,8},{10,11... | collective-permute-start | bytes 356360 | tf_op jit(solution)/shard_map/ppermute | solution.py:368
  19.9 3.3 %inner_rows.1 = (f32[10,960,128]{2,1,0:T(8,128)S(1)}, f32[3832,128]{1,0:T(8,128)S(1)}) custom-call(f32[10,960,128]{2,1,0:T(8,128)S(1)} %get-tuple-element.52._, s16[2,976,128]{2,1,0:T(8,128)(2,1)S(1)} %collective-permute-done.2.near_ref, s32[3832,128]{1,0:T(8,128)S(1)} %broadcast_in_dim.2.bv_ref.refs_3_, ...), custom_call_target="tpu_custom_call", output_to_operand_aliasing={{0}: (0, {})} | custom-call | tf_op jit(solution)/shard_map/inner_rows/pallas_call | solution.py:395
  23.2 1.0 %collective-permute-done.3.refs_1_ = s16[2,992,128]{2,1,0:T(8,128)(2,1)S(1)} collective-permute-done((s16[2,992,128]{2,1,0:T(8,128)(2,1)S(1)}, s16[2,992,128]{2,1,0:T(8,128)(2,1)S(1)}, u32[]{:S(2)}, u32[]{:S(2)}) %collective-permute-start.3) | collective-permute-done | bytes 507936 | tf_op jit(solution)/shard_map/ppermute | solution.py:373
  24.3 2.3 %outer_rows.3 = (f32[10,960,128]{2,1,0:T(8,128)S(1)}, f32[3832,128]{1,0:T(8,128)S(1)}, s16[1,464,128]{2,1,0:T(8,128)(2,1)S(1)}, s16[1,464,128]{2,1,0:T(8,128)(2,...) custom-call(f32[10,960,128]{2,1,0:T(8,128)S(1)} %get-tuple-element.5, ...), custom_call_target="tpu_custom_call", output_to_operand_aliasing={{0}: (0, {}), {1}: (2, {})} | custom-call | tf_op jit(solution)/shard_map/outer_rows/pallas_call | solution.py:413
  26.6 1.6 %collective-permute-start.13 = (s16[1,464,128]{2,1,0:T(8,128)(2,1)S(1)}, s16[1,464,128]{2,1,0:T(8,128)(2,1)S(1)}, u32[]{:S(2)}, u32[]{:S(2)}) collective-permute-start(s16[1,464,128]{2,1,0:T(8,128)(2,1)S(1)} %get-tuple-element.65), channel_id=1, source_target_pairs={{0,1},{1,0},{2,3},{3,2},{4,5},{5,4},{6,7},{7,6},{8,9},{9,8},{10,11... | collective-permute-start | bytes 356360 | tf_op jit(solution)/shard_map/ppermute | solution.py:368
  28.3 1.1 %collective-permute-start.7 = (s16[1,464,128]{2,1,0:T(8,128)(2,1)S(1)}, s16[1,464,128]{2,1,0:T(8,128)(2,1)S(1)}, u32[]{:S(2)}, u32[]{:S(2)}) collective-permute-start(s16[1,464,128]{2,1,0:T(8,128)(2,1)S(1)} %pass_sums.3), channel_id=1, source_target_pairs={{0,2},{1,3},{2,0},{3,1},{4,6},{5,7},{6,4},{7,5},{8,10},{9,11},{10,... | collective-permute-start | bytes 356360 | tf_op jit(solution)/shard_map/ppermute | solution.py:368
  29.9 1.5 %collective-permute-start.12 = (s16[1,464,128]{2,1,0:T(8,128)(2,1)S(1)}, s16[1,464,128]{2,1,0:T(8,128)(2,1)S(1)}, u32[]{:S(2)}, u32[]{:S(2)}) collective-permute-start(s16[1,464,128]{2,1,0:T(8,128)(2,1)S(1)} %get-tuple-element.63), channel_id=1, source_target_pairs={{0,1},{1,0},{2,3},{3,2},{4,5},{5,4},{6,7},{7,6},{8,9},{9,8},{10,11... | collective-permute-start | bytes 356360 | tf_op jit(solution)/shard_map/ppermute | solution.py:368
  31.7 2.2 %collective-permute-start.14 = (s16[1,464,128]{2,1,0:T(8,128)(2,1)S(1)}, s16[1,464,128]{2,1,0:T(8,128)(2,1)S(1)}, u32[]{:S(2)}, u32[]{:S(2)}) collective-permute-start(s16[1,464,128]{2,1,0:T(8,128)(2,1)S(1)} %pass_sums.5), channel_id=1, source_target_pairs={{0,2},{1,3},{2,0},{3,1},{4,6},{5,7},{6,4},{7,5},{8,10},{9,11},{10,... | collective-permute-start | bytes 356360 | tf_op jit(solution)/shard_map/ppermute | solution.py:368
  33.9 1.5 %collective-permute-start.4 = (s16[2,464,128]{2,1,0:T(8,128)(2,1)S(1)}, s16[2,464,128]{2,1,0:T(8,128)(2,1)S(1)}, u32[]{:S(2)}, u32[]{:S(2)}) collective-permute-start(s16[2,464,128]{2,1,0:T(8,128)(2,1)S(1)} %get-tuple-element.57), channel_id=1, source_target_pairs={{0,1},{1,0},{2,3},{3,2},{4,5},{5,4},{6,7},{7,6},{8,9},{9,8},{10,11... | collective-permute-start | bytes 712712 | tf_op jit(solution)/shard_map/ppermute | solution.py:368
  35.6 0.8 %collective-permute-start.8 = (s16[1,464,128]{2,1,0:T(8,128)(2,1)S(1)}, s16[1,464,128]{2,1,0:T(8,128)(2,1)S(1)}, u32[]{:S(2)}, u32[]{:S(2)}) collective-permute-start(s16[1,464,128]{2,1,0:T(8,128)(2,1)S(1)} %get-tuple-element.58), channel_id=1, source_target_pairs={{0,2},{1,3},{2,0},{3,1},{4,6},{5,7},{6,4},{7,5},{8,10},{9,11},{10,... | collective-permute-start | bytes 356360 | tf_op jit(solution)/shard_map/ppermute | solution.py:368
  36.4 2.6 %collective-permute-start.9 = (s16[1,464,128]{2,1,0:T(8,128)(2,1)S(1)}, s16[1,464,128]{2,1,0:T(8,128)(2,1)S(1)}, u32[]{:S(2)}, u32[]{:S(2)}) collective-permute-start(s16[1,464,128]{2,1,0:T(8,128)(2,1)S(1)} %get-tuple-element.59), channel_id=1, source_target_pairs={{0,4},{1,5},{2,6},{3,7},{4,0},{5,1},{6,2},{7,3},{8,12},{9,13},{10,... | collective-permute-start | bytes 356360 | tf_op jit(solution)/shard_map/ppermute | solution.py:368
  39.1 1.3 %collective-permute-start.11 = (s16[1,464,128]{2,1,0:T(8,128)(2,1)S(1)}, s16[1,464,128]{2,1,0:T(8,128)(2,1)S(1)}, u32[]{:S(2)}, u32[]{:S(2)}) collective-permute-start(s16[1,464,128]{2,1,0:T(8,128)(2,1)S(1)} %pass_sums.4), channel_id=1, source_target_pairs={{0,2},{1,3},{2,0},{3,1},{4,6},{5,7},{6,4},{7,5},{8,10},{9,11},{10,... | collective-permute-start | bytes 356360 | tf_op jit(solution)/shard_map/ppermute | solution.py:368
  40.6 1.3 %collective-permute-start.15 = (s16[1,464,128]{2,1,0:T(8,128)(2,1)S(1)}, s16[1,464,128]{2,1,0:T(8,128)(2,1)S(1)}, u32[]{:S(2)}, u32[]{:S(2)}) collective-permute-start(s16[1,464,128]{2,1,0:T(8,128)(2,1)S(1)} %join_sums.3), channel_id=1, source_target_pairs={{0,4},{1,5},{2,6},{3,7},{4,0},{5,1},{6,2},{7,3},{8,12},{9,13},{10,... | collective-permute-start | bytes 356360 | tf_op jit(solution)/shard_map/ppermute | solution.py:368
  41.9 2.5 %collective-permute-done.8.refs_1_ = s16[1,464,128]{2,1,0:T(8,128)(2,1)S(1)} collective-permute-done((s16[1,464,128]{2,1,0:T(8,128)(2,1)S(1)}, s16[1,464,128]{2,1,0:T(8,128)(2,1)S(1)}, u32[]{:S(2)}, u32[]{:S(2)}) %collective-permute-start.8) | collective-permute-done | bytes 118816 | tf_op jit(solution)/shard_map/ppermute | solution.py:368
  44.4 1.3 %collective-permute-done.11.refs_4_ = s16[1,464,128]{2,1,0:T(8,128)(2,1)S(1)} collective-permute-done((s16[1,464,128]{2,1,0:T(8,128)(2,1)S(1)}, s16[1,464,128]{2,1,0:T(8,128)(2,1)S(1)}, u32[]{:S(2)}, u32[]{:S(2)}) %collective-permute-start.11) | collective-permute-done | bytes 118816 | tf_op jit(solution)/shard_map/ppermute | solution.py:368
  45.7 2.0 %collective-permute-done.15.refs_5_ = s16[1,464,128]{2,1,0:T(8,128)(2,1)S(1)} collective-permute-done((s16[1,464,128]{2,1,0:T(8,128)(2,1)S(1)}, s16[1,464,128]{2,1,0:T(8,128)(2,1)S(1)}, u32[]{:S(2)}, u32[]{:S(2)}) %collective-permute-start.15) | collective-permute-done | bytes 118816 | tf_op jit(solution)/shard_map/ppermute | solution.py:368
  47.7 1.0 %last_sums.1 = f32[448,256]{1,0:T(8,128)} custom-call(s16[2,464,128]{2,1,0:T(8,128)(2,1)S(1)} %collective-permute-done.4.side_ref, f32[1,448,128]{2,1,0:T(8,128)S(1)} %get-tuple-element.51.refs_0_, s16[1,464,128]{2,1,0:T(8,128)(2,1)S(1)} %collective-permute-done.8.refs_1_, s16[1,464,128]{2,1,0:T(8,128)(2,1)S(1)} %collective-permute-done.9.refs_2_, ...), custom_call_target="tpu_custom_call" | custom-call | tf_op jit(solution)/shard_map/last_sums/pallas_call | solution.py:455
  (23 shorter events, 2.2 us)
Async XLA Ops:
  4.1 4.8 %collective-permute-start = (s16[2,976,128]{2,1,0:T(8,128)(2,1)S(1)}, s16[2,976,128]{2,1,0:T(8,128)(2,1)S(1)}, u32[]{:S(2)}, u32[]{:S(2)}) collective-permute-start(s16[2,976,128]{2,1,0:T(8,128)(2,1)S(1)} %get-tuple-element.36), channel_id=1, source_target_pairs={{0,8},{8,0},{16,24},{24,16},{1,9},{9,1},{17,25},{25,17},{2,10},{10... | collective-permute-start | bytes 1499144 | tf_op jit(solution)/shard_map/ppermute | solution.py:372
  4.6 10.8 %collective-permute-start.1 = (s16[2,992,128]{2,1,0:T(8,128)(2,1)S(1)}, s16[2,992,128]{2,1,0:T(8,128)(2,1)S(1)}, u32[]{:S(2)}, u32[]{:S(2)}) collective-permute-start(s16[2,992,128]{2,1,0:T(8,128)(2,1)S(1)} %get-tuple-element.44), channel_id=1, source_target_pairs={{0,2},{1,3},{2,0},{3,1},{4,6},{5,7},{6,4},{7,5},{8,16},{9,17},{10,... | collective-permute-start | bytes 1523720 | tf_op jit(solution)/shard_map/ppermute | solution.py:373
  15.2 9.1 %collective-permute-start.3 = (s16[2,992,128]{2,1,0:T(8,128)(2,1)S(1)}, s16[2,992,128]{2,1,0:T(8,128)(2,1)S(1)}, u32[]{:S(2)}, u32[]{:S(2)}) collective-permute-start(s16[2,992,128]{2,1,0:T(8,128)(2,1)S(1)} %get-tuple-element.55), channel_id=1, source_target_pairs={{0,2},{1,3},{2,0},{3,1},{4,6},{5,7},{6,4},{7,5},{8,16},{9,17},{10,... | collective-permute-start | bytes 1523720 | tf_op jit(solution)/shard_map/ppermute | solution.py:373
  15.4 4.5 %collective-permute-start.2 = (s16[2,976,128]{2,1,0:T(8,128)(2,1)S(1)}, s16[2,976,128]{2,1,0:T(8,128)(2,1)S(1)}, u32[]{:S(2)}, u32[]{:S(2)}) collective-permute-start(s16[2,976,128]{2,1,0:T(8,128)(2,1)S(1)} %get-tuple-element.53), channel_id=1, source_target_pairs={{0,8},{8,0},{16,24},{24,16},{1,9},{9,1},{17,25},{25,17},{2,10},{10... | collective-permute-start | bytes 1499144 | tf_op jit(solution)/shard_map/ppermute | solution.py:372
  17.8 10.4 %collective-permute-start.6 = (s16[1,464,128]{2,1,0:T(8,128)(2,1)S(1)}, s16[1,464,128]{2,1,0:T(8,128)(2,1)S(1)}, u32[]{:S(2)}, u32[]{:S(2)}) collective-permute-start(s16[1,464,128]{2,1,0:T(8,128)(2,1)S(1)} %get-tuple-element.46), channel_id=1, source_target_pairs={{0,1},{1,0},{2,3},{3,2},{4,5},{5,4},{6,7},{7,6},{8,9},{9,8},{10,11... | collective-permute-start | bytes 356360 | tf_op jit(solution)/shard_map/ppermute | solution.py:368
  19.8 15.6 %collective-permute-start.5 = (s16[2,464,128]{2,1,0:T(8,128)(2,1)S(1)}, s16[2,464,128]{2,1,0:T(8,128)(2,1)S(1)}, u32[]{:S(2)}, u32[]{:S(2)}) collective-permute-start(s16[2,464,128]{2,1,0:T(8,128)(2,1)S(1)} %get-tuple-element.47), channel_id=1, source_target_pairs={{0,1},{1,0},{2,3},{3,2},{4,5},{5,4},{6,7},{7,6},{8,9},{9,8},{10,11... | collective-permute-start | bytes 712712 | tf_op jit(solution)/shard_map/ppermute | solution.py:368
  26.6 5.0 %collective-permute-start.13 = (s16[1,464,128]{2,1,0:T(8,128)(2,1)S(1)}, s16[1,464,128]{2,1,0:T(8,128)(2,1)S(1)}, u32[]{:S(2)}, u32[]{:S(2)}) collective-permute-start(s16[1,464,128]{2,1,0:T(8,128)(2,1)S(1)} %get-tuple-element.65), channel_id=1, source_target_pairs={{0,1},{1,0},{2,3},{3,2},{4,5},{5,4},{6,7},{7,6},{8,9},{9,8},{10,11... | collective-permute-start | bytes 356360 | tf_op jit(solution)/shard_map/ppermute | solution.py:368
  28.3 5.6 %collective-permute-start.7 = (s16[1,464,128]{2,1,0:T(8,128)(2,1)S(1)}, s16[1,464,128]{2,1,0:T(8,128)(2,1)S(1)}, u32[]{:S(2)}, u32[]{:S(2)}) collective-permute-start(s16[1,464,128]{2,1,0:T(8,128)(2,1)S(1)} %pass_sums.3), channel_id=1, source_target_pairs={{0,2},{1,3},{2,0},{3,1},{4,6},{5,7},{6,4},{7,5},{8,10},{9,11},{10,... | collective-permute-start | bytes 356360 | tf_op jit(solution)/shard_map/ppermute | solution.py:368
  29.3 7.1 %collective-permute-start.10 = (s16[1,464,128]{2,1,0:T(8,128)(2,1)S(1)}, s16[1,464,128]{2,1,0:T(8,128)(2,1)S(1)}, u32[]{:S(2)}, u32[]{:S(2)}) collective-permute-start(s16[1,464,128]{2,1,0:T(8,128)(2,1)S(1)} %get-tuple-element.61), channel_id=1, source_target_pairs={{0,1},{1,0},{2,3},{3,2},{4,5},{5,4},{6,7},{7,6},{8,9},{9,8},{10,11... | collective-permute-start | bytes 356360 | tf_op jit(solution)/shard_map/ppermute | solution.py:368
  29.9 9.2 %collective-permute-start.12 = (s16[1,464,128]{2,1,0:T(8,128)(2,1)S(1)}, s16[1,464,128]{2,1,0:T(8,128)(2,1)S(1)}, u32[]{:S(2)}, u32[]{:S(2)}) collective-permute-start(s16[1,464,128]{2,1,0:T(8,128)(2,1)S(1)} %get-tuple-element.63), channel_id=1, source_target_pairs={{0,1},{1,0},{2,3},{3,2},{4,5},{5,4},{6,7},{7,6},{8,9},{9,8},{10,11... | collective-permute-start | bytes 356360 | tf_op jit(solution)/shard_map/ppermute | solution.py:368
  31.7 8.8 %collective-permute-start.14 = (s16[1,464,128]{2,1,0:T(8,128)(2,1)S(1)}, s16[1,464,128]{2,1,0:T(8,128)(2,1)S(1)}, u32[]{:S(2)}, u32[]{:S(2)}) collective-permute-start(s16[1,464,128]{2,1,0:T(8,128)(2,1)S(1)} %pass_sums.5), channel_id=1, source_target_pairs={{0,2},{1,3},{2,0},{3,1},{4,6},{5,7},{6,4},{7,5},{8,10},{9,11},{10,... | collective-permute-start | bytes 356360 | tf_op jit(solution)/shard_map/ppermute | solution.py:368
  33.9 11.8 %collective-permute-start.4 = (s16[2,464,128]{2,1,0:T(8,128)(2,1)S(1)}, s16[2,464,128]{2,1,0:T(8,128)(2,1)S(1)}, u32[]{:S(2)}, u32[]{:S(2)}) collective-permute-start(s16[2,464,128]{2,1,0:T(8,128)(2,1)S(1)} %get-tuple-element.57), channel_id=1, source_target_pairs={{0,1},{1,0},{2,3},{3,2},{4,5},{5,4},{6,7},{7,6},{8,9},{9,8},{10,11... | collective-permute-start | bytes 712712 | tf_op jit(solution)/shard_map/ppermute | solution.py:368
  35.6 8.7 %collective-permute-start.8 = (s16[1,464,128]{2,1,0:T(8,128)(2,1)S(1)}, s16[1,464,128]{2,1,0:T(8,128)(2,1)S(1)}, u32[]{:S(2)}, u32[]{:S(2)}) collective-permute-start(s16[1,464,128]{2,1,0:T(8,128)(2,1)S(1)} %get-tuple-element.58), channel_id=1, source_target_pairs={{0,2},{1,3},{2,0},{3,1},{4,6},{5,7},{6,4},{7,5},{8,10},{9,11},{10,... | collective-permute-start | bytes 356360 | tf_op jit(solution)/shard_map/ppermute | solution.py:368
  36.4 7.9 %collective-permute-start.9 = (s16[1,464,128]{2,1,0:T(8,128)(2,1)S(1)}, s16[1,464,128]{2,1,0:T(8,128)(2,1)S(1)}, u32[]{:S(2)}, u32[]{:S(2)}) collective-permute-start(s16[1,464,128]{2,1,0:T(8,128)(2,1)S(1)} %get-tuple-element.59), channel_id=1, source_target_pairs={{0,4},{1,5},{2,6},{3,7},{4,0},{5,1},{6,2},{7,3},{8,12},{9,13},{10,... | collective-permute-start | bytes 356360 | tf_op jit(solution)/shard_map/ppermute | solution.py:368
  39.1 6.5 %collective-permute-start.11 = (s16[1,464,128]{2,1,0:T(8,128)(2,1)S(1)}, s16[1,464,128]{2,1,0:T(8,128)(2,1)S(1)}, u32[]{:S(2)}, u32[]{:S(2)}) collective-permute-start(s16[1,464,128]{2,1,0:T(8,128)(2,1)S(1)} %pass_sums.4), channel_id=1, source_target_pairs={{0,2},{1,3},{2,0},{3,1},{4,6},{5,7},{6,4},{7,5},{8,10},{9,11},{10,... | collective-permute-start | bytes 356360 | tf_op jit(solution)/shard_map/ppermute | solution.py:368
  40.6 7.1 %collective-permute-start.15 = (s16[1,464,128]{2,1,0:T(8,128)(2,1)S(1)}, s16[1,464,128]{2,1,0:T(8,128)(2,1)S(1)}, u32[]{:S(2)}, u32[]{:S(2)}) collective-permute-start(s16[1,464,128]{2,1,0:T(8,128)(2,1)S(1)} %join_sums.3), channel_id=1, source_target_pairs={{0,4},{1,5},{2,6},{3,7},{4,0},{5,1},{6,2},{7,3},{8,12},{9,13},{10,... | collective-permute-start | bytes 356360 | tf_op jit(solution)/shard_map/ppermute | solution.py:368

commit v5 on v4

--- a/solution.py
+++ b/solution.py
@@ -52,33 +52,58 @@
     return q.reshape(size, q.shape[-1])
 
 
-def product_kernel(plan, pack_first, cells, chunks, v_hbm, w_hbm, *refs):
-    outs, (buf, wbuf, sem) = refs[:-3], refs[-3:]
-    planes, packs = plan(lax.axis_index("gz") % 2)
-    msgs, prods = outs[: len(packs)], outs[len(packs) :]
-    load = pltpu.make_async_copy(w_hbm, wbuf, sem.at[len(planes)])
-    load.start()
-    copies = []
-    for i, plane in enumerate(planes):
-        rows = pl.ds(pl.multiple_of(plane * cells, cells), cells)
-        copies.append(pltpu.make_async_copy(v_hbm.at[rows, :], buf.at[i], sem.at[i]))
-        copies[-1].start()
-
-    def pack():
-        for msg, (c, plane, parts) in zip(msgs, packs):
-            for i in range(2):
-                pack_block(prods[c][plane + 2 + i], msg.at[i], parts)
-
-    if pack_first:
-        pack()
-    load.wait()
-    for i, plane in enumerate(planes):
-        copies[i].wait()
-        product = jnp.dot(buf[i], wbuf[...], preferred_element_type=F32)
-        for c in range(chunks):
-            prods[c][plane + 2] = product[:, c * LANES : (c + 1) * LANES]
-    if not pack_first:
-        pack()
+def pack_planes(msgs, prods, packs):
+    for msg, (c, plane, parts) in zip(msgs, packs):
+        for i in range(2):
+            pack_block(prods[c][plane + 2 + i], msg.at[i], parts)
+
+
+def multiply_planes(source, weights, prods, slots, first, cells):
+    for i, slot in enumerate(slots):
+        rows = pl.ds(pl.multiple_of((first + i) * cells, cells), cells)
+        product = jnp.dot(source[rows, :], weights[...], preferred_element_type=F32)
+        for c, prod in enumerate(prods):
+            prod[slot] = product[:, c * LANES : (c + 1) * LANES]
+
+
+def far_kernel(
+    planes, cells, chunks, packs_of, v_hbm, w_hbm, bv_hbm, msg_ref, bv_ref, wide_ref, w_ref, *refs
+):
+    prods, buf, sem = refs[:chunks], refs[chunks], refs[chunks + 1]
+    odd = lax.axis_index("gz") % 2
+    far = (planes - 2) * odd
+    load_bv = pltpu.make_async_copy(bv_hbm, bv_ref, sem.at[0])
+    load_bv.start()
+    load_w = pltpu.make_async_copy(w_hbm, w_ref, sem.at[1])
+    load_w.start()
+    rows = pl.ds(pl.multiple_of(far * cells, cells), 2 * cells)
+    load_v = pltpu.make_async_copy(v_hbm.at[rows, :], buf, sem.at[2])
+    load_v.start()
+    load_bv.wait()
+    rows, lanes = bv_ref.shape
+    for k in range(rows):
+        spread = jnp.broadcast_to(bv_ref[k : k + 1, :], (lanes, lanes))
+        wide_ref[k * lanes : (k + 1) * lanes, :] = spread.T
+    tail = wide_ref.shape[0] - rows * lanes
+    wide_ref[rows * lanes :, :] = jnp.full((tail, lanes), -1, jnp.int32)
+    load_w.wait()
+    load_v.wait()
+    multiply_planes(buf, w_ref, prods, (far + 2, far + 3), 0, cells)
+    pack_planes((msg_ref,), prods, packs_of([0], odd)[:1])
+
+
+def near_kernel(planes, cells, chunks, packs_of, v_ref, w_ref, *refs):
+    msg, prods = refs[chunks], refs[chunks + 1 :]
+    odd = lax.axis_index("gz") % 2
+    near = (planes - 2) * (1 - odd)
+    multiply_planes(v_ref, w_ref, prods, (near + 2, near + 3), near, cells)
+    pack_planes((msg,), prods, packs_of([0], odd)[1:])
+
+
+def middle_kernel(planes, cells, chunks, packs_of, v_ref, w_ref, *refs):
+    msgs, prods = refs[chunks:-chunks], refs[-chunks:]
+    multiply_planes(v_ref, w_ref, prods, range(4, planes), 2, cells)
+    pack_planes(msgs, prods, packs_of(range(1, chunks), lax.axis_index("gz") % 2))
 
 
 def unpack_planes(ref, prod, slot, cells, parts, factor):
@@ -161,19 +186,7 @@
     )
 
 
-def middle_inner_kernel(
-    ratios, shape, planes, tile, plan, chunks, v_hbm, w_hbm, near_ref, bv_ref, first_ref, *refs
-):
-    outs, (pad, buf, wbuf, sem) = refs[chunks:-4], refs[-4:]
-    picked, msgs, prods = outs[0], outs[1:-chunks], outs[-chunks:]
-    cells = shape[0] * shape[1]
-    product_kernel(plan, True, cells, chunks, v_hbm, w_hbm, *msgs, *prods, buf, wbuf, sem)
-    inner_kernel(
-        ratios, shape, planes, tile, near_ref, bv_ref, first_ref, prods[0], picked, pad
-    )
-
-
-def later_inner_kernel(ratios, shape, planes, tile, _, near_ref, bv_ref, first_ref, *refs):
+def inner_rows_kernel(ratios, shape, planes, tile, _, near_ref, bv_ref, first_ref, *refs):
     inner_kernel(ratios, shape, planes, tile, near_ref, bv_ref, first_ref, *refs)
 
 
@@ -204,18 +217,22 @@
         for k, d in enumerate(piece):
             theirs_at = pl.multiple_of((2 * (z ^ d) + 1 - mine) * share, 8)
             mine_at = pl.multiple_of((2 * (z ^ d) + mine) * share, 8)
-            pack_block(picked[pl.ds(theirs_at, share), :], send.at[skip + k])
+            parts = (send.shape[1] - share) // 8
+            pack_block(picked[pl.ds(theirs_at, share), :], send.at[skip + k], parts)
             keep[k] = picked[pl.ds(mine_at, share), :]
 
 
 def unpack_block(block, rows):
-    scales = unpack_scales(block, rows)
-    return jnp.concatenate([unpack_part(block, rows, part, scales) for part in range(2)], axis=0)
+    parts = (block.shape[0] - rows) // 8
+    scales = unpack_scales(block, rows, parts)
+    pieces = [unpack_part(block, rows, part, scales, parts) for part in range(parts)]
+    return jnp.concatenate(pieces, axis=0)
 
 
 def pass_kernel(share, got_ref, keep_ref, out_ref):
+    parts = (out_ref.shape[1] - share) // 8
     for k in range(got_ref.shape[0]):
-        pack_block(keep_ref[k] + unpack_block(got_ref.at[k], share), out_ref.at[k])
+        pack_block(keep_ref[k] + unpack_block(got_ref.at[k], share), out_ref.at[k], parts)
 
 
 def join_kernel(share, got_ref, keep_ref, near_ref, keep_out, *send_out):
@@ -243,7 +260,7 @@
         total = keep_ref[k] + unpack_block(got_ref.at[k], share)
         if k == 0:
             total = total + unpack_block(near_ref.at[0], share)
-        pack_block(total, out.at[0])
+        pack_block(total, out.at[0], (out.shape[1] - share) // 8)
 
 
 def last_kernel(scale, share, chunks, *refs):
@@ -290,13 +307,6 @@
             for parts in (FAR_PARTS, NEAR_PARTS)
         ]
 
-    def product_scratch(count):
-        return [
-            pltpu.VMEM((count, cells, time_local), jnp.bfloat16),
-            pltpu.VMEM((time_local, rank), jnp.bfloat16),
-            pltpu.SemaphoreType.DMA((count + 1,)),
-        ]
-
     def packs_of(which, odd):
         top = planes - 2
         return [
@@ -305,39 +315,55 @@
             for plane, parts in ((top * odd, FAR_PARTS), (top * (1 - odd), NEAR_PARTS))
         ]
 
-    def edge_plan(odd):
-        far, near = (planes - 2) * odd, (planes - 2) * (1 - odd)
-        return [far, far + 1, near, near + 1], packs_of([0], odd)
-
-    def middle_plan(odd):
-        return list(range(2, planes - 2)), packs_of(range(1, chunks), odd)
-
     held_shape = jax.ShapeDtypeStruct((planes + 4, cells, LANES), F32)
     picked_shape = jax.ShapeDtypeStruct((picks + window, LANES), F32)
-    matrices = (
-        pltpu.with_memory_space_constraint(flat, pltpu.HBM),
-        pltpu.with_memory_space_constraint(sketch_matrix, pltpu.HBM),
-    )
-    shapes = message_shapes([0]) + [held_shape] * chunks
+    indices = brain_voxels.reshape(picks // LANES, LANES)
+    shapes = message_shapes([0])[:1] + [
+        jax.ShapeDtypeStruct(indices.shape, jnp.int32),
+        jax.ShapeDtypeStruct((picks + window, LANES), jnp.int32),
+        jax.ShapeDtypeStruct((time_local, rank), jnp.bfloat16),
+    ]
+    shapes += [held_shape] * chunks
     out = pl.pallas_call(
-        functools.partial(product_kernel, edge_plan, False, cells, chunks),
+        functools.partial(far_kernel, planes, cells, chunks, packs_of),
         out_shape=shapes,
-        in_specs=[hbm, hbm],
+        in_specs=[hbm, hbm, hbm],
         out_specs=[vmem] * len(shapes),
-        scratch_shapes=product_scratch(4),
+        scratch_shapes=[
+            pltpu.VMEM((2 * cells, time_local), jnp.bfloat16),
+            pltpu.SemaphoreType.DMA((3,)),
+        ],
         compiler_params=VMEM,
         cost_estimate=COST,
-        name="edge_products",
-    )(*matrices)
-    messages, prods = list(out[:2]), out[2:]
-    prods, brain_voxels = lax.optimization_barrier((prods, brain_voxels))
+        name="far_products",
+    )(*[pltpu.with_memory_space_constraint(x, pltpu.HBM) for x in (flat, sketch_matrix, indices)])
+    far_message, indices, wide, weights = out[:4]
+    prods = out[4:]
+
+    def more_products(kernel, shapes, prods, name):
+        out = pl.pallas_call(
+            functools.partial(kernel, planes, cells, chunks, packs_of),
+            out_shape=shapes + [held_shape] * chunks,
+            in_specs=[vmem] * (2 + chunks),
+            out_specs=[vmem] * (len(shapes) + chunks),
+            input_output_aliases={2 + i: len(shapes) + i for i in range(chunks)},
+            compiler_params=VMEM,
+            cost_estimate=COST,
+            name=name,
+        )(flat, weights, *prods)
+        return list(out[:-chunks]), out[-chunks:]
+
+    near_message, prods = more_products(
+        near_kernel, message_shapes([0])[1:], prods, "near_products"
+    )
+    messages, prods = more_products(
+        middle_kernel, message_shapes(range(1, chunks)), prods, "middle_products"
+    )
+    messages = [far_message] + near_message + messages
     first = jnp.sum(
-        brain_voxels[None, :] < (jnp.arange(tiles, dtype=jnp.int32) * tile)[:, None],
+        indices.reshape(1, picks) < (jnp.arange(tiles, dtype=jnp.int32) * tile)[:, None],
         axis=1,
         dtype=jnp.int32,
-    )
-    wide = jnp.broadcast_to(
-        jnp.pad(brain_voxels, (0, window), constant_values=-1)[:, None], (picks + window, LANES)
     )
 
     even_pairs = [(i, i ^ 1) for i in range(n_gz)]
@@ -367,49 +393,47 @@
     def across(value, mask):
         return lax.ppermute(value, "ta", [(i, i ^ mask) for i in range(n_ta)])
 
-    results, carried = [], []
+    one, urgent = message_of(1), jax.ShapeDtypeStruct((1, share + 32, LANES), I16)
+
+    def finish(near_got, side, kept, before=None):
+        shapes = [urgent, one]
+        far, near = sums(short_join_kernel, shapes, (side[0], kept[0], near_got), "join_sums")
+        if before is not None:
+            near, before[-2] = lax.optimization_barrier((near, before[-2]))
+        return far, [kept[-1], across(near, 2), across(far, 4)]
+
+    results, carried, waiting = [], [], None
     for c in range(chunks):
         near = lax.ppermute(messages[2 * c + 1], "gz", even_pairs)
         far = lax.ppermute(messages[2 * c], ("gz", "ta"), odd_pairs)
-        if c == 0:
-            shapes = [picked_shape] + message_shapes(range(1, chunks)) + [held_shape] * chunks
-            out = pl.pallas_call(
-                functools.partial(
-                    middle_inner_kernel, ratios, (width_x, width_y), planes, tile,
-                    middle_plan, chunks,
-                ),
-                out_shape=shapes,
-                in_specs=[hbm, hbm, vmem, vmem, smem] + [vmem] * chunks,
-                out_specs=[vmem] * len(shapes),
-                input_output_aliases={5 + i: len(shapes) - chunks + i for i in range(chunks)},
-                scratch_shapes=[pad] + product_scratch(planes - 4),
-                compiler_params=VMEM,
-                cost_estimate=COST,
-                name="middle_and_inner_rows",
-            )(*matrices, near, wide, first, *prods)
-            picked, prods = out[0], list(out[-chunks:])
-            messages += out[1:-chunks]
-            held = prods[0]
-        else:
-            held, rows = lax.optimization_barrier((prods[c], rows))
-            held, picked = pl.pallas_call(
-                functools.partial(later_inner_kernel, ratios, (width_x, width_y), planes, tile),
-                out_shape=[held_shape, picked_shape],
-                in_specs=[vmem, vmem, vmem, smem],
-                out_specs=[vmem] * 2,
-                input_output_aliases={0: 0},
-                scratch_shapes=[pad],
-                compiler_params=VMEM,
-                cost_estimate=COST,
-                name="inner_rows",
-            )(held, near, wide, first)
+        held = prods[c]
+        if c:
+            held, rows = lax.optimization_barrier((held, rows))
+        held, picked = pl.pallas_call(
+            functools.partial(inner_rows_kernel, ratios, (width_x, width_y), planes, tile),
+            out_shape=[held_shape, picked_shape],
+            in_specs=[vmem, vmem, vmem, smem],
+            out_specs=[vmem] * 2,
+            input_output_aliases={0: 0},
+            scratch_shapes=[pad],
+            compiler_params=VMEM,
+            cost_estimate=COST,
+            name="inner_rows",
+        )(held, near, wide, first)
+        if waiting:
+            picked, waiting[1] = lax.optimization_barrier((picked, waiting[1]))
+            out = sums(pass_kernel, [urgent], waiting[:2], "pass_sums")[0]
+            picked, out = lax.optimization_barrier((picked, out))
+            waiting[:2] = [across(out, 2)]
         if short:
-            pieces = ((3,), (2,), (1,), (0,)) if c else ((3,), (2, 1), (0,))
+            pieces = ((3,), (2, 1), (0,))
         else:
             pieces = (range(1, blocks, 2), range(0, blocks, 2))
         counts = [len(piece) for piece in pieces]
         ends = carried if c == chunks - 1 else []
         sent = [message_of(count) for count in counts[:-1]] + [message_of(counts[-1] + len(ends))]
+        if short and not waiting:
+            sent[1] = jax.ShapeDtypeStruct((counts[1], share + 32, LANES), I16)
         rows = pl.pallas_call(
             functools.partial(
                 outer_kernel, ratios, (width_x, width_y), planes, tile, share, pieces, len(ends)
@@ -424,19 +448,24 @@
             name="outer_rows",
         )(held, far, picked, wide, first, *ends)[2:]
         sent, kept = rows[: len(pieces)], rows[len(pieces) :]
-        one = message_of(1)
         if short:
+            done = None
+            if waiting:
+                waiting[0], *sent = lax.optimization_barrier((waiting[0], *sent))
+                done, result = finish(*waiting)
+                results += result
             side = [across(value, 1) for value in sent[:-1]]
-            (out,) = sums(pass_kernel, [one], (side[0], kept[0]), "pass_sums")
-            near_got = across(out, 2)
-            shapes = [one] * counts[1]
-            out = sums(short_join_kernel, shapes, (side[1], kept[1], near_got), "join_sums")
-            far_got = across(out[0], 4)
-            if len(out) == 1:
-                out = [out[0]] + list(sums(pass_kernel, [one], (side[2], kept[2]), "pass_sums"))
-            results += [kept[-1], across(out[1], 2), far_got]
+            if done is not None:
+                kept = list(kept)
+                kept[0], done = lax.optimization_barrier((kept[0], done))
+            waiting = [side[0], kept[0], side[1:], kept[1:]]
             carried.append(sent[-1])
             if c == chunks - 1:
+                (out,) = sums(pass_kernel, [urgent], waiting[:2], "pass_sums")
+                near_got = across(out, 2)
+                if results:
+                    near_got, results[-1] = lax.optimization_barrier((near_got, results[-1]))
+                results += finish(near_got, *waiting[2:], results or None)[1]
                 results = [across(sent[-1], 1)] + results
         else:
             side = [across(value, 1) for value in sent]

time: 49 us -> 47.3 us (0.965)
  Pallas kernels: 19.3 us -> 17 us
  waiting for transfers between devices: 7.12 us -> 8.62 us
  starting transfers between devices: 19.9 us -> 21.3 us
  local copies, waits for them, and re-layouts: 1.28 us -> 0.01 us
  other arithmetic: 0.93 us -> 0.22 us
    ppermute x12 -> x11, waiting for transfers between devices: 6.08 us -> 8.61 us  [across(): return lax.ppermute(value, 'ta', [(i, i ^ mask) for i in range(n_ta)])]
    pallas_call x3 -> x5, Pallas kernels: 13.1 us -> 10.8 us  [the longest x2 6.69 us: shards(): pl.pallas_call(functools.partial(inner_rows_kernel, ratios, (width_x, wid...]
    ppermute x2, starting transfers between devices: 2.85 us -> 4.29 us  [shards(): far = lax.ppermute(messages[2 * c], ('gz', 'ta'), odd_pairs)]
    ppermute x2, waiting for transfers between devices: 1.04 us -> 0.01 us  [shards(): far = lax.ppermute(messages[2 * c], ('gz', 'ta'), odd_pairs)]
    pad x1 -> x0, local copies, waits for them, and re-layouts: 0.72 us -> none  [shards(): jnp.pad(brain_voxels, (0, window), constant_values=-1)[:, None]]
    reduce_sum x1, other arithmetic: 0.93 us -> 0.22 us  [shards(): jnp.sum(indices.reshape(1, picks) < (jnp.arange(tiles, dtype=jnp.int32) *...]
    broadcast_in_dim x1 -> x0, local copies, waits for them, and re-layouts: 0.56 us -> none  [shards(): jnp.broadcast_to(jnp.pad(brain_voxels, (0, window), constant_values=-1)[:...]
    ppermute x12 -> x11, starting transfers between devices: 16.5 us -> 16.3 us  [across(): return lax.ppermute(value, 'ta', [(i, i ^ mask) for i in range(n_ta)])]
  transfers between devices with their start and end apart: 16 -> 15, of which waited for: 5 -> 5; matrix products, arithmetic and copies ran while one was open for 5% -> 0% of each run, Pallas kernels for 29% -> 29%
where the time goes in v5:
time: 47.3 us; the launch traced here: 47.2 us
  starting transfers between devices  21.3 us (45%)
  Pallas kernels  17 us (36%)
  waiting for transfers between devices  8.62 us (18%)
    ppermute x11, starting transfers between devices, across(): return lax.ppermute(value, 'ta', [(i, i ^ mask) for i in range(n_ta)])  16.3 us
    ppermute x11, waiting for transfers between devices, across(): return lax.ppermute(value, 'ta', [(i, i ^ mask) for i in range(n_ta)])  8.61 us
    pallas_call x2, Pallas kernels, shards(): pl.pallas_call(functools.partial(inner_rows_kernel, ratios, (width_x, wid...  6.69 us
    pallas_call x2, Pallas kernels, shards(): pl.pallas_call(functools.partial(outer_kernel, ratios, (width_x, width_y)...  4.69 us
    ppermute x2, starting transfers between devices, shards(): far = lax.ppermute(messages[2 * c], ('gz', 'ta'), odd_pairs)  4.29 us
    pallas_call x1, Pallas kernels, shards(): pl.pallas_call(functools.partial(far_kernel, planes, cells, chunks, packs...  2.39 us
    pallas_call x2, Pallas kernels, more_products(): pl.pallas_call(functools.partial(kernel, planes, cells, chunks, packs_of)...  1.71 us
    pallas_call x1, Pallas kernels, shards(): pl.pallas_call(functools.partial(short_last_kernel if short else last_ker...  0.98 us
  transfers between devices with their start and end apart: 15, of which 5 were waited for; matrix products, arithmetic and copies ran while one was open for 0% of the time, Pallas kernels for 29%

profile of v5, /device:TPU:0, one launch (start us, length us, event | category | flops | bytes accessed | tf_op | source)
XLA Modules:
  0.0 47.2 jit_solution(8902546182315796323)
XLA Ops:
  0.0 2.4 %far_products.1 = (s16[2,992,128]{2,1,0:T(8,128)(2,1)S(1)}, s32[28,128]{1,0:T(8,128)S(1)}, s32[3832,128]{1,0:T(8,128)S(1)}, bf16[384,256]{1,0:T(8,128)(2,1)S(1)}...) custom-call(bf16[5760,384]{1,0:T(8,128)(2,1)} %bitcast.3, bf16[384,256]{1,0:T(8,128)(2,1)} %w_hbm.1, ...), custom_call_target="tpu_custom_call" | custom-call | tf_op jit(solution)/shard_map/far_products/pallas_call | solution.py:327
  2.4 3.1 %collective-permute-start.1 = (s16[2,992,128]{2,1,0:T(8,128)(2,1)S(1)}, s16[2,992,128]{2,1,0:T(8,128)(2,1)S(1)}, u32[]{:S(2)}, u32[]{:S(2)}) collective-permute-start(s16[2,992,128]{2,1,0:T(8,128)(2,1)S(1)} %get-tuple-element.63), channel_id=1, source_target_pairs={{0,2},{1,3},{2,0},{3,1},{4,6},{5,7},{6,4},{7,5},{8,16},{9,17},{10,... | collective-permute-start | bytes 1523720 | tf_op jit(solution)/shard_map/ppermute | solution.py:408
  5.5 0.8 %near_products.1 = (s16[2,976,128]{2,1,0:T(8,128)(2,1)S(1)}, f32[10,960,128]{2,1,0:T(8,128)S(1)}, f32[10,960,128]{2,1,0:T(8,128)S(1)}) custom-call(bf16[5760,384]{1,0:T(8,128)(2,1)S(1)} %bitcast.4, bf16[384,256]{1,0:T(8,128)(2,1)S(1)} %get-tuple-element.52.w_ref, ...), custom_call_target="tpu_custom_call", output_to_operand_aliasing={{1}: (2, {}), {2}: (3, {})} | custom-call | tf_op jit(solution)/shard_map/near_products/pallas_call | solution.py:344
  6.4 1.0 %middle_products.1 = (s16[2,992,128]{2,1,0:T(8,128)(2,1)S(1)}, s16[2,976,128]{2,1,0:T(8,128)(2,1)S(1)}, f32[10,960,128]{2,1,0:T(8,128)S(1)}, f32[10,960,128]{2,1,0:T(8,128)S(1)}) custom-call(bf16[5760,384]{1,0:T(8,128)(2,1)S(1)} %bitcast.5, bf16[384,256]{1,0:T(8,128)(2,1)S(1)} %get-tuple-element.52.w_ref, ...), custom_call_target="tpu_custom_call", output_to_operand_aliasing={{2}: (2, {}), {3}: (3, {})} | custom-call | tf_op jit(solution)/shard_map/middle_products/pallas_call | solution.py:344
  7.3 0.5 %collective-permute-start.2 = (s16[2,976,128]{2,1,0:T(8,128)(2,1)S(1)}, s16[2,976,128]{2,1,0:T(8,128)(2,1)S(1)}, u32[]{:S(2)}, u32[]{:S(2)}) collective-permute-start(s16[2,976,128]{2,1,0:T(8,128)(2,1)S(1)} %get-tuple-element.72), channel_id=1, source_target_pairs={{0,8},{8,0},{16,24},{24,16},{1,9},{9,1},{17,25},{25,17},{2,10},{10... | collective-permute-start | bytes 1499144 | tf_op jit(solution)/shard_map/ppermute | solution.py:407
  7.9 1.2 %collective-permute-start.5 = (s16[2,992,128]{2,1,0:T(8,128)(2,1)S(1)}, s16[2,992,128]{2,1,0:T(8,128)(2,1)S(1)}, u32[]{:S(2)}, u32[]{:S(2)}) collective-permute-start(s16[2,992,128]{2,1,0:T(8,128)(2,1)S(1)} %get-tuple-element.78), channel_id=1, source_target_pairs={{0,2},{1,3},{2,0},{3,1},{4,6},{5,7},{6,4},{7,5},{8,16},{9,17},{10,... | collective-permute-start | bytes 1523720 | tf_op jit(solution)/shard_map/ppermute | solution.py:408
  9.3 3.3 %inner_rows.2 = (f32[10,960,128]{2,1,0:T(8,128)S(1)}, f32[3832,128]{1,0:T(8,128)S(1)}) custom-call(f32[10,960,128]{2,1,0:T(8,128)S(1)} %get-tuple-element.58._, s16[2,976,128]{2,1,0:T(8,128)(2,1)S(1)} %collective-permute-done.near_ref, s32[3832,128]{1,0:T(8,128)S(1)} %get-tuple-element.60.bv_ref.refs_3_, ...), custom_call_target="tpu_custom_call", output_to_operand_aliasing={{0}: (0, {})} | custom-call | tf_op jit(solution)/shard_map/inner_rows/pallas_call | solution.py:412
  12.7 2.3 %outer_rows.2 = (f32[10,960,128]{2,1,0:T(8,128)S(1)}, f32[3832,128]{1,0:T(8,128)S(1)}, s16[1,464,128]{2,1,0:T(8,128)(2,1)S(1)}, s16[2,480,128]{2,1,0:T(8,128)(2,...) custom-call(f32[10,960,128]{2,1,0:T(8,128)S(1)} %get-tuple-element.6, ...), custom_call_target="tpu_custom_call", output_to_operand_aliasing={{0}: (0, {}), {1}: (2, {})} | custom-call | tf_op jit(solution)/shard_map/outer_rows/pallas_call | solution.py:437
  15.0 1.8 %collective-permute-start.3 = (s16[1,464,128]{2,1,0:T(8,128)(2,1)S(1)}, s16[1,464,128]{2,1,0:T(8,128)(2,1)S(1)}, u32[]{:S(2)}, u32[]{:S(2)}) collective-permute-start(s16[1,464,128]{2,1,0:T(8,128)(2,1)S(1)} %get-tuple-element.65), channel_id=1, source_target_pairs={{0,1},{1,0},{2,3},{3,2},{4,5},{5,4},{6,7},{7,6},{8,9},{9,8},{10,11... | collective-permute-start | bytes 356360 | tf_op jit(solution)/shard_map/ppermute | solution.py:394
  17.1 3.3 %inner_rows.3 = (f32[10,960,128]{2,1,0:T(8,128)S(1)}, f32[3832,128]{1,0:T(8,128)S(1)}) custom-call(f32[10,960,128]{2,1,0:T(8,128)S(1)} %get-tuple-element.71._, s16[2,976,128]{2,1,0:T(8,128)(2,1)S(1)} %collective-permute-done.2.near_ref, s32[3832,128]{1,0:T(8,128)S(1)} %get-tuple-element.60.bv_ref.refs_3_, ...), custom_call_target="tpu_custom_call", output_to_operand_aliasing={{0}: (0, {})} | custom-call | tf_op jit(solution)/shard_map/inner_rows/pallas_call | solution.py:412
  20.4 0.7 %collective-permute-done.3.got_ref = s16[1,464,128]{2,1,0:T(8,128)(2,1)S(1)} collective-permute-done((s16[1,464,128]{2,1,0:T(8,128)(2,1)S(1)}, s16[1,464,128]{2,1,0:T(8,128)(2,1)S(1)}, u32[]{:S(2)}, u32[]{:S(2)}) %collective-permute-start.3) | collective-permute-done | bytes 118816 | tf_op jit(solution)/shard_map/ppermute | solution.py:394
  21.3 1.9 %collective-permute-start.4 = (s16[1,480,128]{2,1,0:T(8,128)(2,1)S(1)}, s16[1,480,128]{2,1,0:T(8,128)(2,1)S(1)}, u32[]{:S(2)}, u32[]{:S(2)}) collective-permute-start(s16[1,480,128]{2,1,0:T(8,128)(2,1)S(1)} %pass_sums.2), channel_id=1, source_target_pairs={{0,2},{1,3},{2,0},{3,1},{4,6},{5,7},{6,4},{7,5},{8,10},{9,11},{10,... | collective-permute-start | bytes 368648 | tf_op jit(solution)/shard_map/ppermute | solution.py:394
  23.2 2.3 %outer_rows.3 = (f32[10,960,128]{2,1,0:T(8,128)S(1)}, f32[3832,128]{1,0:T(8,128)S(1)}, s16[1,464,128]{2,1,0:T(8,128)(2,1)S(1)}, s16[2,464,128]{2,1,0:T(8,128)(2,...) custom-call(f32[10,960,128]{2,1,0:T(8,128)S(1)} %get-tuple-element.7, ...), custom_call_target="tpu_custom_call", output_to_operand_aliasing={{0}: (0, {}), {1}: (2, {})} | custom-call | tf_op jit(solution)/shard_map/outer_rows/pallas_call | solution.py:437
  25.6 0.7 %collective-permute-done.4.near_ref = s16[1,480,128]{2,1,0:T(8,128)(2,1)S(1)} collective-permute-done((s16[1,480,128]{2,1,0:T(8,128)(2,1)S(1)}, s16[1,480,128]{2,1,0:T(8,128)(2,1)S(1)}, u32[]{:S(2)}, u32[]{:S(2)}) %collective-permute-start.4) | collective-permute-done | bytes 122912 | tf_op jit(solution)/shard_map/ppermute | solution.py:394
  26.2 1.8 %collective-permute-start.8 = (s16[1,464,128]{2,1,0:T(8,128)(2,1)S(1)}, s16[1,464,128]{2,1,0:T(8,128)(2,1)S(1)}, u32[]{:S(2)}, u32[]{:S(2)}) collective-permute-start(s16[1,464,128]{2,1,0:T(8,128)(2,1)S(1)} %get-tuple-element.86), channel_id=1, source_target_pairs={{0,1},{1,0},{2,3},{3,2},{4,5},{5,4},{6,7},{7,6},{8,9},{9,8},{10,11... | collective-permute-start | bytes 356360 | tf_op jit(solution)/shard_map/ppermute | solution.py:394
  28.4 2.9 %collective-permute-start.11 = (s16[1,480,128]{2,1,0:T(8,128)(2,1)S(1)}, s16[1,480,128]{2,1,0:T(8,128)(2,1)S(1)}, u32[]{:S(2)}, u32[]{:S(2)}) collective-permute-start(s16[1,480,128]{2,1,0:T(8,128)(2,1)S(1)} %get-tuple-element.89), channel_id=1, source_target_pairs={{0,4},{1,5},{2,6},{3,7},{4,0},{5,1},{6,2},{7,3},{8,12},{9,13},{10,... | collective-permute-start | bytes 368648 | tf_op jit(solution)/shard_map/ppermute | solution.py:394
  31.8 1.6 %collective-permute-start.10 = (s16[1,480,128]{2,1,0:T(8,128)(2,1)S(1)}, s16[1,480,128]{2,1,0:T(8,128)(2,1)S(1)}, u32[]{:S(2)}, u32[]{:S(2)}) collective-permute-start(s16[1,480,128]{2,1,0:T(8,128)(2,1)S(1)} %pass_sums.3), channel_id=1, source_target_pairs={{0,2},{1,3},{2,0},{3,1},{4,6},{5,7},{6,4},{7,5},{8,10},{9,11},{10,... | collective-permute-start | bytes 368648 | tf_op jit(solution)/shard_map/ppermute | solution.py:394
  33.4 0.4 collective-permute-start.12
  33.8 1.5 %collective-permute-start.6 = (s16[2,464,128]{2,1,0:T(8,128)(2,1)S(1)}, s16[2,464,128]{2,1,0:T(8,128)(2,1)S(1)}, u32[]{:S(2)}, u32[]{:S(2)}) collective-permute-start(s16[2,464,128]{2,1,0:T(8,128)(2,1)S(1)} %get-tuple-element.83), channel_id=1, source_target_pairs={{0,1},{1,0},{2,3},{3,2},{4,5},{5,4},{6,7},{7,6},{8,9},{9,8},{10,11... | collective-permute-start | bytes 712712 | tf_op jit(solution)/shard_map/ppermute | solution.py:394
  35.3 2.7 %collective-permute-done.10.near_ref = s16[1,480,128]{2,1,0:T(8,128)(2,1)S(1)} collective-permute-done((s16[1,480,128]{2,1,0:T(8,128)(2,1)S(1)}, s16[1,480,128]{2,1,0:T(8,128)(2,1)S(1)}, u32[]{:S(2)}, u32[]{:S(2)}) %collective-permute-start.10) | collective-permute-done | bytes 122912 | tf_op jit(solution)/shard_map/ppermute | solution.py:394
  38.2 2.4 %collective-permute-start.14 = (s16[1,480,128]{2,1,0:T(8,128)(2,1)S(1)}, s16[1,480,128]{2,1,0:T(8,128)(2,1)S(1)}, u32[]{:S(2)}, u32[]{:S(2)}) collective-permute-start(s16[1,480,128]{2,1,0:T(8,128)(2,1)S(1)} %get-tuple-element.98), channel_id=1, source_target_pairs={{0,4},{1,5},{2,6},{3,7},{4,0},{5,1},{6,2},{7,3},{8,12},{9,13},{10,... | collective-permute-start | bytes 368648 | tf_op jit(solution)/shard_map/ppermute | solution.py:394
  40.6 1.4 %collective-permute-start.13 = (s16[1,464,128]{2,1,0:T(8,128)(2,1)S(1)}, s16[1,464,128]{2,1,0:T(8,128)(2,1)S(1)}, u32[]{:S(2)}, u32[]{:S(2)}) collective-permute-start(s16[1,464,128]{2,1,0:T(8,128)(2,1)S(1)} %get-tuple-element.97), channel_id=1, source_target_pairs={{0,2},{1,3},{2,0},{3,1},{4,6},{5,7},{6,4},{7,5},{8,10},{9,11},{10,... | collective-permute-start | bytes 356360 | tf_op jit(solution)/shard_map/ppermute | solution.py:394
  42.0 4.2 %collective-permute-done.13.refs_4_ = s16[1,464,128]{2,1,0:T(8,128)(2,1)S(1)} collective-permute-done((s16[1,464,128]{2,1,0:T(8,128)(2,1)S(1)}, s16[1,464,128]{2,1,0:T(8,128)(2,1)S(1)}, u32[]{:S(2)}, u32[]{:S(2)}) %collective-permute-start.13) | collective-permute-done | bytes 118816 | tf_op jit(solution)/shard_map/ppermute | solution.py:394
  46.2 1.0 %last_sums.1 = f32[448,256]{1,0:T(8,128)} custom-call(s16[2,464,128]{2,1,0:T(8,128)(2,1)S(1)} %collective-permute-done.6.side_ref, f32[1,448,128]{2,1,0:T(8,128)S(1)} %get-tuple-element.70.refs_0_, s16[1,464,128]{2,1,0:T(8,128)(2,1)S(1)} %collective-permute-done.12.refs_1_, s16[1,480,128]{2,1,0:T(8,128)(2,1)S(1)} %collective-permute-done.11.refs_2_, ...), custom_call_target="tpu_custom_call" | custom-call | tf_op jit(solution)/shard_map/last_sums/pallas_call | solution.py:484
  (22 shorter events, 1.7 us)
Async XLA Ops:
  0.0 5.5 %copy-start = (bf16[6,24,40,384]{3,2,1,0:T(8,128)(2,1)S(1)}, bf16[6,24,40,384]{3,2,1,0:T(8,128)(2,1)}, u32[]{:S(2)}) copy-start(bf16[6,24,40,384]{3,2,1,0:T(8,128)(2,1)} %param.3) | copy-start | bytes 13271044
  2.4 10.2 %collective-permute-start.1 = (s16[2,992,128]{2,1,0:T(8,128)(2,1)S(1)}, s16[2,992,128]{2,1,0:T(8,128)(2,1)S(1)}, u32[]{:S(2)}, u32[]{:S(2)}) collective-permute-start(s16[2,992,128]{2,1,0:T(8,128)(2,1)S(1)} %get-tuple-element.63), channel_id=1, source_target_pairs={{0,2},{1,3},{2,0},{3,1},{4,6},{5,7},{6,4},{7,5},{8,16},{9,17},{10,... | collective-permute-start | bytes 1523720 | tf_op jit(solution)/shard_map/ppermute | solution.py:408
  6.3 3.0 %collective-permute-start = (s16[2,976,128]{2,1,0:T(8,128)(2,1)S(1)}, s16[2,976,128]{2,1,0:T(8,128)(2,1)S(1)}, u32[]{:S(2)}, u32[]{:S(2)}) collective-permute-start(s16[2,976,128]{2,1,0:T(8,128)(2,1)S(1)} %get-tuple-element.59), channel_id=1, source_target_pairs={{0,8},{8,0},{16,24},{24,16},{1,9},{9,1},{17,25},{25,17},{2,10},{10... | collective-permute-start | bytes 1499144 | tf_op jit(solution)/shard_map/ppermute | solution.py:407
  7.3 9.8 %collective-permute-start.2 = (s16[2,976,128]{2,1,0:T(8,128)(2,1)S(1)}, s16[2,976,128]{2,1,0:T(8,128)(2,1)S(1)}, u32[]{:S(2)}, u32[]{:S(2)}) collective-permute-start(s16[2,976,128]{2,1,0:T(8,128)(2,1)S(1)} %get-tuple-element.72), channel_id=1, source_target_pairs={{0,8},{8,0},{16,24},{24,16},{1,9},{9,1},{17,25},{25,17},{2,10},{10... | collective-permute-start | bytes 1499144 | tf_op jit(solution)/shard_map/ppermute | solution.py:407
  7.9 15.3 %collective-permute-start.5 = (s16[2,992,128]{2,1,0:T(8,128)(2,1)S(1)}, s16[2,992,128]{2,1,0:T(8,128)(2,1)S(1)}, u32[]{:S(2)}, u32[]{:S(2)}) collective-permute-start(s16[2,992,128]{2,1,0:T(8,128)(2,1)S(1)} %get-tuple-element.78), channel_id=1, source_target_pairs={{0,2},{1,3},{2,0},{3,1},{4,6},{5,7},{6,4},{7,5},{8,16},{9,17},{10,... | collective-permute-start | bytes 1523720 | tf_op jit(solution)/shard_map/ppermute | solution.py:408
  15.0 6.2 %collective-permute-start.3 = (s16[1,464,128]{2,1,0:T(8,128)(2,1)S(1)}, s16[1,464,128]{2,1,0:T(8,128)(2,1)S(1)}, u32[]{:S(2)}, u32[]{:S(2)}) collective-permute-start(s16[1,464,128]{2,1,0:T(8,128)(2,1)S(1)} %get-tuple-element.65), channel_id=1, source_target_pairs={{0,1},{1,0},{2,3},{3,2},{4,5},{5,4},{6,7},{7,6},{8,9},{9,8},{10,11... | collective-permute-start | bytes 356360 | tf_op jit(solution)/shard_map/ppermute | solution.py:394
  16.8 11.4 %collective-permute-start.9 = (s16[2,480,128]{2,1,0:T(8,128)(2,1)S(1)}, s16[2,480,128]{2,1,0:T(8,128)(2,1)S(1)}, u32[]{:S(2)}, u32[]{:S(2)}) collective-permute-start(s16[2,480,128]{2,1,0:T(8,128)(2,1)S(1)} %get-tuple-element.66), channel_id=1, source_target_pairs={{0,1},{1,0},{2,3},{3,2},{4,5},{5,4},{6,7},{7,6},{8,9},{9,8},{10,11... | collective-permute-start | bytes 737288 | tf_op jit(solution)/shard_map/ppermute | solution.py:394
  21.3 4.9 %collective-permute-start.4 = (s16[1,480,128]{2,1,0:T(8,128)(2,1)S(1)}, s16[1,480,128]{2,1,0:T(8,128)(2,1)S(1)}, u32[]{:S(2)}, u32[]{:S(2)}) collective-permute-start(s16[1,480,128]{2,1,0:T(8,128)(2,1)S(1)} %pass_sums.2), channel_id=1, source_target_pairs={{0,2},{1,3},{2,0},{3,1},{4,6},{5,7},{6,4},{7,5},{8,10},{9,11},{10,... | collective-permute-start | bytes 368648 | tf_op jit(solution)/shard_map/ppermute | solution.py:394
  26.2 5.5 %collective-permute-start.8 = (s16[1,464,128]{2,1,0:T(8,128)(2,1)S(1)}, s16[1,464,128]{2,1,0:T(8,128)(2,1)S(1)}, u32[]{:S(2)}, u32[]{:S(2)}) collective-permute-start(s16[1,464,128]{2,1,0:T(8,128)(2,1)S(1)} %get-tuple-element.86), channel_id=1, source_target_pairs={{0,1},{1,0},{2,3},{3,2},{4,5},{5,4},{6,7},{7,6},{8,9},{9,8},{10,11... | collective-permute-start | bytes 356360 | tf_op jit(solution)/shard_map/ppermute | solution.py:394
  28.0 10.0 %collective-permute-start.7 = (s16[2,464,128]{2,1,0:T(8,128)(2,1)S(1)}, s16[2,464,128]{2,1,0:T(8,128)(2,1)S(1)}, u32[]{:S(2)}, u32[]{:S(2)}) collective-permute-start(s16[2,464,128]{2,1,0:T(8,128)(2,1)S(1)} %get-tuple-element.84), channel_id=1, source_target_pairs={{0,1},{1,0},{2,3},{3,2},{4,5},{5,4},{6,7},{7,6},{8,9},{9,8},{10,11... | collective-permute-start | bytes 712712 | tf_op jit(solution)/shard_map/ppermute | solution.py:394
  28.4 6.9 %collective-permute-start.11 = (s16[1,480,128]{2,1,0:T(8,128)(2,1)S(1)}, s16[1,480,128]{2,1,0:T(8,128)(2,1)S(1)}, u32[]{:S(2)}, u32[]{:S(2)}) collective-permute-start(s16[1,480,128]{2,1,0:T(8,128)(2,1)S(1)} %get-tuple-element.89), channel_id=1, source_target_pairs={{0,4},{1,5},{2,6},{3,7},{4,0},{5,1},{6,2},{7,3},{8,12},{9,13},{10,... | collective-permute-start | bytes 368648 | tf_op jit(solution)/shard_map/ppermute | solution.py:394
  31.8 6.3 %collective-permute-start.10 = (s16[1,480,128]{2,1,0:T(8,128)(2,1)S(1)}, s16[1,480,128]{2,1,0:T(8,128)(2,1)S(1)}, u32[]{:S(2)}, u32[]{:S(2)}) collective-permute-start(s16[1,480,128]{2,1,0:T(8,128)(2,1)S(1)} %pass_sums.3), channel_id=1, source_target_pairs={{0,2},{1,3},{2,0},{3,1},{4,6},{5,7},{6,4},{7,5},{8,10},{9,11},{10,... | collective-permute-start | bytes 368648 | tf_op jit(solution)/shard_map/ppermute | solution.py:394
  33.4 7.2 %collective-permute-start.12 = (s16[1,464,128]{2,1,0:T(8,128)(2,1)S(1)}, s16[1,464,128]{2,1,0:T(8,128)(2,1)S(1)}, u32[]{:S(2)}, u32[]{:S(2)}) collective-permute-start(s16[1,464,128]{2,1,0:T(8,128)(2,1)S(1)} %get-tuple-element.93), channel_id=1, source_target_pairs={{0,2},{1,3},{2,0},{3,1},{4,6},{5,7},{6,4},{7,5},{8,10},{9,11},{10,... | collective-permute-start | bytes 356360 | tf_op jit(solution)/shard_map/ppermute | solution.py:394
  33.8 8.1 %collective-permute-start.6 = (s16[2,464,128]{2,1,0:T(8,128)(2,1)S(1)}, s16[2,464,128]{2,1,0:T(8,128)(2,1)S(1)}, u32[]{:S(2)}, u32[]{:S(2)}) collective-permute-start(s16[2,464,128]{2,1,0:T(8,128)(2,1)S(1)} %get-tuple-element.83), channel_id=1, source_target_pairs={{0,1},{1,0},{2,3},{3,2},{4,5},{5,4},{6,7},{7,6},{8,9},{9,8},{10,11... | collective-permute-start | bytes 712712 | tf_op jit(solution)/shard_map/ppermute | solution.py:394
  38.2 8.0 %collective-permute-start.14 = (s16[1,480,128]{2,1,0:T(8,128)(2,1)S(1)}, s16[1,480,128]{2,1,0:T(8,128)(2,1)S(1)}, u32[]{:S(2)}, u32[]{:S(2)}) collective-permute-start(s16[1,480,128]{2,1,0:T(8,128)(2,1)S(1)} %get-tuple-element.98), channel_id=1, source_target_pairs={{0,4},{1,5},{2,6},{3,7},{4,0},{5,1},{6,2},{7,3},{8,12},{9,13},{10,... | collective-permute-start | bytes 368648 | tf_op jit(solution)/shard_map/ppermute | solution.py:394
  40.6 5.6 %collective-permute-start.13 = (s16[1,464,128]{2,1,0:T(8,128)(2,1)S(1)}, s16[1,464,128]{2,1,0:T(8,128)(2,1)S(1)}, u32[]{:S(2)}, u32[]{:S(2)}) collective-permute-start(s16[1,464,128]{2,1,0:T(8,128)(2,1)S(1)} %get-tuple-element.97), channel_id=1, source_target_pairs={{0,2},{1,3},{2,0},{3,1},{4,6},{5,7},{6,4},{7,5},{8,10},{9,11},{10,... | collective-permute-start | bytes 356360 | tf_op jit(solution)/shard_map/ppermute | solution.py:394

commit v6 on v5

--- a/solution.py
+++ b/solution.py
@@ -37,7 +37,9 @@
         q = jnp.round(v * inverse[None]).astype(jnp.int32)
         codes.append(code.astype(jnp.int32))
         out[part * size : (part + 1) * size, :] = q.reshape(size, cols).astype(I16)
-    out[rows : rows + 8 * parts, :] = jnp.concatenate(codes, axis=0).astype(I16)
+    codes = codes * 2 if parts == 1 else codes
+    fill = [jnp.zeros_like(codes[0])] * ((out.shape[0] - rows) // 8 - len(codes))
+    out[rows:, :] = jnp.concatenate(codes + fill, axis=0).astype(I16)
 
 
 def unpack_scales(block, rows, parts=2):
@@ -118,8 +120,30 @@
 
 
 def smooth_and_pick(ratios, shape, tile, prod, bv_ref, first_ref, pad, first_plane, count, write):
+    tiles = shape[0] * shape[1] // tile
+    picks = bv_ref.shape[0] - tile - 8
+    total = first_ref.shape[0]
+    most = jnp.int32(0)
+    for i in range(count * tiles):
+        number = first_plane * tiles + i
+        after = jnp.where(number + 1 < total, first_ref[jnp.minimum(number + 1, total - 1)], picks)
+        most = jnp.maximum(most, after - (first_ref[number] // 8) * 8)
+    short = tile // 4 * 3 + 4
+    args = (ratios, shape, tile, prod, bv_ref, first_ref, pad, first_plane, count, write)
+
+    @pl.when(most <= short)
+    def _():
+        smooth_tiles(short, *args)
+
+    @pl.when(most > short)
+    def _():
+        smooth_tiles(tile + 8, *args)
+
+
+def smooth_tiles(
+    window, ratios, shape, tile, prod, bv_ref, first_ref, pad, first_plane, count, write
+):
     width_x, width_y = shape
-    window = tile + 8
     r1, r2 = ratios
     stride = width_y + 8
     for side in range(2):
@@ -217,20 +241,25 @@
         for k, d in enumerate(piece):
             theirs_at = pl.multiple_of((2 * (z ^ d) + 1 - mine) * share, 8)
             mine_at = pl.multiple_of((2 * (z ^ d) + mine) * share, 8)
-            parts = (send.shape[1] - share) // 8
+            parts = parts_of(send.shape[1], share)
             pack_block(picked[pl.ds(theirs_at, share), :], send.at[skip + k], parts)
             keep[k] = picked[pl.ds(mine_at, share), :]
 
 
+def parts_of(total, rows):
+    parts = (total - rows) // 8
+    return parts if rows // parts % 16 == 0 else 1
+
+
 def unpack_block(block, rows):
-    parts = (block.shape[0] - rows) // 8
+    parts = parts_of(block.shape[0], rows)
     scales = unpack_scales(block, rows, parts)
     pieces = [unpack_part(block, rows, part, scales, parts) for part in range(parts)]
     return jnp.concatenate(pieces, axis=0)
 
 
 def pass_kernel(share, got_ref, keep_ref, out_ref):
-    parts = (out_ref.shape[1] - share) // 8
+    parts = parts_of(out_ref.shape[1], share)
     for k in range(got_ref.shape[0]):
         pack_block(keep_ref[k] + unpack_block(got_ref.at[k], share), out_ref.at[k], parts)
 
@@ -241,7 +270,7 @@
         total = keep_ref[k] + unpack_block(got_ref.at[k], share)
         total = total + unpack_block(near_ref.at[k], share)
         if k % 2:
-            pack_block(total, send_out[0].at[k // 2])
+            pack_block(total, send_out[0].at[k // 2], parts_of(send_out[0].shape[1], share))
         else:
             keep_out[k // 2] = total
 
@@ -250,7 +279,7 @@
     for k in range(got_ref.shape[0]):
         total = keep_ref[k] + unpack_block(got_ref.at[k], share)
         if k % 2:
-            pack_block(total, send_out[0].at[k // 2])
+            pack_block(total, send_out[0].at[k // 2], parts_of(send_out[0].shape[1], share))
         else:
             keep_out[k // 2] = total
 
@@ -260,7 +289,7 @@
         total = keep_ref[k] + unpack_block(got_ref.at[k], share)
         if k == 0:
             total = total + unpack_block(near_ref.at[0], share)
-        pack_block(total, out.at[0], (out.shape[1] - share) // 8)
+        pack_block(total, out.at[0], parts_of(out.shape[1], share))
 
 
 def last_kernel(scale, share, chunks, *refs):
@@ -393,10 +422,12 @@
     def across(value, mask):
         return lax.ppermute(value, "ta", [(i, i ^ mask) for i in range(n_ta)])
 
-    one, urgent = message_of(1), jax.ShapeDtypeStruct((1, share + 32, LANES), I16)
+    one, urgent, most_urgent = [
+        jax.ShapeDtypeStruct((1, share + extra, LANES), I16) for extra in (16, 32, 64)
+    ]
 
     def finish(near_got, side, kept, before=None):
-        shapes = [urgent, one]
+        shapes = [urgent if before else most_urgent, one]
         far, near = sums(short_join_kernel, shapes, (side[0], kept[0], near_got), "join_sums")
         if before is not None:
             near, before[-2] = lax.optimization_barrier((near, before[-2]))
@@ -447,11 +478,11 @@
             cost_estimate=COST,
             name="outer_rows",
         )(held, far, picked, wide, first, *ends)[2:]
-        sent, kept = rows[: len(pieces)], rows[len(pieces) :]
+        sent, kept = list(rows[: len(pieces)]), rows[len(pieces) :]
         if short:
             done = None
             if waiting:
-                waiting[0], *sent = lax.optimization_barrier((waiting[0], *sent))
+                waiting[0], *sent[1:] = lax.optimization_barrier((waiting[0], *sent[1:]))
                 done, result = finish(*waiting)
                 results += result
             side = [across(value, 1) for value in sent[:-1]]

time: 47.3 us -> 46.6 us (0.985)
  waiting for transfers between devices: 8.62 us -> 6.29 us
  starting transfers between devices: 21.3 us -> 23.5 us
  Pallas kernels: 17 us -> 16.2 us
    ppermute x11, waiting for transfers between devices: 8.61 us -> 6.22 us  [across(): return lax.ppermute(value, 'ta', [(i, i ^ mask) for i in range(n_ta)])]
    ppermute x11, starting transfers between devices: 16.3 us -> 18.6 us  [across(): return lax.ppermute(value, 'ta', [(i, i ^ mask) for i in range(n_ta)])]
    pallas_call x2, Pallas kernels: 4.69 us -> 4.21 us  [shards(): pl.pallas_call(functools.partial(outer_kernel, ratios, (width_x, width_y)...]
  transfers between devices with their start and end apart: 15 -> 15, of which waited for: 5 -> 5; matrix products, arithmetic and copies ran while one was open for 0% -> 0% of each run, Pallas kernels for 29% -> 28%
where the time goes in v6:
time: 46.6 us; the launch traced here: 46.4 us
  starting transfers between devices  23.5 us (50%)
  Pallas kernels  16.2 us (35%)
  waiting for transfers between devices  6.29 us (13%)
    ppermute x11, starting transfers between devices, across(): return lax.ppermute(value, 'ta', [(i, i ^ mask) for i in range(n_ta)])  18.6 us
    pallas_call x2, Pallas kernels, shards(): pl.pallas_call(functools.partial(inner_rows_kernel, ratios, (width_x, wid...  6.41 us
    ppermute x11, waiting for transfers between devices, across(): return lax.ppermute(value, 'ta', [(i, i ^ mask) for i in range(n_ta)])  6.22 us
    ppermute x2, starting transfers between devices, shards(): far = lax.ppermute(messages[2 * c], ('gz', 'ta'), odd_pairs)  4.28 us
    pallas_call x2, Pallas kernels, shards(): pl.pallas_call(functools.partial(outer_kernel, ratios, (width_x, width_y)...  4.21 us
    pallas_call x1, Pallas kernels, shards(): pl.pallas_call(functools.partial(far_kernel, planes, cells, chunks, packs...  2.39 us
    pallas_call x2, Pallas kernels, more_products(): pl.pallas_call(functools.partial(kernel, planes, cells, chunks, packs_of)...  1.71 us
    pallas_call x1, Pallas kernels, shards(): pl.pallas_call(functools.partial(short_last_kernel if short else last_ker...  0.98 us
  transfers between devices with their start and end apart: 15, of which 5 were waited for; matrix products, arithmetic and copies ran while one was open for 0% of the time, Pallas kernels for 28%

profile of v6, /device:TPU:0, one launch (start us, length us, event | category | flops | bytes accessed | tf_op | source)
XLA Modules:
  0.0 46.4 jit_solution(15744001052918640219)
XLA Ops:
  0.0 2.4 %far_products.1 = (s16[2,992,128]{2,1,0:T(8,128)(2,1)S(1)}, s32[28,128]{1,0:T(8,128)S(1)}, s32[3832,128]{1,0:T(8,128)S(1)}, bf16[384,256]{1,0:T(8,128)(2,1)S(1)}...) custom-call(bf16[5760,384]{1,0:T(8,128)(2,1)} %bitcast.3, bf16[384,256]{1,0:T(8,128)(2,1)} %w_hbm.1, ...), custom_call_target="tpu_custom_call" | custom-call | tf_op jit(solution)/shard_map/far_products/pallas_call | solution.py:356
  2.4 3.1 %collective-permute-start.1 = (s16[2,992,128]{2,1,0:T(8,128)(2,1)S(1)}, s16[2,992,128]{2,1,0:T(8,128)(2,1)S(1)}, u32[]{:S(2)}, u32[]{:S(2)}) collective-permute-start(s16[2,992,128]{2,1,0:T(8,128)(2,1)S(1)} %get-tuple-element.62), channel_id=1, source_target_pairs={{0,2},{1,3},{2,0},{3,1},{4,6},{5,7},{6,4},{7,5},{8,16},{9,17},{10,... | collective-permute-start | bytes 1523720 | tf_op jit(solution)/shard_map/ppermute | solution.py:439
  5.5 0.8 %near_products.1 = (s16[2,976,128]{2,1,0:T(8,128)(2,1)S(1)}, f32[10,960,128]{2,1,0:T(8,128)S(1)}, f32[10,960,128]{2,1,0:T(8,128)S(1)}) custom-call(bf16[5760,384]{1,0:T(8,128)(2,1)S(1)} %bitcast.4, bf16[384,256]{1,0:T(8,128)(2,1)S(1)} %get-tuple-element.51.w_ref, ...), custom_call_target="tpu_custom_call", output_to_operand_aliasing={{1}: (2, {}), {2}: (3, {})} | custom-call | tf_op jit(solution)/shard_map/near_products/pallas_call | solution.py:373
  6.4 1.0 %middle_products.1 = (s16[2,992,128]{2,1,0:T(8,128)(2,1)S(1)}, s16[2,976,128]{2,1,0:T(8,128)(2,1)S(1)}, f32[10,960,128]{2,1,0:T(8,128)S(1)}, f32[10,960,128]{2,1,0:T(8,128)S(1)}) custom-call(bf16[5760,384]{1,0:T(8,128)(2,1)S(1)} %bitcast.5, bf16[384,256]{1,0:T(8,128)(2,1)S(1)} %get-tuple-element.51.w_ref, ...), custom_call_target="tpu_custom_call", output_to_operand_aliasing={{2}: (2, {}), {3}: (3, {})} | custom-call | tf_op jit(solution)/shard_map/middle_products/pallas_call | solution.py:373
  7.3 0.5 %collective-permute-start.2 = (s16[2,976,128]{2,1,0:T(8,128)(2,1)S(1)}, s16[2,976,128]{2,1,0:T(8,128)(2,1)S(1)}, u32[]{:S(2)}, u32[]{:S(2)}) collective-permute-start(s16[2,976,128]{2,1,0:T(8,128)(2,1)S(1)} %get-tuple-element.71), channel_id=1, source_target_pairs={{0,8},{8,0},{16,24},{24,16},{1,9},{9,1},{17,25},{25,17},{2,10},{10... | collective-permute-start | bytes 1499144 | tf_op jit(solution)/shard_map/ppermute | solution.py:438
  7.9 1.2 %collective-permute-start.5 = (s16[2,992,128]{2,1,0:T(8,128)(2,1)S(1)}, s16[2,992,128]{2,1,0:T(8,128)(2,1)S(1)}, u32[]{:S(2)}, u32[]{:S(2)}) collective-permute-start(s16[2,992,128]{2,1,0:T(8,128)(2,1)S(1)} %get-tuple-element.77), channel_id=1, source_target_pairs={{0,2},{1,3},{2,0},{3,1},{4,6},{5,7},{6,4},{7,5},{8,16},{9,17},{10,... | collective-permute-start | bytes 1523720 | tf_op jit(solution)/shard_map/ppermute | solution.py:439
  9.3 3.1 %inner_rows.2 = (f32[10,960,128]{2,1,0:T(8,128)S(1)}, f32[3832,128]{1,0:T(8,128)S(1)}) custom-call(f32[10,960,128]{2,1,0:T(8,128)S(1)} %get-tuple-element.57._, s16[2,976,128]{2,1,0:T(8,128)(2,1)S(1)} %collective-permute-done.near_ref, s32[3832,128]{1,0:T(8,128)S(1)} %get-tuple-element.59.bv_ref.refs_3_, ...), custom_call_target="tpu_custom_call", output_to_operand_aliasing={{0}: (0, {})} | custom-call | tf_op jit(solution)/shard_map/inner_rows/pallas_call | solution.py:443
  12.5 2.1 %outer_rows.2 = (f32[10,960,128]{2,1,0:T(8,128)S(1)}, f32[3832,128]{1,0:T(8,128)S(1)}, s16[1,464,128]{2,1,0:T(8,128)(2,1)S(1)}, s16[2,480,128]{2,1,0:T(8,128)(2,...) custom-call(f32[10,960,128]{2,1,0:T(8,128)S(1)} %get-tuple-element.6, ...), custom_call_target="tpu_custom_call", output_to_operand_aliasing={{0}: (0, {}), {1}: (2, {})} | custom-call | tf_op jit(solution)/shard_map/outer_rows/pallas_call | solution.py:468
  14.6 2.0 %collective-permute-start.3 = (s16[1,464,128]{2,1,0:T(8,128)(2,1)S(1)}, s16[1,464,128]{2,1,0:T(8,128)(2,1)S(1)}, u32[]{:S(2)}, u32[]{:S(2)}) collective-permute-start(s16[1,464,128]{2,1,0:T(8,128)(2,1)S(1)} %get-tuple-element.64), channel_id=1, source_target_pairs={{0,1},{1,0},{2,3},{3,2},{4,5},{5,4},{6,7},{7,6},{8,9},{9,8},{10,11... | collective-permute-start | bytes 356360 | tf_op jit(solution)/shard_map/ppermute | solution.py:423
  16.7 3.3 %inner_rows.3 = (f32[10,960,128]{2,1,0:T(8,128)S(1)}, f32[3832,128]{1,0:T(8,128)S(1)}) custom-call(f32[10,960,128]{2,1,0:T(8,128)S(1)} %get-tuple-element.70._, s16[2,976,128]{2,1,0:T(8,128)(2,1)S(1)} %collective-permute-done.2.near_ref, s32[3832,128]{1,0:T(8,128)S(1)} %get-tuple-element.59.bv_ref.refs_3_, ...), custom_call_target="tpu_custom_call", output_to_operand_aliasing={{0}: (0, {})} | custom-call | tf_op jit(solution)/shard_map/inner_rows/pallas_call | solution.py:443
  20.0 0.8 %collective-permute-done.3.got_ref = s16[1,464,128]{2,1,0:T(8,128)(2,1)S(1)} collective-permute-done((s16[1,464,128]{2,1,0:T(8,128)(2,1)S(1)}, s16[1,464,128]{2,1,0:T(8,128)(2,1)S(1)}, u32[]{:S(2)}, u32[]{:S(2)}) %collective-permute-start.3) | collective-permute-done | bytes 118816 | tf_op jit(solution)/shard_map/ppermute | solution.py:423
  20.8 2.1 %collective-permute-start.4 = (s16[1,480,128]{2,1,0:T(8,128)(2,1)S(1)}, s16[1,480,128]{2,1,0:T(8,128)(2,1)S(1)}, u32[]{:S(2)}, u32[]{:S(2)}) collective-permute-start(s16[1,480,128]{2,1,0:T(8,128)(2,1)S(1)} %pass_sums.2), channel_id=1, source_target_pairs={{0,2},{1,3},{2,0},{3,1},{4,6},{5,7},{6,4},{7,5},{8,10},{9,11},{10,... | collective-permute-start | bytes 368648 | tf_op jit(solution)/shard_map/ppermute | solution.py:423
  23.0 2.1 %outer_rows.3 = (f32[10,960,128]{2,1,0:T(8,128)S(1)}, f32[3832,128]{1,0:T(8,128)S(1)}, s16[1,464,128]{2,1,0:T(8,128)(2,1)S(1)}, s16[2,464,128]{2,1,0:T(8,128)(2,...) custom-call(f32[10,960,128]{2,1,0:T(8,128)S(1)} %get-tuple-element.7, ...), custom_call_target="tpu_custom_call", output_to_operand_aliasing={{0}: (0, {}), {1}: (2, {})} | custom-call | tf_op jit(solution)/shard_map/outer_rows/pallas_call | solution.py:468
  25.1 1.6 %collective-permute-start.8 = (s16[1,464,128]{2,1,0:T(8,128)(2,1)S(1)}, s16[1,464,128]{2,1,0:T(8,128)(2,1)S(1)}, u32[]{:S(2)}, u32[]{:S(2)}) collective-permute-start(s16[1,464,128]{2,1,0:T(8,128)(2,1)S(1)} %get-tuple-element.84), channel_id=1, source_target_pairs={{0,1},{1,0},{2,3},{3,2},{4,5},{5,4},{6,7},{7,6},{8,9},{9,8},{10,11... | collective-permute-start | bytes 356360 | tf_op jit(solution)/shard_map/ppermute | solution.py:423
  26.6 1.1 %collective-permute-start.7 = (s16[2,464,128]{2,1,0:T(8,128)(2,1)S(1)}, s16[2,464,128]{2,1,0:T(8,128)(2,1)S(1)}, u32[]{:S(2)}, u32[]{:S(2)}) collective-permute-start(s16[2,464,128]{2,1,0:T(8,128)(2,1)S(1)} %get-tuple-element.82), channel_id=1, source_target_pairs={{0,1},{1,0},{2,3},{3,2},{4,5},{5,4},{6,7},{7,6},{8,9},{9,8},{10,11... | collective-permute-start | bytes 712712 | tf_op jit(solution)/shard_map/ppermute | solution.py:423
  28.0 2.7 %collective-permute-start.11 = (s16[1,512,128]{2,1,0:T(8,128)(2,1)S(1)}, s16[1,512,128]{2,1,0:T(8,128)(2,1)S(1)}, u32[]{:S(2)}, u32[]{:S(2)}) collective-permute-start(s16[1,512,128]{2,1,0:T(8,128)(2,1)S(1)} %get-tuple-element.87), channel_id=1, source_target_pairs={{0,4},{1,5},{2,6},{3,7},{4,0},{5,1},{6,2},{7,3},{8,12},{9,13},{10,... | collective-permute-start | bytes 393224 | tf_op jit(solution)/shard_map/ppermute | solution.py:423
  30.9 1.5 %collective-permute-start.10 = (s16[1,480,128]{2,1,0:T(8,128)(2,1)S(1)}, s16[1,480,128]{2,1,0:T(8,128)(2,1)S(1)}, u32[]{:S(2)}, u32[]{:S(2)}) collective-permute-start(s16[1,480,128]{2,1,0:T(8,128)(2,1)S(1)} %pass_sums.3), channel_id=1, source_target_pairs={{0,2},{1,3},{2,0},{3,1},{4,6},{5,7},{6,4},{7,5},{8,10},{9,11},{10,... | collective-permute-start | bytes 368648 | tf_op jit(solution)/shard_map/ppermute | solution.py:423
  32.4 0.6 %collective-permute-start.12 = (s16[1,464,128]{2,1,0:T(8,128)(2,1)S(1)}, s16[1,464,128]{2,1,0:T(8,128)(2,1)S(1)}, u32[]{:S(2)}, u32[]{:S(2)}) collective-permute-start(s16[1,464,128]{2,1,0:T(8,128)(2,1)S(1)} %get-tuple-element.91), channel_id=1, source_target_pairs={{0,2},{1,3},{2,0},{3,1},{4,6},{5,7},{6,4},{7,5},{8,10},{9,11},{10,... | collective-permute-start | bytes 356360 | tf_op jit(solution)/shard_map/ppermute | solution.py:423
  33.0 1.5 %collective-permute-start.6 = (s16[2,464,128]{2,1,0:T(8,128)(2,1)S(1)}, s16[2,464,128]{2,1,0:T(8,128)(2,1)S(1)}, u32[]{:S(2)}, u32[]{:S(2)}) collective-permute-start(s16[2,464,128]{2,1,0:T(8,128)(2,1)S(1)} %get-tuple-element.81), channel_id=1, source_target_pairs={{0,1},{1,0},{2,3},{3,2},{4,5},{5,4},{6,7},{7,6},{8,9},{9,8},{10,11... | collective-permute-start | bytes 712712 | tf_op jit(solution)/shard_map/ppermute | solution.py:423
  34.5 2.4 %collective-permute-done.10.near_ref = s16[1,480,128]{2,1,0:T(8,128)(2,1)S(1)} collective-permute-done((s16[1,480,128]{2,1,0:T(8,128)(2,1)S(1)}, s16[1,480,128]{2,1,0:T(8,128)(2,1)S(1)}, u32[]{:S(2)}, u32[]{:S(2)}) %collective-permute-start.10) | collective-permute-done | bytes 122912 | tf_op jit(solution)/shard_map/ppermute | solution.py:423
  37.1 2.8 %collective-permute-start.14 = (s16[1,480,128]{2,1,0:T(8,128)(2,1)S(1)}, s16[1,480,128]{2,1,0:T(8,128)(2,1)S(1)}, u32[]{:S(2)}, u32[]{:S(2)}) collective-permute-start(s16[1,480,128]{2,1,0:T(8,128)(2,1)S(1)} %get-tuple-element.96), channel_id=1, source_target_pairs={{0,4},{1,5},{2,6},{3,7},{4,0},{5,1},{6,2},{7,3},{8,12},{9,13},{10,... | collective-permute-start | bytes 368648 | tf_op jit(solution)/shard_map/ppermute | solution.py:423
  39.9 2.7 %collective-permute-start.13 = (s16[1,464,128]{2,1,0:T(8,128)(2,1)S(1)}, s16[1,464,128]{2,1,0:T(8,128)(2,1)S(1)}, u32[]{:S(2)}, u32[]{:S(2)}) collective-permute-start(s16[1,464,128]{2,1,0:T(8,128)(2,1)S(1)} %get-tuple-element.95), channel_id=1, source_target_pairs={{0,2},{1,3},{2,0},{3,1},{4,6},{5,7},{6,4},{7,5},{8,10},{9,11},{10,... | collective-permute-start | bytes 356360 | tf_op jit(solution)/shard_map/ppermute | solution.py:423
  42.6 2.8 %collective-permute-done.13.refs_4_ = s16[1,464,128]{2,1,0:T(8,128)(2,1)S(1)} collective-permute-done((s16[1,464,128]{2,1,0:T(8,128)(2,1)S(1)}, s16[1,464,128]{2,1,0:T(8,128)(2,1)S(1)}, u32[]{:S(2)}, u32[]{:S(2)}) %collective-permute-start.13) | collective-permute-done | bytes 118816 | tf_op jit(solution)/shard_map/ppermute | solution.py:423
  45.4 1.0 %last_sums.1 = f32[448,256]{1,0:T(8,128)} custom-call(s16[2,464,128]{2,1,0:T(8,128)(2,1)S(1)} %collective-permute-done.6.side_ref, f32[1,448,128]{2,1,0:T(8,128)S(1)} %get-tuple-element.69.refs_0_, s16[1,464,128]{2,1,0:T(8,128)(2,1)S(1)} %collective-permute-done.12.refs_1_, s16[1,512,128]{2,1,0:T(8,128)(2,1)S(1)} %collective-permute-done.11.refs_2_, ...), custom_call_target="tpu_custom_call" | custom-call | tf_op jit(solution)/shard_map/last_sums/pallas_call | solution.py:515
  (22 shorter events, 1.3 us)
Async XLA Ops:
  0.0 5.5 %copy-start = (bf16[6,24,40,384]{3,2,1,0:T(8,128)(2,1)S(1)}, bf16[6,24,40,384]{3,2,1,0:T(8,128)(2,1)}, u32[]{:S(2)}) copy-start(bf16[6,24,40,384]{3,2,1,0:T(8,128)(2,1)} %param.3) | copy-start | bytes 13271044
  2.4 10.1 %collective-permute-start.1 = (s16[2,992,128]{2,1,0:T(8,128)(2,1)S(1)}, s16[2,992,128]{2,1,0:T(8,128)(2,1)S(1)}, u32[]{:S(2)}, u32[]{:S(2)}) collective-permute-start(s16[2,992,128]{2,1,0:T(8,128)(2,1)S(1)} %get-tuple-element.62), channel_id=1, source_target_pairs={{0,2},{1,3},{2,0},{3,1},{4,6},{5,7},{6,4},{7,5},{8,16},{9,17},{10,... | collective-permute-start | bytes 1523720 | tf_op jit(solution)/shard_map/ppermute | solution.py:439
  6.3 3.0 %collective-permute-start = (s16[2,976,128]{2,1,0:T(8,128)(2,1)S(1)}, s16[2,976,128]{2,1,0:T(8,128)(2,1)S(1)}, u32[]{:S(2)}, u32[]{:S(2)}) collective-permute-start(s16[2,976,128]{2,1,0:T(8,128)(2,1)S(1)} %get-tuple-element.58), channel_id=1, source_target_pairs={{0,8},{8,0},{16,24},{24,16},{1,9},{9,1},{17,25},{25,17},{2,10},{10... | collective-permute-start | bytes 1499144 | tf_op jit(solution)/shard_map/ppermute | solution.py:438
  7.3 9.3 %collective-permute-start.2 = (s16[2,976,128]{2,1,0:T(8,128)(2,1)S(1)}, s16[2,976,128]{2,1,0:T(8,128)(2,1)S(1)}, u32[]{:S(2)}, u32[]{:S(2)}) collective-permute-start(s16[2,976,128]{2,1,0:T(8,128)(2,1)S(1)} %get-tuple-element.71), channel_id=1, source_target_pairs={{0,8},{8,0},{16,24},{24,16},{1,9},{9,1},{17,25},{25,17},{2,10},{10... | collective-permute-start | bytes 1499144 | tf_op jit(solution)/shard_map/ppermute | solution.py:438
  7.9 15.1 %collective-permute-start.5 = (s16[2,992,128]{2,1,0:T(8,128)(2,1)S(1)}, s16[2,992,128]{2,1,0:T(8,128)(2,1)S(1)}, u32[]{:S(2)}, u32[]{:S(2)}) collective-permute-start(s16[2,992,128]{2,1,0:T(8,128)(2,1)S(1)} %get-tuple-element.77), channel_id=1, source_target_pairs={{0,2},{1,3},{2,0},{3,1},{4,6},{5,7},{6,4},{7,5},{8,16},{9,17},{10,... | collective-permute-start | bytes 1523720 | tf_op jit(solution)/shard_map/ppermute | solution.py:439
  14.6 6.2 %collective-permute-start.3 = (s16[1,464,128]{2,1,0:T(8,128)(2,1)S(1)}, s16[1,464,128]{2,1,0:T(8,128)(2,1)S(1)}, u32[]{:S(2)}, u32[]{:S(2)}) collective-permute-start(s16[1,464,128]{2,1,0:T(8,128)(2,1)S(1)} %get-tuple-element.64), channel_id=1, source_target_pairs={{0,1},{1,0},{2,3},{3,2},{4,5},{5,4},{6,7},{7,6},{8,9},{9,8},{10,11... | collective-permute-start | bytes 356360 | tf_op jit(solution)/shard_map/ppermute | solution.py:423
  16.6 11.2 %collective-permute-start.9 = (s16[2,480,128]{2,1,0:T(8,128)(2,1)S(1)}, s16[2,480,128]{2,1,0:T(8,128)(2,1)S(1)}, u32[]{:S(2)}, u32[]{:S(2)}) collective-permute-start(s16[2,480,128]{2,1,0:T(8,128)(2,1)S(1)} %get-tuple-element.65), channel_id=1, source_target_pairs={{0,1},{1,0},{2,3},{3,2},{4,5},{5,4},{6,7},{7,6},{8,9},{9,8},{10,11... | collective-permute-start | bytes 737288 | tf_op jit(solution)/shard_map/ppermute | solution.py:423
  20.8 5.8 %collective-permute-start.4 = (s16[1,480,128]{2,1,0:T(8,128)(2,1)S(1)}, s16[1,480,128]{2,1,0:T(8,128)(2,1)S(1)}, u32[]{:S(2)}, u32[]{:S(2)}) collective-permute-start(s16[1,480,128]{2,1,0:T(8,128)(2,1)S(1)} %pass_sums.2), channel_id=1, source_target_pairs={{0,2},{1,3},{2,0},{3,1},{4,6},{5,7},{6,4},{7,5},{8,10},{9,11},{10,... | collective-permute-start | bytes 368648 | tf_op jit(solution)/shard_map/ppermute | solution.py:423
  25.1 5.7 %collective-permute-start.8 = (s16[1,464,128]{2,1,0:T(8,128)(2,1)S(1)}, s16[1,464,128]{2,1,0:T(8,128)(2,1)S(1)}, u32[]{:S(2)}, u32[]{:S(2)}) collective-permute-start(s16[1,464,128]{2,1,0:T(8,128)(2,1)S(1)} %get-tuple-element.84), channel_id=1, source_target_pairs={{0,1},{1,0},{2,3},{3,2},{4,5},{5,4},{6,7},{7,6},{8,9},{9,8},{10,11... | collective-permute-start | bytes 356360 | tf_op jit(solution)/shard_map/ppermute | solution.py:423
  26.6 10.3 %collective-permute-start.7 = (s16[2,464,128]{2,1,0:T(8,128)(2,1)S(1)}, s16[2,464,128]{2,1,0:T(8,128)(2,1)S(1)}, u32[]{:S(2)}, u32[]{:S(2)}) collective-permute-start(s16[2,464,128]{2,1,0:T(8,128)(2,1)S(1)} %get-tuple-element.82), channel_id=1, source_target_pairs={{0,1},{1,0},{2,3},{3,2},{4,5},{5,4},{6,7},{7,6},{8,9},{9,8},{10,11... | collective-permute-start | bytes 712712 | tf_op jit(solution)/shard_map/ppermute | solution.py:423
  28.0 9.0 %collective-permute-start.11 = (s16[1,512,128]{2,1,0:T(8,128)(2,1)S(1)}, s16[1,512,128]{2,1,0:T(8,128)(2,1)S(1)}, u32[]{:S(2)}, u32[]{:S(2)}) collective-permute-start(s16[1,512,128]{2,1,0:T(8,128)(2,1)S(1)} %get-tuple-element.87), channel_id=1, source_target_pairs={{0,4},{1,5},{2,6},{3,7},{4,0},{5,1},{6,2},{7,3},{8,12},{9,13},{10,... | collective-permute-start | bytes 393224 | tf_op jit(solution)/shard_map/ppermute | solution.py:423
  30.9 6.0 %collective-permute-start.10 = (s16[1,480,128]{2,1,0:T(8,128)(2,1)S(1)}, s16[1,480,128]{2,1,0:T(8,128)(2,1)S(1)}, u32[]{:S(2)}, u32[]{:S(2)}) collective-permute-start(s16[1,480,128]{2,1,0:T(8,128)(2,1)S(1)} %pass_sums.3), channel_id=1, source_target_pairs={{0,2},{1,3},{2,0},{3,1},{4,6},{5,7},{6,4},{7,5},{8,10},{9,11},{10,... | collective-permute-start | bytes 368648 | tf_op jit(solution)/shard_map/ppermute | solution.py:423
  32.4 7.6 %collective-permute-start.12 = (s16[1,464,128]{2,1,0:T(8,128)(2,1)S(1)}, s16[1,464,128]{2,1,0:T(8,128)(2,1)S(1)}, u32[]{:S(2)}, u32[]{:S(2)}) collective-permute-start(s16[1,464,128]{2,1,0:T(8,128)(2,1)S(1)} %get-tuple-element.91), channel_id=1, source_target_pairs={{0,2},{1,3},{2,0},{3,1},{4,6},{5,7},{6,4},{7,5},{8,10},{9,11},{10,... | collective-permute-start | bytes 356360 | tf_op jit(solution)/shard_map/ppermute | solution.py:423
  33.0 9.6 %collective-permute-start.6 = (s16[2,464,128]{2,1,0:T(8,128)(2,1)S(1)}, s16[2,464,128]{2,1,0:T(8,128)(2,1)S(1)}, u32[]{:S(2)}, u32[]{:S(2)}) collective-permute-start(s16[2,464,128]{2,1,0:T(8,128)(2,1)S(1)} %get-tuple-element.81), channel_id=1, source_target_pairs={{0,1},{1,0},{2,3},{3,2},{4,5},{5,4},{6,7},{7,6},{8,9},{9,8},{10,11... | collective-permute-start | bytes 712712 | tf_op jit(solution)/shard_map/ppermute | solution.py:423
  37.1 8.3 %collective-permute-start.14 = (s16[1,480,128]{2,1,0:T(8,128)(2,1)S(1)}, s16[1,480,128]{2,1,0:T(8,128)(2,1)S(1)}, u32[]{:S(2)}, u32[]{:S(2)}) collective-permute-start(s16[1,480,128]{2,1,0:T(8,128)(2,1)S(1)} %get-tuple-element.96), channel_id=1, source_target_pairs={{0,4},{1,5},{2,6},{3,7},{4,0},{5,1},{6,2},{7,3},{8,12},{9,13},{10,... | collective-permute-start | bytes 368648 | tf_op jit(solution)/shard_map/ppermute | solution.py:423
  39.9 5.5 %collective-permute-start.13 = (s16[1,464,128]{2,1,0:T(8,128)(2,1)S(1)}, s16[1,464,128]{2,1,0:T(8,128)(2,1)S(1)}, u32[]{:S(2)}, u32[]{:S(2)}) collective-permute-start(s16[1,464,128]{2,1,0:T(8,128)(2,1)S(1)} %get-tuple-element.95), channel_id=1, source_target_pairs={{0,2},{1,3},{2,0},{3,1},{4,6},{5,7},{6,4},{7,5},{8,10},{9,11},{10,... | collective-permute-start | bytes 356360 | tf_op jit(solution)/shard_map/ppermute | solution.py:423

commit v7 on v6

--- a/solution.py
+++ b/solution.py
@@ -300,13 +300,19 @@
         out_ref[:, c * LANES : (c + 1) * LANES] = value * scale
 
 
-def short_last_kernel(scale, share, chunks, side_ref, *refs):
-    out_ref = refs[-1]
-    for c in range(chunks):
-        own, near, far = refs[3 * c : 3 * c + 3]
-        value = own[0] + unpack_block(side_ref.at[c], share)
-        value = value + unpack_block(near.at[0], share) + unpack_block(far.at[0], share)
-        out_ref[:, c * LANES : (c + 1) * LANES] = value * scale
+def column_kernel(scale, share, chunk, side_ref, own, near, far, *refs):
+    out_hbm, buf, sem = refs[-3:]
+    half = share // 2
+    parts = [unpack_block(ref, share) for ref in (side_ref.at[chunk], near.at[0], far.at[0])]
+    copies = []
+    for k in range(2):
+        rows = slice(k * half, (k + 1) * half)
+        buf[rows, :] = (own[0, rows, :] + sum(part[rows] for part in parts)) * scale
+        place = out_hbm.at[pl.ds(k * half, half), pl.ds(chunk * LANES, LANES)]
+        copies.append(pltpu.make_async_copy(buf.at[pl.ds(k * half, half), :], place, sem.at[k]))
+        copies[-1].start()
+    for copy in copies:
+        copy.wait()
 
 
 def shards(volume, sketch_matrix, brain_voxels):
@@ -423,7 +429,7 @@
         return lax.ppermute(value, "ta", [(i, i ^ mask) for i in range(n_ta)])
 
     one, urgent, most_urgent = [
-        jax.ShapeDtypeStruct((1, share + extra, LANES), I16) for extra in (16, 32, 64)
+        jax.ShapeDtypeStruct((1, share + extra, LANES), I16) for extra in (16, 32, 48)
     ]
 
     def finish(near_got, side, kept, before=None):
@@ -451,11 +457,6 @@
             cost_estimate=COST,
             name="inner_rows",
         )(held, near, wide, first)
-        if waiting:
-            picked, waiting[1] = lax.optimization_barrier((picked, waiting[1]))
-            out = sums(pass_kernel, [urgent], waiting[:2], "pass_sums")[0]
-            picked, out = lax.optimization_barrier((picked, out))
-            waiting[:2] = [across(out, 2)]
         if short:
             pieces = ((3,), (2, 1), (0,))
         else:
@@ -463,8 +464,6 @@
         counts = [len(piece) for piece in pieces]
         ends = carried if c == chunks - 1 else []
         sent = [message_of(count) for count in counts[:-1]] + [message_of(counts[-1] + len(ends))]
-        if short and not waiting:
-            sent[1] = jax.ShapeDtypeStruct((counts[1], share + 32, LANES), I16)
         rows = pl.pallas_call(
             functools.partial(
                 outer_kernel, ratios, (width_x, width_y), planes, tile, share, pieces, len(ends)
@@ -482,8 +481,10 @@
         if short:
             done = None
             if waiting:
-                waiting[0], *sent[1:] = lax.optimization_barrier((waiting[0], *sent[1:]))
-                done, result = finish(*waiting)
+                waiting[1], *sent = lax.optimization_barrier((waiting[1], *sent))
+                (out,) = sums(pass_kernel, [urgent], waiting[:2], "pass_sums")
+                out, *sent = lax.optimization_barrier((out, *sent))
+                done, result = finish(across(out, 2), *waiting[2:])
                 results += result
             side = [across(value, 1) for value in sent[:-1]]
             if done is not None:
@@ -512,11 +513,31 @@
                 mask *= 2
             results += [keep, across(out, mask)]
 
+    result = jax.ShapeDtypeStruct((share, rank), F32)
+    if short:
+        outs = []
+        for c in range(chunks):
+            args = [results[0]] + results[1 + 3 * c : 4 + 3 * c]
+            outs = [
+                pl.pallas_call(
+                    functools.partial(column_kernel, taps[2] ** 3, share, c),
+                    out_shape=result,
+                    in_specs=[vmem] * len(args) + [hbm] * len(outs),
+                    out_specs=hbm,
+                    input_output_aliases={len(args): 0} if outs else {},
+                    scratch_shapes=[
+                        pltpu.VMEM((share, LANES), F32),
+                        pltpu.SemaphoreType.DMA((2,)),
+                    ],
+                    compiler_params=VMEM,
+                    cost_estimate=COST,
+                    name="result_columns",
+                )(*args, *outs)
+            ]
+        return outs[0]
     return pl.pallas_call(
-        functools.partial(
-            short_last_kernel if short else last_kernel, taps[2] ** 3, share, chunks
-        ),
-        out_shape=jax.ShapeDtypeStruct((share, rank), F32),
+        functools.partial(last_kernel, taps[2] ** 3, share, chunks),
+        out_shape=result,
         in_specs=[vmem] * len(results),
         out_specs=vmem,
         compiler_params=VMEM,

time: 46.6 us -> 45.9 us (0.985)
  starting transfers between devices: 23.5 us -> 19.9 us
  waiting for transfers between devices: 6.29 us -> 8.58 us
  Pallas kernels: 16.2 us -> 16.8 us
    ppermute x11, starting transfers between devices: 18.6 us -> 15 us  [across(): return lax.ppermute(value, 'ta', [(i, i ^ mask) for i in range(n_ta)])]
    ppermute x11, waiting for transfers between devices: 6.22 us -> 8.42 us  [across(): return lax.ppermute(value, 'ta', [(i, i ^ mask) for i in range(n_ta)])]
    pallas_call x1 -> x2, Pallas kernels: 0.98 us -> 1.54 us  [shards(): pl.pallas_call(functools.partial(column_kernel, taps[2] ** 3, share, c),...]
    ppermute x2, starting transfers between devices: 0.65 us -> 0.12 us  [shards(): near = lax.ppermute(messages[2 * c + 1], 'gz', even_pairs)]
  transfers between devices with their start and end apart: 15 -> 15, of which waited for: 5 -> 5; matrix products, arithmetic and copies ran while one was open for 0% -> 0% of each run, Pallas kernels for 28% -> 30%
where the time goes in v7:
time: 45.9 us; the launch traced here: 45.7 us
  starting transfers between devices  19.9 us (43%)
  Pallas kernels  16.8 us (37%)
  waiting for transfers between devices  8.58 us (19%)
    ppermute x11, starting transfers between devices, across(): return lax.ppermute(value, 'ta', [(i, i ^ mask) for i in range(n_ta)])  15 us
    ppermute x11, waiting for transfers between devices, across(): return lax.ppermute(value, 'ta', [(i, i ^ mask) for i in range(n_ta)])  8.42 us
    pallas_call x2, Pallas kernels, shards(): pl.pallas_call(functools.partial(inner_rows_kernel, ratios, (width_x, wid...  6.38 us
    ppermute x2, starting transfers between devices, shards(): far = lax.ppermute(messages[2 * c], ('gz', 'ta'), odd_pairs)  4.73 us
    pallas_call x2, Pallas kernels, shards(): pl.pallas_call(functools.partial(outer_kernel, ratios, (width_x, width_y)...  4.23 us
    pallas_call x1, Pallas kernels, shards(): pl.pallas_call(functools.partial(far_kernel, planes, cells, chunks, packs...  2.39 us
    pallas_call x2, Pallas kernels, more_products(): pl.pallas_call(functools.partial(kernel, planes, cells, chunks, packs_of)...  1.71 us
    pallas_call x2, Pallas kernels, shards(): pl.pallas_call(functools.partial(column_kernel, taps[2] ** 3, share, c),...  1.54 us
  transfers between devices with their start and end apart: 15, of which 5 were waited for; matrix products, arithmetic and copies ran while one was open for 0% of the time, Pallas kernels for 30%

profile of v7, /device:TPU:0, one launch (start us, length us, event | category | flops | bytes accessed | tf_op | source)
XLA Modules:
  0.0 45.7 jit_solution(6762824142350406114)
XLA Ops:
  0.0 2.4 %far_products.1 = (s16[2,992,128]{2,1,0:T(8,128)(2,1)S(1)}, s32[28,128]{1,0:T(8,128)S(1)}, s32[3832,128]{1,0:T(8,128)S(1)}, bf16[384,256]{1,0:T(8,128)(2,1)S(1)}...) custom-call(bf16[5760,384]{1,0:T(8,128)(2,1)} %bitcast.3, bf16[384,256]{1,0:T(8,128)(2,1)} %w_hbm.1, ...), custom_call_target="tpu_custom_call" | custom-call | tf_op jit(solution)/shard_map/far_products/pallas_call | solution.py:362
  2.4 3.1 %collective-permute-start.1 = (s16[2,992,128]{2,1,0:T(8,128)(2,1)S(1)}, s16[2,992,128]{2,1,0:T(8,128)(2,1)S(1)}, u32[]{:S(2)}, u32[]{:S(2)}) collective-permute-start(s16[2,992,128]{2,1,0:T(8,128)(2,1)S(1)} %get-tuple-element.62), channel_id=1, source_target_pairs={{0,2},{1,3},{2,0},{3,1},{4,6},{5,7},{6,4},{7,5},{8,16},{9,17},{10,... | collective-permute-start | bytes 1523720 | tf_op jit(solution)/shard_map/ppermute | solution.py:445
  5.5 0.8 %near_products.1 = (s16[2,976,128]{2,1,0:T(8,128)(2,1)S(1)}, f32[10,960,128]{2,1,0:T(8,128)S(1)}, f32[10,960,128]{2,1,0:T(8,128)S(1)}) custom-call(bf16[5760,384]{1,0:T(8,128)(2,1)S(1)} %bitcast.4, bf16[384,256]{1,0:T(8,128)(2,1)S(1)} %get-tuple-element.52.w_ref, ...), custom_call_target="tpu_custom_call", output_to_operand_aliasing={{1}: (2, {}), {2}: (3, {})} | custom-call | tf_op jit(solution)/shard_map/near_products/pallas_call | solution.py:379
  6.4 1.0 %middle_products.1 = (s16[2,992,128]{2,1,0:T(8,128)(2,1)S(1)}, s16[2,976,128]{2,1,0:T(8,128)(2,1)S(1)}, f32[10,960,128]{2,1,0:T(8,128)S(1)}, f32[10,960,128]{2,1,0:T(8,128)S(1)}) custom-call(bf16[5760,384]{1,0:T(8,128)(2,1)S(1)} %bitcast.5, bf16[384,256]{1,0:T(8,128)(2,1)S(1)} %get-tuple-element.52.w_ref, ...), custom_call_target="tpu_custom_call", output_to_operand_aliasing={{2}: (2, {}), {3}: (3, {})} | custom-call | tf_op jit(solution)/shard_map/middle_products/pallas_call | solution.py:379
  7.3 1.6 %collective-permute-start.4 = (s16[2,992,128]{2,1,0:T(8,128)(2,1)S(1)}, s16[2,992,128]{2,1,0:T(8,128)(2,1)S(1)}, u32[]{:S(2)}, u32[]{:S(2)}) collective-permute-start(s16[2,992,128]{2,1,0:T(8,128)(2,1)S(1)} %get-tuple-element.74), channel_id=1, source_target_pairs={{0,2},{1,3},{2,0},{3,1},{4,6},{5,7},{6,4},{7,5},{8,16},{9,17},{10,... | collective-permute-start | bytes 1523720 | tf_op jit(solution)/shard_map/ppermute | solution.py:445
  9.2 3.1 %inner_rows.2 = (f32[10,960,128]{2,1,0:T(8,128)S(1)}, f32[3832,128]{1,0:T(8,128)S(1)}) custom-call(f32[10,960,128]{2,1,0:T(8,128)S(1)} %get-tuple-element.57._, s16[2,976,128]{2,1,0:T(8,128)(2,1)S(1)} %collective-permute-done.near_ref, s32[3832,128]{1,0:T(8,128)S(1)} %get-tuple-element.59.bv_ref.refs_3_, ...), custom_call_target="tpu_custom_call", output_to_operand_aliasing={{0}: (0, {})} | custom-call | tf_op jit(solution)/shard_map/inner_rows/pallas_call | solution.py:449
  12.5 2.1 %outer_rows.2 = (f32[10,960,128]{2,1,0:T(8,128)S(1)}, f32[3832,128]{1,0:T(8,128)S(1)}, s16[1,464,128]{2,1,0:T(8,128)(2,1)S(1)}, s16[2,464,128]{2,1,0:T(8,128)(2,...) custom-call(f32[10,960,128]{2,1,0:T(8,128)S(1)} %get-tuple-element.6, ...), custom_call_target="tpu_custom_call", output_to_operand_aliasing={{0}: (0, {}), {1}: (2, {})} | custom-call | tf_op jit(solution)/shard_map/outer_rows/pallas_call | solution.py:467
  14.6 2.0 %collective-permute-start.2 = (s16[1,464,128]{2,1,0:T(8,128)(2,1)S(1)}, s16[1,464,128]{2,1,0:T(8,128)(2,1)S(1)}, u32[]{:S(2)}, u32[]{:S(2)}) collective-permute-start(s16[1,464,128]{2,1,0:T(8,128)(2,1)S(1)} %get-tuple-element.64), channel_id=1, source_target_pairs={{0,1},{1,0},{2,3},{3,2},{4,5},{5,4},{6,7},{7,6},{8,9},{9,8},{10,11... | collective-permute-start | bytes 356360 | tf_op jit(solution)/shard_map/ppermute | solution.py:429
  16.7 3.3 %inner_rows.3 = (f32[10,960,128]{2,1,0:T(8,128)S(1)}, f32[3832,128]{1,0:T(8,128)S(1)}) custom-call(f32[10,960,128]{2,1,0:T(8,128)S(1)} %get-tuple-element.71._, s16[2,976,128]{2,1,0:T(8,128)(2,1)S(1)} %collective-permute-done.3.near_ref, s32[3832,128]{1,0:T(8,128)S(1)} %get-tuple-element.59.bv_ref.refs_3_, ...), custom_call_target="tpu_custom_call", output_to_operand_aliasing={{0}: (0, {})} | custom-call | tf_op jit(solution)/shard_map/inner_rows/pallas_call | solution.py:449
  20.0 2.1 %outer_rows.3 = (f32[10,960,128]{2,1,0:T(8,128)S(1)}, f32[3832,128]{1,0:T(8,128)S(1)}, s16[1,464,128]{2,1,0:T(8,128)(2,1)S(1)}, s16[2,464,128]{2,1,0:T(8,128)(2,...) custom-call(f32[10,960,128]{2,1,0:T(8,128)S(1)} %get-tuple-element.7, ...), custom_call_target="tpu_custom_call", output_to_operand_aliasing={{0}: (0, {}), {1}: (2, {})} | custom-call | tf_op jit(solution)/shard_map/outer_rows/pallas_call | solution.py:467
  22.2 2.1 %collective-permute-start.9 = (s16[1,480,128]{2,1,0:T(8,128)(2,1)S(1)}, s16[1,480,128]{2,1,0:T(8,128)(2,1)S(1)}, u32[]{:S(2)}, u32[]{:S(2)}) collective-permute-start(s16[1,480,128]{2,1,0:T(8,128)(2,1)S(1)} %pass_sums.2), channel_id=1, source_target_pairs={{0,2},{1,3},{2,0},{3,1},{4,6},{5,7},{6,4},{7,5},{8,10},{9,11},{10,... | collective-permute-start | bytes 368648 | tf_op jit(solution)/shard_map/ppermute | solution.py:429
  24.3 1.5 %collective-permute-start.7 = (s16[1,464,128]{2,1,0:T(8,128)(2,1)S(1)}, s16[1,464,128]{2,1,0:T(8,128)(2,1)S(1)}, u32[]{:S(2)}, u32[]{:S(2)}) collective-permute-start(s16[1,464,128]{2,1,0:T(8,128)(2,1)S(1)} %get-tuple-element.87), channel_id=1, source_target_pairs={{0,1},{1,0},{2,3},{3,2},{4,5},{5,4},{6,7},{7,6},{8,9},{9,8},{10,11... | collective-permute-start | bytes 356360 | tf_op jit(solution)/shard_map/ppermute | solution.py:429
  25.8 0.5 %collective-permute-start.6 = (s16[2,464,128]{2,1,0:T(8,128)(2,1)S(1)}, s16[2,464,128]{2,1,0:T(8,128)(2,1)S(1)}, u32[]{:S(2)}, u32[]{:S(2)}) collective-permute-start(s16[2,464,128]{2,1,0:T(8,128)(2,1)S(1)} %get-tuple-element.85), channel_id=1, source_target_pairs={{0,1},{1,0},{2,3},{3,2},{4,5},{5,4},{6,7},{7,6},{8,9},{9,8},{10,11... | collective-permute-start | bytes 712712 | tf_op jit(solution)/shard_map/ppermute | solution.py:429
  26.3 1.0 %collective-permute-done.9.near_ref = s16[1,480,128]{2,1,0:T(8,128)(2,1)S(1)} collective-permute-done((s16[1,480,128]{2,1,0:T(8,128)(2,1)S(1)}, s16[1,480,128]{2,1,0:T(8,128)(2,1)S(1)}, u32[]{:S(2)}, u32[]{:S(2)}) %collective-permute-start.9) | collective-permute-done | bytes 122912 | tf_op jit(solution)/shard_map/ppermute | solution.py:429
  27.5 2.9 %collective-permute-start.11 = (s16[1,496,128]{2,1,0:T(8,128)(2,1)S(1)}, s16[1,496,128]{2,1,0:T(8,128)(2,1)S(1)}, u32[]{:S(2)}, u32[]{:S(2)}) collective-permute-start(s16[1,496,128]{2,1,0:T(8,128)(2,1)S(1)} %get-tuple-element.90), channel_id=1, source_target_pairs={{0,4},{1,5},{2,6},{3,7},{4,0},{5,1},{6,2},{7,3},{8,12},{9,13},{10,... | collective-permute-start | bytes 380936 | tf_op jit(solution)/shard_map/ppermute | solution.py:429
  30.6 1.6 %collective-permute-start.10 = (s16[1,480,128]{2,1,0:T(8,128)(2,1)S(1)}, s16[1,480,128]{2,1,0:T(8,128)(2,1)S(1)}, u32[]{:S(2)}, u32[]{:S(2)}) collective-permute-start(s16[1,480,128]{2,1,0:T(8,128)(2,1)S(1)} %pass_sums.3), channel_id=1, source_target_pairs={{0,2},{1,3},{2,0},{3,1},{4,6},{5,7},{6,4},{7,5},{8,10},{9,11},{10,... | collective-permute-start | bytes 368648 | tf_op jit(solution)/shard_map/ppermute | solution.py:429
  32.2 0.5 %collective-permute-start.12 = (s16[1,464,128]{2,1,0:T(8,128)(2,1)S(1)}, s16[1,464,128]{2,1,0:T(8,128)(2,1)S(1)}, u32[]{:S(2)}, u32[]{:S(2)}) collective-permute-start(s16[1,464,128]{2,1,0:T(8,128)(2,1)S(1)} %get-tuple-element.94), channel_id=1, source_target_pairs={{0,2},{1,3},{2,0},{3,1},{4,6},{5,7},{6,4},{7,5},{8,10},{9,11},{10,... | collective-permute-start | bytes 356360 | tf_op jit(solution)/shard_map/ppermute | solution.py:429
  32.7 1.5 %collective-permute-start.5 = (s16[2,464,128]{2,1,0:T(8,128)(2,1)S(1)}, s16[2,464,128]{2,1,0:T(8,128)(2,1)S(1)}, u32[]{:S(2)}, u32[]{:S(2)}) collective-permute-start(s16[2,464,128]{2,1,0:T(8,128)(2,1)S(1)} %get-tuple-element.83), channel_id=1, source_target_pairs={{0,1},{1,0},{2,3},{3,2},{4,5},{5,4},{6,7},{7,6},{8,9},{9,8},{10,11... | collective-permute-start | bytes 712712 | tf_op jit(solution)/shard_map/ppermute | solution.py:429
  34.1 3.1 %collective-permute-done.10.near_ref = s16[1,480,128]{2,1,0:T(8,128)(2,1)S(1)} collective-permute-done((s16[1,480,128]{2,1,0:T(8,128)(2,1)S(1)}, s16[1,480,128]{2,1,0:T(8,128)(2,1)S(1)}, u32[]{:S(2)}, u32[]{:S(2)}) %collective-permute-start.10) | collective-permute-done | bytes 122912 | tf_op jit(solution)/shard_map/ppermute | solution.py:429
  37.4 0.9 %collective-permute-start.14 = (s16[1,480,128]{2,1,0:T(8,128)(2,1)S(1)}, s16[1,480,128]{2,1,0:T(8,128)(2,1)S(1)}, u32[]{:S(2)}, u32[]{:S(2)}) collective-permute-start(s16[1,480,128]{2,1,0:T(8,128)(2,1)S(1)} %get-tuple-element.96), channel_id=1, source_target_pairs={{0,4},{1,5},{2,6},{3,7},{4,0},{5,1},{6,2},{7,3},{8,12},{9,13},{10,... | collective-permute-start | bytes 368648 | tf_op jit(solution)/shard_map/ppermute | solution.py:429
  38.7 1.4 %collective-permute-start.13 = (s16[1,464,128]{2,1,0:T(8,128)(2,1)S(1)}, s16[1,464,128]{2,1,0:T(8,128)(2,1)S(1)}, u32[]{:S(2)}, u32[]{:S(2)}) collective-permute-start(s16[1,464,128]{2,1,0:T(8,128)(2,1)S(1)} %get-tuple-element.95), channel_id=1, source_target_pairs={{0,2},{1,3},{2,0},{3,1},{4,6},{5,7},{6,4},{7,5},{8,10},{9,11},{10,... | collective-permute-start | bytes 356360 | tf_op jit(solution)/shard_map/ppermute | solution.py:429
  40.1 0.8 %result_columns.2.refs_0_ = f32[448,256]{1,0:T(8,128)} custom-call(s16[2,464,128]{2,1,0:T(8,128)(2,1)S(1)} %collective-permute-done.5.side_ref, f32[1,448,128]{2,1,0:T(8,128)S(1)} %get-tuple-element.70.own, s16[1,464,128]{2,1,0:T(8,128)(2,1)S(1)} %collective-permute-done.12.near, s16[1,496,128]{2,1,0:T(8,128)(2,1)S(1)} %collective-permute-done.11.far), custom_call_target="tpu_custom_call" | custom-call | tf_op jit(solution)/shard_map/result_columns/pallas_call | solution.py:522
  40.8 4.0 %collective-permute-done.13.near = s16[1,464,128]{2,1,0:T(8,128)(2,1)S(1)} collective-permute-done((s16[1,464,128]{2,1,0:T(8,128)(2,1)S(1)}, s16[1,464,128]{2,1,0:T(8,128)(2,1)S(1)}, u32[]{:S(2)}, u32[]{:S(2)}) %collective-permute-start.13) | collective-permute-done | bytes 118816 | tf_op jit(solution)/shard_map/ppermute | solution.py:429
  44.8 0.8 %result_columns.3 = f32[448,256]{1,0:T(8,128)} custom-call(s16[2,464,128]{2,1,0:T(8,128)(2,1)S(1)} %collective-permute-done.5.side_ref, f32[1,448,128]{2,1,0:T(8,128)S(1)} %get-tuple-element.84.own, s16[1,464,128]{2,1,0:T(8,128)(2,1)S(1)} %collective-permute-done.13.near, ...), custom_call_target="tpu_custom_call", output_to_operand_aliasing={{}: (4, {})} | custom-call | tf_op jit(solution)/shard_map/result_columns/pallas_call | solution.py:522
  (23 shorter events, 1.5 us)
Async XLA Ops:
  0.0 5.5 %copy-start = (bf16[6,24,40,384]{3,2,1,0:T(8,128)(2,1)S(1)}, bf16[6,24,40,384]{3,2,1,0:T(8,128)(2,1)}, u32[]{:S(2)}) copy-start(bf16[6,24,40,384]{3,2,1,0:T(8,128)(2,1)} %param.3) | copy-start | bytes 13271044
  2.4 10.1 %collective-permute-start.1 = (s16[2,992,128]{2,1,0:T(8,128)(2,1)S(1)}, s16[2,992,128]{2,1,0:T(8,128)(2,1)S(1)}, u32[]{:S(2)}, u32[]{:S(2)}) collective-permute-start(s16[2,992,128]{2,1,0:T(8,128)(2,1)S(1)} %get-tuple-element.62), channel_id=1, source_target_pairs={{0,2},{1,3},{2,0},{3,1},{4,6},{5,7},{6,4},{7,5},{8,16},{9,17},{10,... | collective-permute-start | bytes 1523720 | tf_op jit(solution)/shard_map/ppermute | solution.py:445
  6.3 3.0 %collective-permute-start = (s16[2,976,128]{2,1,0:T(8,128)(2,1)S(1)}, s16[2,976,128]{2,1,0:T(8,128)(2,1)S(1)}, u32[]{:S(2)}, u32[]{:S(2)}) collective-permute-start(s16[2,976,128]{2,1,0:T(8,128)(2,1)S(1)} %get-tuple-element.58), channel_id=1, source_target_pairs={{0,8},{8,0},{16,24},{24,16},{1,9},{9,1},{17,25},{25,17},{2,10},{10... | collective-permute-start | bytes 1499144 | tf_op jit(solution)/shard_map/ppermute | solution.py:444
  7.3 12.7 %collective-permute-start.4 = (s16[2,992,128]{2,1,0:T(8,128)(2,1)S(1)}, s16[2,992,128]{2,1,0:T(8,128)(2,1)S(1)}, u32[]{:S(2)}, u32[]{:S(2)}) collective-permute-start(s16[2,992,128]{2,1,0:T(8,128)(2,1)S(1)} %get-tuple-element.74), channel_id=1, source_target_pairs={{0,2},{1,3},{2,0},{3,1},{4,6},{5,7},{6,4},{7,5},{8,16},{9,17},{10,... | collective-permute-start | bytes 1523720 | tf_op jit(solution)/shard_map/ppermute | solution.py:445
  9.0 7.7 %collective-permute-start.3 = (s16[2,976,128]{2,1,0:T(8,128)(2,1)S(1)}, s16[2,976,128]{2,1,0:T(8,128)(2,1)S(1)}, u32[]{:S(2)}, u32[]{:S(2)}) collective-permute-start(s16[2,976,128]{2,1,0:T(8,128)(2,1)S(1)} %get-tuple-element.72), channel_id=1, source_target_pairs={{0,8},{8,0},{16,24},{24,16},{1,9},{9,1},{17,25},{25,17},{2,10},{10... | collective-permute-start | bytes 1499144 | tf_op jit(solution)/shard_map/ppermute | solution.py:444
  14.6 7.5 %collective-permute-start.2 = (s16[1,464,128]{2,1,0:T(8,128)(2,1)S(1)}, s16[1,464,128]{2,1,0:T(8,128)(2,1)S(1)}, u32[]{:S(2)}, u32[]{:S(2)}) collective-permute-start(s16[1,464,128]{2,1,0:T(8,128)(2,1)S(1)} %get-tuple-element.64), channel_id=1, source_target_pairs={{0,1},{1,0},{2,3},{3,2},{4,5},{5,4},{6,7},{7,6},{8,9},{9,8},{10,11... | collective-permute-start | bytes 356360 | tf_op jit(solution)/shard_map/ppermute | solution.py:429
  16.6 9.7 %collective-permute-start.8 = (s16[2,464,128]{2,1,0:T(8,128)(2,1)S(1)}, s16[2,464,128]{2,1,0:T(8,128)(2,1)S(1)}, u32[]{:S(2)}, u32[]{:S(2)}) collective-permute-start(s16[2,464,128]{2,1,0:T(8,128)(2,1)S(1)} %get-tuple-element.67), channel_id=1, source_target_pairs={{0,1},{1,0},{2,3},{3,2},{4,5},{5,4},{6,7},{7,6},{8,9},{9,8},{10,11... | collective-permute-start | bytes 712712 | tf_op jit(solution)/shard_map/ppermute | solution.py:429
  22.2 5.1 %collective-permute-start.9 = (s16[1,480,128]{2,1,0:T(8,128)(2,1)S(1)}, s16[1,480,128]{2,1,0:T(8,128)(2,1)S(1)}, u32[]{:S(2)}, u32[]{:S(2)}) collective-permute-start(s16[1,480,128]{2,1,0:T(8,128)(2,1)S(1)} %pass_sums.2), channel_id=1, source_target_pairs={{0,2},{1,3},{2,0},{3,1},{4,6},{5,7},{6,4},{7,5},{8,10},{9,11},{10,... | collective-permute-start | bytes 368648 | tf_op jit(solution)/shard_map/ppermute | solution.py:429
  24.3 6.2 %collective-permute-start.7 = (s16[1,464,128]{2,1,0:T(8,128)(2,1)S(1)}, s16[1,464,128]{2,1,0:T(8,128)(2,1)S(1)}, u32[]{:S(2)}, u32[]{:S(2)}) collective-permute-start(s16[1,464,128]{2,1,0:T(8,128)(2,1)S(1)} %get-tuple-element.87), channel_id=1, source_target_pairs={{0,1},{1,0},{2,3},{3,2},{4,5},{5,4},{6,7},{7,6},{8,9},{9,8},{10,11... | collective-permute-start | bytes 356360 | tf_op jit(solution)/shard_map/ppermute | solution.py:429
  25.8 11.4 %collective-permute-start.6 = (s16[2,464,128]{2,1,0:T(8,128)(2,1)S(1)}, s16[2,464,128]{2,1,0:T(8,128)(2,1)S(1)}, u32[]{:S(2)}, u32[]{:S(2)}) collective-permute-start(s16[2,464,128]{2,1,0:T(8,128)(2,1)S(1)} %get-tuple-element.85), channel_id=1, source_target_pairs={{0,1},{1,0},{2,3},{3,2},{4,5},{5,4},{6,7},{7,6},{8,9},{9,8},{10,11... | collective-permute-start | bytes 712712 | tf_op jit(solution)/shard_map/ppermute | solution.py:429
  27.5 9.7 %collective-permute-start.11 = (s16[1,496,128]{2,1,0:T(8,128)(2,1)S(1)}, s16[1,496,128]{2,1,0:T(8,128)(2,1)S(1)}, u32[]{:S(2)}, u32[]{:S(2)}) collective-permute-start(s16[1,496,128]{2,1,0:T(8,128)(2,1)S(1)} %get-tuple-element.90), channel_id=1, source_target_pairs={{0,4},{1,5},{2,6},{3,7},{4,0},{5,1},{6,2},{7,3},{8,12},{9,13},{10,... | collective-permute-start | bytes 380936 | tf_op jit(solution)/shard_map/ppermute | solution.py:429
  30.6 6.7 %collective-permute-start.10 = (s16[1,480,128]{2,1,0:T(8,128)(2,1)S(1)}, s16[1,480,128]{2,1,0:T(8,128)(2,1)S(1)}, u32[]{:S(2)}, u32[]{:S(2)}) collective-permute-start(s16[1,480,128]{2,1,0:T(8,128)(2,1)S(1)} %pass_sums.3), channel_id=1, source_target_pairs={{0,2},{1,3},{2,0},{3,1},{4,6},{5,7},{6,4},{7,5},{8,10},{9,11},{10,... | collective-permute-start | bytes 368648 | tf_op jit(solution)/shard_map/ppermute | solution.py:429
  32.2 6.5 %collective-permute-start.12 = (s16[1,464,128]{2,1,0:T(8,128)(2,1)S(1)}, s16[1,464,128]{2,1,0:T(8,128)(2,1)S(1)}, u32[]{:S(2)}, u32[]{:S(2)}) collective-permute-start(s16[1,464,128]{2,1,0:T(8,128)(2,1)S(1)} %get-tuple-element.94), channel_id=1, source_target_pairs={{0,2},{1,3},{2,0},{3,1},{4,6},{5,7},{6,4},{7,5},{8,10},{9,11},{10,... | collective-permute-start | bytes 356360 | tf_op jit(solution)/shard_map/ppermute | solution.py:429
  32.7 7.4 %collective-permute-start.5 = (s16[2,464,128]{2,1,0:T(8,128)(2,1)S(1)}, s16[2,464,128]{2,1,0:T(8,128)(2,1)S(1)}, u32[]{:S(2)}, u32[]{:S(2)}) collective-permute-start(s16[2,464,128]{2,1,0:T(8,128)(2,1)S(1)} %get-tuple-element.83), channel_id=1, source_target_pairs={{0,1},{1,0},{2,3},{3,2},{4,5},{5,4},{6,7},{7,6},{8,9},{9,8},{10,11... | collective-permute-start | bytes 712712 | tf_op jit(solution)/shard_map/ppermute | solution.py:429
  37.4 7.4 %collective-permute-start.14 = (s16[1,480,128]{2,1,0:T(8,128)(2,1)S(1)}, s16[1,480,128]{2,1,0:T(8,128)(2,1)S(1)}, u32[]{:S(2)}, u32[]{:S(2)}) collective-permute-start(s16[1,480,128]{2,1,0:T(8,128)(2,1)S(1)} %get-tuple-element.96), channel_id=1, source_target_pairs={{0,4},{1,5},{2,6},{3,7},{4,0},{5,1},{6,2},{7,3},{8,12},{9,13},{10,... | collective-permute-start | bytes 368648 | tf_op jit(solution)/shard_map/ppermute | solution.py:429
  38.7 6.1 %collective-permute-start.13 = (s16[1,464,128]{2,1,0:T(8,128)(2,1)S(1)}, s16[1,464,128]{2,1,0:T(8,128)(2,1)S(1)}, u32[]{:S(2)}, u32[]{:S(2)}) collective-permute-start(s16[1,464,128]{2,1,0:T(8,128)(2,1)S(1)} %get-tuple-element.95), channel_id=1, source_target_pairs={{0,2},{1,3},{2,0},{3,1},{4,6},{5,7},{6,4},{7,5},{8,10},{9,11},{10,... | collective-permute-start | bytes 356360 | tf_op jit(solution)/shard_map/ppermute | solution.py:429

commit v8 on v7

--- a/solution.py
+++ b/solution.py
@@ -61,17 +61,17 @@
 
 
 def multiply_planes(source, weights, prods, slots, first, cells):
+    rows = pl.ds(pl.multiple_of(first * cells, cells), len(slots) * cells)
+    product = jnp.dot(source[rows, :], weights[...], preferred_element_type=F32)
     for i, slot in enumerate(slots):
-        rows = pl.ds(pl.multiple_of((first + i) * cells, cells), cells)
-        product = jnp.dot(source[rows, :], weights[...], preferred_element_type=F32)
         for c, prod in enumerate(prods):
-            prod[slot] = product[:, c * LANES : (c + 1) * LANES]
+            prod[slot] = product[i * cells : (i + 1) * cells, c * LANES : (c + 1) * LANES]
 
 
 def far_kernel(
-    planes, cells, chunks, packs_of, v_hbm, w_hbm, bv_hbm, msg_ref, bv_ref, wide_ref, w_ref, *refs
+    planes, cells, chunks, packs_of, v_hbm, w_hbm, bv_hbm, msg_ref, first_ref, wide_ref, w_ref, *refs
 ):
-    prods, buf, sem = refs[:chunks], refs[chunks], refs[chunks + 1]
+    prods, (buf, bv_ref, sem) = refs[:chunks], refs[chunks:]
     odd = lax.axis_index("gz") % 2
     far = (planes - 2) * odd
     load_bv = pltpu.make_async_copy(bv_hbm, bv_ref, sem.at[0])
@@ -86,6 +86,10 @@
     for k in range(rows):
         spread = jnp.broadcast_to(bv_ref[k : k + 1, :], (lanes, lanes))
         wide_ref[k * lanes : (k + 1) * lanes, :] = spread.T
+    tiles = first_ref.shape[0]
+    for t in range(tiles):
+        below = jnp.where(bv_ref[...] < t * (planes * cells // tiles), 1.0, 0.0)
+        first_ref[t] = jnp.sum(below).astype(jnp.int32)
     tail = wide_ref.shape[0] - rows * lanes
     wide_ref[rows * lanes :, :] = jnp.full((tail, lanes), -1, jnp.int32)
     load_w.wait()
@@ -354,7 +358,7 @@
     picked_shape = jax.ShapeDtypeStruct((picks + window, LANES), F32)
     indices = brain_voxels.reshape(picks // LANES, LANES)
     shapes = message_shapes([0])[:1] + [
-        jax.ShapeDtypeStruct(indices.shape, jnp.int32),
+        jax.ShapeDtypeStruct((tiles,), jnp.int32),
         jax.ShapeDtypeStruct((picks + window, LANES), jnp.int32),
         jax.ShapeDtypeStruct((time_local, rank), jnp.bfloat16),
     ]
@@ -363,16 +367,17 @@
         functools.partial(far_kernel, planes, cells, chunks, packs_of),
         out_shape=shapes,
         in_specs=[hbm, hbm, hbm],
-        out_specs=[vmem] * len(shapes),
+        out_specs=[vmem, smem] + [vmem] * (len(shapes) - 2),
         scratch_shapes=[
             pltpu.VMEM((2 * cells, time_local), jnp.bfloat16),
+            pltpu.VMEM(indices.shape, jnp.int32),
             pltpu.SemaphoreType.DMA((3,)),
         ],
         compiler_params=VMEM,
         cost_estimate=COST,
         name="far_products",
     )(*[pltpu.with_memory_space_constraint(x, pltpu.HBM) for x in (flat, sketch_matrix, indices)])
-    far_message, indices, wide, weights = out[:4]
+    far_message, first, wide, weights = out[:4]
     prods = out[4:]
 
     def more_products(kernel, shapes, prods, name):
@@ -395,11 +400,6 @@
         middle_kernel, message_shapes(range(1, chunks)), prods, "middle_products"
     )
     messages = [far_message] + near_message + messages
-    first = jnp.sum(
-        indices.reshape(1, picks) < (jnp.arange(tiles, dtype=jnp.int32) * tile)[:, None],
-        axis=1,
-        dtype=jnp.int32,
-    )
 
     even_pairs = [(i, i ^ 1) for i in range(n_gz)]
     odd_pairs = []

time: 45.9 us -> 45 us (0.980)
  waiting for transfers between devices: 8.58 us -> 6.14 us
  starting transfers between devices: 19.9 us -> 21.7 us
    ppermute x11, waiting for transfers between devices: 8.42 us -> 5.75 us  [across(): return lax.ppermute(value, 'ta', [(i, i ^ mask) for i in range(n_ta)])]
    ppermute x11, starting transfers between devices: 15 us -> 16.8 us  [across(): return lax.ppermute(value, 'ta', [(i, i ^ mask) for i in range(n_ta)])]
where the time goes in v8:
time: 45 us; the launch traced here: 44.8 us
  starting transfers between devices  21.7 us (48%)
  Pallas kernels  16.8 us (37%)
  waiting for transfers between devices  6.14 us (14%)
    ppermute x11, starting transfers between devices, across(): return lax.ppermute(value, 'ta', [(i, i ^ mask) for i in range(n_ta)])  16.8 us
    pallas_call x2, Pallas kernels, shards(): pl.pallas_call(functools.partial(inner_rows_kernel, ratios, (width_x, wid...  6.39 us
    ppermute x11, waiting for transfers between devices, across(): return lax.ppermute(value, 'ta', [(i, i ^ mask) for i in range(n_ta)])  5.75 us
    ppermute x2, starting transfers between devices, shards(): far = lax.ppermute(messages[2 * c], ('gz', 'ta'), odd_pairs)  4.73 us
    pallas_call x2, Pallas kernels, shards(): pl.pallas_call(functools.partial(outer_kernel, ratios, (width_x, width_y)...  4.22 us
    pallas_call x1, Pallas kernels, shards(): pl.pallas_call(functools.partial(far_kernel, planes, cells, chunks, packs...  2.37 us
    pallas_call x2, Pallas kernels, more_products(): pl.pallas_call(functools.partial(kernel, planes, cells, chunks, packs_of)...  1.7 us
    pallas_call x2, Pallas kernels, shards(): pl.pallas_call(functools.partial(column_kernel, taps[2] ** 3, share, c),...  1.54 us
  transfers between devices with their start and end apart: 15, of which 5 were waited for; matrix products, arithmetic and copies ran while one was open for 0% of the time, Pallas kernels for 30%

profile of v8, /device:TPU:0, one launch (start us, length us, event | category | flops | bytes accessed | tf_op | source)
XLA Modules:
  0.0 44.8 jit_solution(17504231813522786698)
XLA Ops:
  0.0 2.4 %far_products.1 = (s16[2,992,128]{2,1,0:T(8,128)(2,1)S(1)}, s32[24]{0:T(128)S(1)}, s32[3832,128]{1,0:T(8,128)S(1)}, bf16[384,256]{1,0:T(8,128)(2,1)S(1)}, f32[10...) custom-call(bf16[5760,384]{1,0:T(8,128)(2,1)} %bitcast.2, bf16[384,256]{1,0:T(8,128)(2,1)} %w_hbm.1, s32[28,128]{1,0:T(8,128)} %bitcast.5), custom_call_target="tpu_custom_call" | custom-call | tf_op jit(solution)/shard_map/far_products/pallas_call | solution.py:366
  2.4 3.1 %collective-permute-start.1 = (s16[2,992,128]{2,1,0:T(8,128)(2,1)S(1)}, s16[2,992,128]{2,1,0:T(8,128)(2,1)S(1)}, u32[]{:S(2)}, u32[]{:S(2)}) collective-permute-start(s16[2,992,128]{2,1,0:T(8,128)(2,1)S(1)} %get-tuple-element.62), channel_id=1, source_target_pairs={{0,2},{1,3},{2,0},{3,1},{4,6},{5,7},{6,4},{7,5},{8,16},{9,17},{10,... | collective-permute-start | bytes 1523720 | tf_op jit(solution)/shard_map/ppermute | solution.py:445
  5.5 0.7 %near_products.1 = (s16[2,976,128]{2,1,0:T(8,128)(2,1)S(1)}, f32[10,960,128]{2,1,0:T(8,128)S(1)}, f32[10,960,128]{2,1,0:T(8,128)S(1)}) custom-call(bf16[5760,384]{1,0:T(8,128)(2,1)S(1)} %bitcast.3, bf16[384,256]{1,0:T(8,128)(2,1)S(1)} %get-tuple-element.52.w_ref, ...), custom_call_target="tpu_custom_call", output_to_operand_aliasing={{1}: (2, {}), {2}: (3, {})} | custom-call | tf_op jit(solution)/shard_map/near_products/pallas_call | solution.py:384
  6.3 1.0 %middle_products.1 = (s16[2,992,128]{2,1,0:T(8,128)(2,1)S(1)}, s16[2,976,128]{2,1,0:T(8,128)(2,1)S(1)}, f32[10,960,128]{2,1,0:T(8,128)S(1)}, f32[10,960,128]{2,1,0:T(8,128)S(1)}) custom-call(bf16[5760,384]{1,0:T(8,128)(2,1)S(1)} %bitcast.4, bf16[384,256]{1,0:T(8,128)(2,1)S(1)} %get-tuple-element.52.w_ref, ...), custom_call_target="tpu_custom_call", output_to_operand_aliasing={{2}: (2, {}), {3}: (3, {})} | custom-call | tf_op jit(solution)/shard_map/middle_products/pallas_call | solution.py:384
  7.3 1.6 %collective-permute-start.4 = (s16[2,992,128]{2,1,0:T(8,128)(2,1)S(1)}, s16[2,992,128]{2,1,0:T(8,128)(2,1)S(1)}, u32[]{:S(2)}, u32[]{:S(2)}) collective-permute-start(s16[2,992,128]{2,1,0:T(8,128)(2,1)S(1)} %get-tuple-element.74), channel_id=1, source_target_pairs={{0,2},{1,3},{2,0},{3,1},{4,6},{5,7},{6,4},{7,5},{8,16},{9,17},{10,... | collective-permute-start | bytes 1523720 | tf_op jit(solution)/shard_map/ppermute | solution.py:445
  9.0 3.1 %inner_rows.2 = (f32[10,960,128]{2,1,0:T(8,128)S(1)}, f32[3832,128]{1,0:T(8,128)S(1)}) custom-call(f32[10,960,128]{2,1,0:T(8,128)S(1)} %get-tuple-element.57._, s16[2,976,128]{2,1,0:T(8,128)(2,1)S(1)} %collective-permute-done.near_ref, s32[3832,128]{1,0:T(8,128)S(1)} %get-tuple-element.59.bv_ref.refs_3_, ...), custom_call_target="tpu_custom_call", output_to_operand_aliasing={{0}: (0, {})} | custom-call | tf_op jit(solution)/shard_map/inner_rows/pallas_call | solution.py:449
  12.5 2.1 %outer_rows.2 = (f32[10,960,128]{2,1,0:T(8,128)S(1)}, f32[3832,128]{1,0:T(8,128)S(1)}, s16[1,464,128]{2,1,0:T(8,128)(2,1)S(1)}, s16[2,464,128]{2,1,0:T(8,128)(2,...) custom-call(f32[10,960,128]{2,1,0:T(8,128)S(1)} %get-tuple-element.6, ...), custom_call_target="tpu_custom_call", output_to_operand_aliasing={{0}: (0, {}), {1}: (2, {})} | custom-call | tf_op jit(solution)/shard_map/outer_rows/pallas_call | solution.py:467
  14.6 2.0 %collective-permute-start.2 = (s16[1,464,128]{2,1,0:T(8,128)(2,1)S(1)}, s16[1,464,128]{2,1,0:T(8,128)(2,1)S(1)}, u32[]{:S(2)}, u32[]{:S(2)}) collective-permute-start(s16[1,464,128]{2,1,0:T(8,128)(2,1)S(1)} %get-tuple-element.64), channel_id=1, source_target_pairs={{0,1},{1,0},{2,3},{3,2},{4,5},{5,4},{6,7},{7,6},{8,9},{9,8},{10,11... | collective-permute-start | bytes 356360 | tf_op jit(solution)/shard_map/ppermute | solution.py:429
  16.7 3.3 %inner_rows.3 = (f32[10,960,128]{2,1,0:T(8,128)S(1)}, f32[3832,128]{1,0:T(8,128)S(1)}) custom-call(f32[10,960,128]{2,1,0:T(8,128)S(1)} %get-tuple-element.71._, s16[2,976,128]{2,1,0:T(8,128)(2,1)S(1)} %collective-permute-done.3.near_ref, s32[3832,128]{1,0:T(8,128)S(1)} %get-tuple-element.59.bv_ref.refs_3_, ...), custom_call_target="tpu_custom_call", output_to_operand_aliasing={{0}: (0, {})} | custom-call | tf_op jit(solution)/shard_map/inner_rows/pallas_call | solution.py:449
  20.0 2.1 %outer_rows.3 = (f32[10,960,128]{2,1,0:T(8,128)S(1)}, f32[3832,128]{1,0:T(8,128)S(1)}, s16[1,464,128]{2,1,0:T(8,128)(2,1)S(1)}, s16[2,464,128]{2,1,0:T(8,128)(2,...) custom-call(f32[10,960,128]{2,1,0:T(8,128)S(1)} %get-tuple-element.7, ...), custom_call_target="tpu_custom_call", output_to_operand_aliasing={{0}: (0, {}), {1}: (2, {})} | custom-call | tf_op jit(solution)/shard_map/outer_rows/pallas_call | solution.py:467
  22.2 2.1 %collective-permute-start.9 = (s16[1,480,128]{2,1,0:T(8,128)(2,1)S(1)}, s16[1,480,128]{2,1,0:T(8,128)(2,1)S(1)}, u32[]{:S(2)}, u32[]{:S(2)}) collective-permute-start(s16[1,480,128]{2,1,0:T(8,128)(2,1)S(1)} %pass_sums.2), channel_id=1, source_target_pairs={{0,2},{1,3},{2,0},{3,1},{4,6},{5,7},{6,4},{7,5},{8,10},{9,11},{10,... | collective-permute-start | bytes 368648 | tf_op jit(solution)/shard_map/ppermute | solution.py:429
  24.3 1.5 %collective-permute-start.7 = (s16[1,464,128]{2,1,0:T(8,128)(2,1)S(1)}, s16[1,464,128]{2,1,0:T(8,128)(2,1)S(1)}, u32[]{:S(2)}, u32[]{:S(2)}) collective-permute-start(s16[1,464,128]{2,1,0:T(8,128)(2,1)S(1)} %get-tuple-element.87), channel_id=1, source_target_pairs={{0,1},{1,0},{2,3},{3,2},{4,5},{5,4},{6,7},{7,6},{8,9},{9,8},{10,11... | collective-permute-start | bytes 356360 | tf_op jit(solution)/shard_map/ppermute | solution.py:429
  25.8 0.5 %collective-permute-start.6 = (s16[2,464,128]{2,1,0:T(8,128)(2,1)S(1)}, s16[2,464,128]{2,1,0:T(8,128)(2,1)S(1)}, u32[]{:S(2)}, u32[]{:S(2)}) collective-permute-start(s16[2,464,128]{2,1,0:T(8,128)(2,1)S(1)} %get-tuple-element.85), channel_id=1, source_target_pairs={{0,1},{1,0},{2,3},{3,2},{4,5},{5,4},{6,7},{7,6},{8,9},{9,8},{10,11... | collective-permute-start | bytes 712712 | tf_op jit(solution)/shard_map/ppermute | solution.py:429
  26.3 0.8 %collective-permute-done.9.near_ref = s16[1,480,128]{2,1,0:T(8,128)(2,1)S(1)} collective-permute-done((s16[1,480,128]{2,1,0:T(8,128)(2,1)S(1)}, s16[1,480,128]{2,1,0:T(8,128)(2,1)S(1)}, u32[]{:S(2)}, u32[]{:S(2)}) %collective-permute-start.9) | collective-permute-done | bytes 122912 | tf_op jit(solution)/shard_map/ppermute | solution.py:429
  27.3 3.1 %collective-permute-start.11 = (s16[1,496,128]{2,1,0:T(8,128)(2,1)S(1)}, s16[1,496,128]{2,1,0:T(8,128)(2,1)S(1)}, u32[]{:S(2)}, u32[]{:S(2)}) collective-permute-start(s16[1,496,128]{2,1,0:T(8,128)(2,1)S(1)} %get-tuple-element.90), channel_id=1, source_target_pairs={{0,4},{1,5},{2,6},{3,7},{4,0},{5,1},{6,2},{7,3},{8,12},{9,13},{10,... | collective-permute-start | bytes 380936 | tf_op jit(solution)/shard_map/ppermute | solution.py:429
  30.5 1.6 %collective-permute-start.10 = (s16[1,480,128]{2,1,0:T(8,128)(2,1)S(1)}, s16[1,480,128]{2,1,0:T(8,128)(2,1)S(1)}, u32[]{:S(2)}, u32[]{:S(2)}) collective-permute-start(s16[1,480,128]{2,1,0:T(8,128)(2,1)S(1)} %pass_sums.3), channel_id=1, source_target_pairs={{0,2},{1,3},{2,0},{3,1},{4,6},{5,7},{6,4},{7,5},{8,10},{9,11},{10,... | collective-permute-start | bytes 368648 | tf_op jit(solution)/shard_map/ppermute | solution.py:429
  32.2 0.5 %collective-permute-start.12 = (s16[1,464,128]{2,1,0:T(8,128)(2,1)S(1)}, s16[1,464,128]{2,1,0:T(8,128)(2,1)S(1)}, u32[]{:S(2)}, u32[]{:S(2)}) collective-permute-start(s16[1,464,128]{2,1,0:T(8,128)(2,1)S(1)} %get-tuple-element.94), channel_id=1, source_target_pairs={{0,2},{1,3},{2,0},{3,1},{4,6},{5,7},{6,4},{7,5},{8,10},{9,11},{10,... | collective-permute-start | bytes 356360 | tf_op jit(solution)/shard_map/ppermute | solution.py:429
  32.6 1.5 %collective-permute-start.5 = (s16[2,464,128]{2,1,0:T(8,128)(2,1)S(1)}, s16[2,464,128]{2,1,0:T(8,128)(2,1)S(1)}, u32[]{:S(2)}, u32[]{:S(2)}) collective-permute-start(s16[2,464,128]{2,1,0:T(8,128)(2,1)S(1)} %get-tuple-element.83), channel_id=1, source_target_pairs={{0,1},{1,0},{2,3},{3,2},{4,5},{5,4},{6,7},{7,6},{8,9},{9,8},{10,11... | collective-permute-start | bytes 712712 | tf_op jit(solution)/shard_map/ppermute | solution.py:429
  34.1 2.4 %collective-permute-done.10.near_ref = s16[1,480,128]{2,1,0:T(8,128)(2,1)S(1)} collective-permute-done((s16[1,480,128]{2,1,0:T(8,128)(2,1)S(1)}, s16[1,480,128]{2,1,0:T(8,128)(2,1)S(1)}, u32[]{:S(2)}, u32[]{:S(2)}) %collective-permute-start.10) | collective-permute-done | bytes 122912 | tf_op jit(solution)/shard_map/ppermute | solution.py:429
  36.7 2.2 %collective-permute-start.14 = (s16[1,480,128]{2,1,0:T(8,128)(2,1)S(1)}, s16[1,480,128]{2,1,0:T(8,128)(2,1)S(1)}, u32[]{:S(2)}, u32[]{:S(2)}) collective-permute-start(s16[1,480,128]{2,1,0:T(8,128)(2,1)S(1)} %get-tuple-element.96), channel_id=1, source_target_pairs={{0,4},{1,5},{2,6},{3,7},{4,0},{5,1},{6,2},{7,3},{8,12},{9,13},{10,... | collective-permute-start | bytes 368648 | tf_op jit(solution)/shard_map/ppermute | solution.py:429
  38.9 1.7 %collective-permute-start.13 = (s16[1,464,128]{2,1,0:T(8,128)(2,1)S(1)}, s16[1,464,128]{2,1,0:T(8,128)(2,1)S(1)}, u32[]{:S(2)}, u32[]{:S(2)}) collective-permute-start(s16[1,464,128]{2,1,0:T(8,128)(2,1)S(1)} %get-tuple-element.95), channel_id=1, source_target_pairs={{0,2},{1,3},{2,0},{3,1},{4,6},{5,7},{6,4},{7,5},{8,10},{9,11},{10,... | collective-permute-start | bytes 356360 | tf_op jit(solution)/shard_map/ppermute | solution.py:429
  40.6 0.8 %result_columns.2.refs_0_ = f32[448,256]{1,0:T(8,128)} custom-call(s16[2,464,128]{2,1,0:T(8,128)(2,1)S(1)} %collective-permute-done.5.side_ref, f32[1,448,128]{2,1,0:T(8,128)S(1)} %get-tuple-element.70.own, s16[1,464,128]{2,1,0:T(8,128)(2,1)S(1)} %collective-permute-done.12.near, s16[1,496,128]{2,1,0:T(8,128)(2,1)S(1)} %collective-permute-done.11.far), custom_call_target="tpu_custom_call" | custom-call | tf_op jit(solution)/shard_map/result_columns/pallas_call | solution.py:522
  41.4 2.3 %collective-permute-done.13.near = s16[1,464,128]{2,1,0:T(8,128)(2,1)S(1)} collective-permute-done((s16[1,464,128]{2,1,0:T(8,128)(2,1)S(1)}, s16[1,464,128]{2,1,0:T(8,128)(2,1)S(1)}, u32[]{:S(2)}, u32[]{:S(2)}) %collective-permute-start.13) | collective-permute-done | bytes 118816 | tf_op jit(solution)/shard_map/ppermute | solution.py:429
  43.9 0.8 %result_columns.3 = f32[448,256]{1,0:T(8,128)} custom-call(s16[2,464,128]{2,1,0:T(8,128)(2,1)S(1)} %collective-permute-done.5.side_ref, f32[1,448,128]{2,1,0:T(8,128)S(1)} %get-tuple-element.84.own, s16[1,464,128]{2,1,0:T(8,128)(2,1)S(1)} %collective-permute-done.13.near, ...), custom_call_target="tpu_custom_call", output_to_operand_aliasing={{}: (4, {})} | custom-call | tf_op jit(solution)/shard_map/result_columns/pallas_call | solution.py:522
  (21 shorter events, 1.4 us)
Async XLA Ops:
  0.0 5.5 %copy-start = (bf16[6,24,40,384]{3,2,1,0:T(8,128)(2,1)S(1)}, bf16[6,24,40,384]{3,2,1,0:T(8,128)(2,1)}, u32[]{:S(2)}) copy-start(bf16[6,24,40,384]{3,2,1,0:T(8,128)(2,1)} %param.3) | copy-start | bytes 13271044
  2.4 10.1 %collective-permute-start.1 = (s16[2,992,128]{2,1,0:T(8,128)(2,1)S(1)}, s16[2,992,128]{2,1,0:T(8,128)(2,1)S(1)}, u32[]{:S(2)}, u32[]{:S(2)}) collective-permute-start(s16[2,992,128]{2,1,0:T(8,128)(2,1)S(1)} %get-tuple-element.62), channel_id=1, source_target_pairs={{0,2},{1,3},{2,0},{3,1},{4,6},{5,7},{6,4},{7,5},{8,16},{9,17},{10,... | collective-permute-start | bytes 1523720 | tf_op jit(solution)/shard_map/ppermute | solution.py:445
  6.2 2.7 %collective-permute-start = (s16[2,976,128]{2,1,0:T(8,128)(2,1)S(1)}, s16[2,976,128]{2,1,0:T(8,128)(2,1)S(1)}, u32[]{:S(2)}, u32[]{:S(2)}) collective-permute-start(s16[2,976,128]{2,1,0:T(8,128)(2,1)S(1)} %get-tuple-element.58), channel_id=1, source_target_pairs={{0,8},{8,0},{16,24},{24,16},{1,9},{9,1},{17,25},{25,17},{2,10},{10... | collective-permute-start | bytes 1499144 | tf_op jit(solution)/shard_map/ppermute | solution.py:444
  7.3 12.7 %collective-permute-start.4 = (s16[2,992,128]{2,1,0:T(8,128)(2,1)S(1)}, s16[2,992,128]{2,1,0:T(8,128)(2,1)S(1)}, u32[]{:S(2)}, u32[]{:S(2)}) collective-permute-start(s16[2,992,128]{2,1,0:T(8,128)(2,1)S(1)} %get-tuple-element.74), channel_id=1, source_target_pairs={{0,2},{1,3},{2,0},{3,1},{4,6},{5,7},{6,4},{7,5},{8,16},{9,17},{10,... | collective-permute-start | bytes 1523720 | tf_op jit(solution)/shard_map/ppermute | solution.py:445
  9.0 7.7 %collective-permute-start.3 = (s16[2,976,128]{2,1,0:T(8,128)(2,1)S(1)}, s16[2,976,128]{2,1,0:T(8,128)(2,1)S(1)}, u32[]{:S(2)}, u32[]{:S(2)}) collective-permute-start(s16[2,976,128]{2,1,0:T(8,128)(2,1)S(1)} %get-tuple-element.72), channel_id=1, source_target_pairs={{0,8},{8,0},{16,24},{24,16},{1,9},{9,1},{17,25},{25,17},{2,10},{10... | collective-permute-start | bytes 1499144 | tf_op jit(solution)/shard_map/ppermute | solution.py:444
  14.6 7.5 %collective-permute-start.2 = (s16[1,464,128]{2,1,0:T(8,128)(2,1)S(1)}, s16[1,464,128]{2,1,0:T(8,128)(2,1)S(1)}, u32[]{:S(2)}, u32[]{:S(2)}) collective-permute-start(s16[1,464,128]{2,1,0:T(8,128)(2,1)S(1)} %get-tuple-element.64), channel_id=1, source_target_pairs={{0,1},{1,0},{2,3},{3,2},{4,5},{5,4},{6,7},{7,6},{8,9},{9,8},{10,11... | collective-permute-start | bytes 356360 | tf_op jit(solution)/shard_map/ppermute | solution.py:429
  16.6 9.7 %collective-permute-start.8 = (s16[2,464,128]{2,1,0:T(8,128)(2,1)S(1)}, s16[2,464,128]{2,1,0:T(8,128)(2,1)S(1)}, u32[]{:S(2)}, u32[]{:S(2)}) collective-permute-start(s16[2,464,128]{2,1,0:T(8,128)(2,1)S(1)} %get-tuple-element.67), channel_id=1, source_target_pairs={{0,1},{1,0},{2,3},{3,2},{4,5},{5,4},{6,7},{7,6},{8,9},{9,8},{10,11... | collective-permute-start | bytes 712712 | tf_op jit(solution)/shard_map/ppermute | solution.py:429
  22.2 4.9 %collective-permute-start.9 = (s16[1,480,128]{2,1,0:T(8,128)(2,1)S(1)}, s16[1,480,128]{2,1,0:T(8,128)(2,1)S(1)}, u32[]{:S(2)}, u32[]{:S(2)}) collective-permute-start(s16[1,480,128]{2,1,0:T(8,128)(2,1)S(1)} %pass_sums.2), channel_id=1, source_target_pairs={{0,2},{1,3},{2,0},{3,1},{4,6},{5,7},{6,4},{7,5},{8,10},{9,11},{10,... | collective-permute-start | bytes 368648 | tf_op jit(solution)/shard_map/ppermute | solution.py:429
  24.3 6.2 %collective-permute-start.7 = (s16[1,464,128]{2,1,0:T(8,128)(2,1)S(1)}, s16[1,464,128]{2,1,0:T(8,128)(2,1)S(1)}, u32[]{:S(2)}, u32[]{:S(2)}) collective-permute-start(s16[1,464,128]{2,1,0:T(8,128)(2,1)S(1)} %get-tuple-element.87), channel_id=1, source_target_pairs={{0,1},{1,0},{2,3},{3,2},{4,5},{5,4},{6,7},{7,6},{8,9},{9,8},{10,11... | collective-permute-start | bytes 356360 | tf_op jit(solution)/shard_map/ppermute | solution.py:429
  25.8 10.7 %collective-permute-start.6 = (s16[2,464,128]{2,1,0:T(8,128)(2,1)S(1)}, s16[2,464,128]{2,1,0:T(8,128)(2,1)S(1)}, u32[]{:S(2)}, u32[]{:S(2)}) collective-permute-start(s16[2,464,128]{2,1,0:T(8,128)(2,1)S(1)} %get-tuple-element.85), channel_id=1, source_target_pairs={{0,1},{1,0},{2,3},{3,2},{4,5},{5,4},{6,7},{7,6},{8,9},{9,8},{10,11... | collective-permute-start | bytes 712712 | tf_op jit(solution)/shard_map/ppermute | solution.py:429
  27.3 9.2 %collective-permute-start.11 = (s16[1,496,128]{2,1,0:T(8,128)(2,1)S(1)}, s16[1,496,128]{2,1,0:T(8,128)(2,1)S(1)}, u32[]{:S(2)}, u32[]{:S(2)}) collective-permute-start(s16[1,496,128]{2,1,0:T(8,128)(2,1)S(1)} %get-tuple-element.90), channel_id=1, source_target_pairs={{0,4},{1,5},{2,6},{3,7},{4,0},{5,1},{6,2},{7,3},{8,12},{9,13},{10,... | collective-permute-start | bytes 380936 | tf_op jit(solution)/shard_map/ppermute | solution.py:429
  30.5 6.0 %collective-permute-start.10 = (s16[1,480,128]{2,1,0:T(8,128)(2,1)S(1)}, s16[1,480,128]{2,1,0:T(8,128)(2,1)S(1)}, u32[]{:S(2)}, u32[]{:S(2)}) collective-permute-start(s16[1,480,128]{2,1,0:T(8,128)(2,1)S(1)} %pass_sums.3), channel_id=1, source_target_pairs={{0,2},{1,3},{2,0},{3,1},{4,6},{5,7},{6,4},{7,5},{8,10},{9,11},{10,... | collective-permute-start | bytes 368648 | tf_op jit(solution)/shard_map/ppermute | solution.py:429
  32.2 6.7 %collective-permute-start.12 = (s16[1,464,128]{2,1,0:T(8,128)(2,1)S(1)}, s16[1,464,128]{2,1,0:T(8,128)(2,1)S(1)}, u32[]{:S(2)}, u32[]{:S(2)}) collective-permute-start(s16[1,464,128]{2,1,0:T(8,128)(2,1)S(1)} %get-tuple-element.94), channel_id=1, source_target_pairs={{0,2},{1,3},{2,0},{3,1},{4,6},{5,7},{6,4},{7,5},{8,10},{9,11},{10,... | collective-permute-start | bytes 356360 | tf_op jit(solution)/shard_map/ppermute | solution.py:429
  32.6 8.0 %collective-permute-start.5 = (s16[2,464,128]{2,1,0:T(8,128)(2,1)S(1)}, s16[2,464,128]{2,1,0:T(8,128)(2,1)S(1)}, u32[]{:S(2)}, u32[]{:S(2)}) collective-permute-start(s16[2,464,128]{2,1,0:T(8,128)(2,1)S(1)} %get-tuple-element.83), channel_id=1, source_target_pairs={{0,1},{1,0},{2,3},{3,2},{4,5},{5,4},{6,7},{7,6},{8,9},{9,8},{10,11... | collective-permute-start | bytes 712712 | tf_op jit(solution)/shard_map/ppermute | solution.py:429
  36.7 7.2 %collective-permute-start.14 = (s16[1,480,128]{2,1,0:T(8,128)(2,1)S(1)}, s16[1,480,128]{2,1,0:T(8,128)(2,1)S(1)}, u32[]{:S(2)}, u32[]{:S(2)}) collective-permute-start(s16[1,480,128]{2,1,0:T(8,128)(2,1)S(1)} %get-tuple-element.96), channel_id=1, source_target_pairs={{0,4},{1,5},{2,6},{3,7},{4,0},{5,1},{6,2},{7,3},{8,12},{9,13},{10,... | collective-permute-start | bytes 368648 | tf_op jit(solution)/shard_map/ppermute | solution.py:429
  38.9 4.8 %collective-permute-start.13 = (s16[1,464,128]{2,1,0:T(8,128)(2,1)S(1)}, s16[1,464,128]{2,1,0:T(8,128)(2,1)S(1)}, u32[]{:S(2)}, u32[]{:S(2)}) collective-permute-start(s16[1,464,128]{2,1,0:T(8,128)(2,1)S(1)} %get-tuple-element.95), channel_id=1, source_target_pairs={{0,2},{1,3},{2,0},{3,1},{4,6},{5,7},{6,4},{7,5},{8,10},{9,11},{10,... | collective-permute-start | bytes 356360 | tf_op jit(solution)/shard_map/ppermute | solution.py:429

commit v9 on v8

--- a/solution.py
+++ b/solution.py
@@ -306,17 +306,14 @@
 
 def column_kernel(scale, share, chunk, side_ref, own, near, far, *refs):
     out_hbm, buf, sem = refs[-3:]
-    half = share // 2
-    parts = [unpack_block(ref, share) for ref in (side_ref.at[chunk], near.at[0], far.at[0])]
-    copies = []
-    for k in range(2):
-        rows = slice(k * half, (k + 1) * half)
-        buf[rows, :] = (own[0, rows, :] + sum(part[rows] for part in parts)) * scale
-        place = out_hbm.at[pl.ds(k * half, half), pl.ds(chunk * LANES, LANES)]
-        copies.append(pltpu.make_async_copy(buf.at[pl.ds(k * half, half), :], place, sem.at[k]))
-        copies[-1].start()
-    for copy in copies:
-        copy.wait()
+    value = own[0]
+    for ref in (side_ref.at[chunk], near.at[0], far.at[0]):
+        value = value + unpack_block(ref, share)
+    buf[...] = value * scale
+    place = out_hbm.at[:, pl.ds(chunk * LANES, LANES)]
+    copy = pltpu.make_async_copy(buf, place, sem.at[0])
+    copy.start()
+    copy.wait()
 
 
 def shards(volume, sketch_matrix, brain_voxels):
@@ -527,7 +524,7 @@
                     input_output_aliases={len(args): 0} if outs else {},
                     scratch_shapes=[
                         pltpu.VMEM((share, LANES), F32),
-                        pltpu.SemaphoreType.DMA((2,)),
+                        pltpu.SemaphoreType.DMA((1,)),
                     ],
                     compiler_params=VMEM,
                     cost_estimate=COST,

time: 45 us -> 45 us (level)
  no operation moved by 1% of the time
where the time goes in v9:
time: 45 us; the launch traced here: 44.9 us
  starting transfers between devices  21.7 us (48%)
  Pallas kernels  16.8 us (37%)
  waiting for transfers between devices  6.07 us (13%)
    ppermute x11, starting transfers between devices, across(): return lax.ppermute(value, 'ta', [(i, i ^ mask) for i in range(n_ta)])  16.8 us
    pallas_call x2, Pallas kernels, shards(): pl.pallas_call(functools.partial(inner_rows_kernel, ratios, (width_x, wid...  6.4 us
    ppermute x11, waiting for transfers between devices, across(): return lax.ppermute(value, 'ta', [(i, i ^ mask) for i in range(n_ta)])  5.68 us
    ppermute x2, starting transfers between devices, shards(): far = lax.ppermute(messages[2 * c], ('gz', 'ta'), odd_pairs)  4.73 us
    pallas_call x2, Pallas kernels, shards(): pl.pallas_call(functools.partial(outer_kernel, ratios, (width_x, width_y)...  4.21 us
    pallas_call x1, Pallas kernels, shards(): pl.pallas_call(functools.partial(far_kernel, planes, cells, chunks, packs...  2.37 us
    pallas_call x2, Pallas kernels, more_products(): pl.pallas_call(functools.partial(kernel, planes, cells, chunks, packs_of)...  1.7 us
    pallas_call x2, Pallas kernels, shards(): pl.pallas_call(functools.partial(column_kernel, taps[2] ** 3, share, c),...  1.61 us
  transfers between devices with their start and end apart: 15, of which 5 were waited for; matrix products, arithmetic and copies ran while one was open for 0% of the time, Pallas kernels for 30%

profile of v9, /device:TPU:0, one launch (start us, length us, event | category | flops | bytes accessed | tf_op | source)
XLA Modules:
  0.0 44.9 jit_solution(7319996885294870847)
XLA Ops:
  0.0 2.4 %far_products.1 = (s16[2,992,128]{2,1,0:T(8,128)(2,1)S(1)}, s32[24]{0:T(128)S(1)}, s32[3832,128]{1,0:T(8,128)S(1)}, bf16[384,256]{1,0:T(8,128)(2,1)S(1)}, f32[10...) custom-call(bf16[5760,384]{1,0:T(8,128)(2,1)} %bitcast.2, bf16[384,256]{1,0:T(8,128)(2,1)} %w_hbm.1, s32[28,128]{1,0:T(8,128)} %bitcast.5), custom_call_target="tpu_custom_call" | custom-call | tf_op jit(solution)/shard_map/far_products/pallas_call | solution.py:363
  2.4 3.1 %collective-permute-start.1 = (s16[2,992,128]{2,1,0:T(8,128)(2,1)S(1)}, s16[2,992,128]{2,1,0:T(8,128)(2,1)S(1)}, u32[]{:S(2)}, u32[]{:S(2)}) collective-permute-start(s16[2,992,128]{2,1,0:T(8,128)(2,1)S(1)} %get-tuple-element.62), channel_id=1, source_target_pairs={{0,2},{1,3},{2,0},{3,1},{4,6},{5,7},{6,4},{7,5},{8,16},{9,17},{10,... | collective-permute-start | bytes 1523720 | tf_op jit(solution)/shard_map/ppermute | solution.py:442
  5.5 0.7 %near_products.1 = (s16[2,976,128]{2,1,0:T(8,128)(2,1)S(1)}, f32[10,960,128]{2,1,0:T(8,128)S(1)}, f32[10,960,128]{2,1,0:T(8,128)S(1)}) custom-call(bf16[5760,384]{1,0:T(8,128)(2,1)S(1)} %bitcast.3, bf16[384,256]{1,0:T(8,128)(2,1)S(1)} %get-tuple-element.52.w_ref, ...), custom_call_target="tpu_custom_call", output_to_operand_aliasing={{1}: (2, {}), {2}: (3, {})} | custom-call | tf_op jit(solution)/shard_map/near_products/pallas_call | solution.py:381
  6.3 1.0 %middle_products.1 = (s16[2,992,128]{2,1,0:T(8,128)(2,1)S(1)}, s16[2,976,128]{2,1,0:T(8,128)(2,1)S(1)}, f32[10,960,128]{2,1,0:T(8,128)S(1)}, f32[10,960,128]{2,1,0:T(8,128)S(1)}) custom-call(bf16[5760,384]{1,0:T(8,128)(2,1)S(1)} %bitcast.4, bf16[384,256]{1,0:T(8,128)(2,1)S(1)} %get-tuple-element.52.w_ref, ...), custom_call_target="tpu_custom_call", output_to_operand_aliasing={{2}: (2, {}), {3}: (3, {})} | custom-call | tf_op jit(solution)/shard_map/middle_products/pallas_call | solution.py:381
  7.3 1.6 %collective-permute-start.4 = (s16[2,992,128]{2,1,0:T(8,128)(2,1)S(1)}, s16[2,992,128]{2,1,0:T(8,128)(2,1)S(1)}, u32[]{:S(2)}, u32[]{:S(2)}) collective-permute-start(s16[2,992,128]{2,1,0:T(8,128)(2,1)S(1)} %get-tuple-element.74), channel_id=1, source_target_pairs={{0,2},{1,3},{2,0},{3,1},{4,6},{5,7},{6,4},{7,5},{8,16},{9,17},{10,... | collective-permute-start | bytes 1523720 | tf_op jit(solution)/shard_map/ppermute | solution.py:442
  9.0 3.1 %inner_rows.2 = (f32[10,960,128]{2,1,0:T(8,128)S(1)}, f32[3832,128]{1,0:T(8,128)S(1)}) custom-call(f32[10,960,128]{2,1,0:T(8,128)S(1)} %get-tuple-element.57._, s16[2,976,128]{2,1,0:T(8,128)(2,1)S(1)} %collective-permute-done.near_ref, s32[3832,128]{1,0:T(8,128)S(1)} %get-tuple-element.59.bv_ref.refs_3_, ...), custom_call_target="tpu_custom_call", output_to_operand_aliasing={{0}: (0, {})} | custom-call | tf_op jit(solution)/shard_map/inner_rows/pallas_call | solution.py:446
  12.5 2.1 %outer_rows.2 = (f32[10,960,128]{2,1,0:T(8,128)S(1)}, f32[3832,128]{1,0:T(8,128)S(1)}, s16[1,464,128]{2,1,0:T(8,128)(2,1)S(1)}, s16[2,464,128]{2,1,0:T(8,128)(2,...) custom-call(f32[10,960,128]{2,1,0:T(8,128)S(1)} %get-tuple-element.6, ...), custom_call_target="tpu_custom_call", output_to_operand_aliasing={{0}: (0, {}), {1}: (2, {})} | custom-call | tf_op jit(solution)/shard_map/outer_rows/pallas_call | solution.py:464
  14.6 2.0 %collective-permute-start.2 = (s16[1,464,128]{2,1,0:T(8,128)(2,1)S(1)}, s16[1,464,128]{2,1,0:T(8,128)(2,1)S(1)}, u32[]{:S(2)}, u32[]{:S(2)}) collective-permute-start(s16[1,464,128]{2,1,0:T(8,128)(2,1)S(1)} %get-tuple-element.64), channel_id=1, source_target_pairs={{0,1},{1,0},{2,3},{3,2},{4,5},{5,4},{6,7},{7,6},{8,9},{9,8},{10,11... | collective-permute-start | bytes 356360 | tf_op jit(solution)/shard_map/ppermute | solution.py:426
  16.7 3.3 %inner_rows.3 = (f32[10,960,128]{2,1,0:T(8,128)S(1)}, f32[3832,128]{1,0:T(8,128)S(1)}) custom-call(f32[10,960,128]{2,1,0:T(8,128)S(1)} %get-tuple-element.71._, s16[2,976,128]{2,1,0:T(8,128)(2,1)S(1)} %collective-permute-done.3.near_ref, s32[3832,128]{1,0:T(8,128)S(1)} %get-tuple-element.59.bv_ref.refs_3_, ...), custom_call_target="tpu_custom_call", output_to_operand_aliasing={{0}: (0, {})} | custom-call | tf_op jit(solution)/shard_map/inner_rows/pallas_call | solution.py:446
  20.0 2.1 %outer_rows.3 = (f32[10,960,128]{2,1,0:T(8,128)S(1)}, f32[3832,128]{1,0:T(8,128)S(1)}, s16[1,464,128]{2,1,0:T(8,128)(2,1)S(1)}, s16[2,464,128]{2,1,0:T(8,128)(2,...) custom-call(f32[10,960,128]{2,1,0:T(8,128)S(1)} %get-tuple-element.7, ...), custom_call_target="tpu_custom_call", output_to_operand_aliasing={{0}: (0, {}), {1}: (2, {})} | custom-call | tf_op jit(solution)/shard_map/outer_rows/pallas_call | solution.py:464
  22.2 2.1 %collective-permute-start.9 = (s16[1,480,128]{2,1,0:T(8,128)(2,1)S(1)}, s16[1,480,128]{2,1,0:T(8,128)(2,1)S(1)}, u32[]{:S(2)}, u32[]{:S(2)}) collective-permute-start(s16[1,480,128]{2,1,0:T(8,128)(2,1)S(1)} %pass_sums.2), channel_id=1, source_target_pairs={{0,2},{1,3},{2,0},{3,1},{4,6},{5,7},{6,4},{7,5},{8,10},{9,11},{10,... | collective-permute-start | bytes 368648 | tf_op jit(solution)/shard_map/ppermute | solution.py:426
  24.3 1.5 %collective-permute-start.7 = (s16[1,464,128]{2,1,0:T(8,128)(2,1)S(1)}, s16[1,464,128]{2,1,0:T(8,128)(2,1)S(1)}, u32[]{:S(2)}, u32[]{:S(2)}) collective-permute-start(s16[1,464,128]{2,1,0:T(8,128)(2,1)S(1)} %get-tuple-element.87), channel_id=1, source_target_pairs={{0,1},{1,0},{2,3},{3,2},{4,5},{5,4},{6,7},{7,6},{8,9},{9,8},{10,11... | collective-permute-start | bytes 356360 | tf_op jit(solution)/shard_map/ppermute | solution.py:426
  25.8 0.5 %collective-permute-start.6 = (s16[2,464,128]{2,1,0:T(8,128)(2,1)S(1)}, s16[2,464,128]{2,1,0:T(8,128)(2,1)S(1)}, u32[]{:S(2)}, u32[]{:S(2)}) collective-permute-start(s16[2,464,128]{2,1,0:T(8,128)(2,1)S(1)} %get-tuple-element.85), channel_id=1, source_target_pairs={{0,1},{1,0},{2,3},{3,2},{4,5},{5,4},{6,7},{7,6},{8,9},{9,8},{10,11... | collective-permute-start | bytes 712712 | tf_op jit(solution)/shard_map/ppermute | solution.py:426
  26.3 0.8 %collective-permute-done.9.near_ref = s16[1,480,128]{2,1,0:T(8,128)(2,1)S(1)} collective-permute-done((s16[1,480,128]{2,1,0:T(8,128)(2,1)S(1)}, s16[1,480,128]{2,1,0:T(8,128)(2,1)S(1)}, u32[]{:S(2)}, u32[]{:S(2)}) %collective-permute-start.9) | collective-permute-done | bytes 122912 | tf_op jit(solution)/shard_map/ppermute | solution.py:426
  27.3 3.1 %collective-permute-start.11 = (s16[1,496,128]{2,1,0:T(8,128)(2,1)S(1)}, s16[1,496,128]{2,1,0:T(8,128)(2,1)S(1)}, u32[]{:S(2)}, u32[]{:S(2)}) collective-permute-start(s16[1,496,128]{2,1,0:T(8,128)(2,1)S(1)} %get-tuple-element.90), channel_id=1, source_target_pairs={{0,4},{1,5},{2,6},{3,7},{4,0},{5,1},{6,2},{7,3},{8,12},{9,13},{10,... | collective-permute-start | bytes 380936 | tf_op jit(solution)/shard_map/ppermute | solution.py:426
  30.5 1.6 %collective-permute-start.10 = (s16[1,480,128]{2,1,0:T(8,128)(2,1)S(1)}, s16[1,480,128]{2,1,0:T(8,128)(2,1)S(1)}, u32[]{:S(2)}, u32[]{:S(2)}) collective-permute-start(s16[1,480,128]{2,1,0:T(8,128)(2,1)S(1)} %pass_sums.3), channel_id=1, source_target_pairs={{0,2},{1,3},{2,0},{3,1},{4,6},{5,7},{6,4},{7,5},{8,10},{9,11},{10,... | collective-permute-start | bytes 368648 | tf_op jit(solution)/shard_map/ppermute | solution.py:426
  32.2 0.5 %collective-permute-start.12 = (s16[1,464,128]{2,1,0:T(8,128)(2,1)S(1)}, s16[1,464,128]{2,1,0:T(8,128)(2,1)S(1)}, u32[]{:S(2)}, u32[]{:S(2)}) collective-permute-start(s16[1,464,128]{2,1,0:T(8,128)(2,1)S(1)} %get-tuple-element.94), channel_id=1, source_target_pairs={{0,2},{1,3},{2,0},{3,1},{4,6},{5,7},{6,4},{7,5},{8,10},{9,11},{10,... | collective-permute-start | bytes 356360 | tf_op jit(solution)/shard_map/ppermute | solution.py:426
  32.6 1.5 %collective-permute-start.5 = (s16[2,464,128]{2,1,0:T(8,128)(2,1)S(1)}, s16[2,464,128]{2,1,0:T(8,128)(2,1)S(1)}, u32[]{:S(2)}, u32[]{:S(2)}) collective-permute-start(s16[2,464,128]{2,1,0:T(8,128)(2,1)S(1)} %get-tuple-element.83), channel_id=1, source_target_pairs={{0,1},{1,0},{2,3},{3,2},{4,5},{5,4},{6,7},{7,6},{8,9},{9,8},{10,11... | collective-permute-start | bytes 712712 | tf_op jit(solution)/shard_map/ppermute | solution.py:426
  34.1 2.3 %collective-permute-done.10.near_ref = s16[1,480,128]{2,1,0:T(8,128)(2,1)S(1)} collective-permute-done((s16[1,480,128]{2,1,0:T(8,128)(2,1)S(1)}, s16[1,480,128]{2,1,0:T(8,128)(2,1)S(1)}, u32[]{:S(2)}, u32[]{:S(2)}) %collective-permute-start.10) | collective-permute-done | bytes 122912 | tf_op jit(solution)/shard_map/ppermute | solution.py:426
  36.7 2.2 %collective-permute-start.14 = (s16[1,480,128]{2,1,0:T(8,128)(2,1)S(1)}, s16[1,480,128]{2,1,0:T(8,128)(2,1)S(1)}, u32[]{:S(2)}, u32[]{:S(2)}) collective-permute-start(s16[1,480,128]{2,1,0:T(8,128)(2,1)S(1)} %get-tuple-element.96), channel_id=1, source_target_pairs={{0,4},{1,5},{2,6},{3,7},{4,0},{5,1},{6,2},{7,3},{8,12},{9,13},{10,... | collective-permute-start | bytes 368648 | tf_op jit(solution)/shard_map/ppermute | solution.py:426
  38.9 1.7 %collective-permute-start.13 = (s16[1,464,128]{2,1,0:T(8,128)(2,1)S(1)}, s16[1,464,128]{2,1,0:T(8,128)(2,1)S(1)}, u32[]{:S(2)}, u32[]{:S(2)}) collective-permute-start(s16[1,464,128]{2,1,0:T(8,128)(2,1)S(1)} %get-tuple-element.95), channel_id=1, source_target_pairs={{0,2},{1,3},{2,0},{3,1},{4,6},{5,7},{6,4},{7,5},{8,10},{9,11},{10,... | collective-permute-start | bytes 356360 | tf_op jit(solution)/shard_map/ppermute | solution.py:426
  40.6 0.8 %result_columns.2.refs_0_ = f32[448,256]{1,0:T(8,128)} custom-call(s16[2,464,128]{2,1,0:T(8,128)(2,1)S(1)} %collective-permute-done.5.side_ref, f32[1,448,128]{2,1,0:T(8,128)S(1)} %get-tuple-element.70.own, s16[1,464,128]{2,1,0:T(8,128)(2,1)S(1)} %collective-permute-done.12.near, s16[1,496,128]{2,1,0:T(8,128)(2,1)S(1)} %collective-permute-done.11.far), custom_call_target="tpu_custom_call" | custom-call | tf_op jit(solution)/shard_map/result_columns/pallas_call | solution.py:519
  41.4 2.3 %collective-permute-done.13.near = s16[1,464,128]{2,1,0:T(8,128)(2,1)S(1)} collective-permute-done((s16[1,464,128]{2,1,0:T(8,128)(2,1)S(1)}, s16[1,464,128]{2,1,0:T(8,128)(2,1)S(1)}, u32[]{:S(2)}, u32[]{:S(2)}) %collective-permute-start.13) | collective-permute-done | bytes 118816 | tf_op jit(solution)/shard_map/ppermute | solution.py:426
  43.9 0.8 %result_columns.3 = f32[448,256]{1,0:T(8,128)} custom-call(s16[2,464,128]{2,1,0:T(8,128)(2,1)S(1)} %collective-permute-done.5.side_ref, f32[1,448,128]{2,1,0:T(8,128)S(1)} %get-tuple-element.84.own, s16[1,464,128]{2,1,0:T(8,128)(2,1)S(1)} %collective-permute-done.13.near, ...), custom_call_target="tpu_custom_call", output_to_operand_aliasing={{}: (4, {})} | custom-call | tf_op jit(solution)/shard_map/result_columns/pallas_call | solution.py:519
  (21 shorter events, 1.4 us)
Async XLA Ops:
  0.0 5.5 %copy-start = (bf16[6,24,40,384]{3,2,1,0:T(8,128)(2,1)S(1)}, bf16[6,24,40,384]{3,2,1,0:T(8,128)(2,1)}, u32[]{:S(2)}) copy-start(bf16[6,24,40,384]{3,2,1,0:T(8,128)(2,1)} %param.3) | copy-start | bytes 13271044
  2.4 10.1 %collective-permute-start.1 = (s16[2,992,128]{2,1,0:T(8,128)(2,1)S(1)}, s16[2,992,128]{2,1,0:T(8,128)(2,1)S(1)}, u32[]{:S(2)}, u32[]{:S(2)}) collective-permute-start(s16[2,992,128]{2,1,0:T(8,128)(2,1)S(1)} %get-tuple-element.62), channel_id=1, source_target_pairs={{0,2},{1,3},{2,0},{3,1},{4,6},{5,7},{6,4},{7,5},{8,16},{9,17},{10,... | collective-permute-start | bytes 1523720 | tf_op jit(solution)/shard_map/ppermute | solution.py:442
  6.2 2.7 %collective-permute-start = (s16[2,976,128]{2,1,0:T(8,128)(2,1)S(1)}, s16[2,976,128]{2,1,0:T(8,128)(2,1)S(1)}, u32[]{:S(2)}, u32[]{:S(2)}) collective-permute-start(s16[2,976,128]{2,1,0:T(8,128)(2,1)S(1)} %get-tuple-element.58), channel_id=1, source_target_pairs={{0,8},{8,0},{16,24},{24,16},{1,9},{9,1},{17,25},{25,17},{2,10},{10... | collective-permute-start | bytes 1499144 | tf_op jit(solution)/shard_map/ppermute | solution.py:441
  7.3 12.7 %collective-permute-start.4 = (s16[2,992,128]{2,1,0:T(8,128)(2,1)S(1)}, s16[2,992,128]{2,1,0:T(8,128)(2,1)S(1)}, u32[]{:S(2)}, u32[]{:S(2)}) collective-permute-start(s16[2,992,128]{2,1,0:T(8,128)(2,1)S(1)} %get-tuple-element.74), channel_id=1, source_target_pairs={{0,2},{1,3},{2,0},{3,1},{4,6},{5,7},{6,4},{7,5},{8,16},{9,17},{10,... | collective-permute-start | bytes 1523720 | tf_op jit(solution)/shard_map/ppermute | solution.py:442
  9.0 7.7 %collective-permute-start.3 = (s16[2,976,128]{2,1,0:T(8,128)(2,1)S(1)}, s16[2,976,128]{2,1,0:T(8,128)(2,1)S(1)}, u32[]{:S(2)}, u32[]{:S(2)}) collective-permute-start(s16[2,976,128]{2,1,0:T(8,128)(2,1)S(1)} %get-tuple-element.72), channel_id=1, source_target_pairs={{0,8},{8,0},{16,24},{24,16},{1,9},{9,1},{17,25},{25,17},{2,10},{10... | collective-permute-start | bytes 1499144 | tf_op jit(solution)/shard_map/ppermute | solution.py:441
  14.6 7.5 %collective-permute-start.2 = (s16[1,464,128]{2,1,0:T(8,128)(2,1)S(1)}, s16[1,464,128]{2,1,0:T(8,128)(2,1)S(1)}, u32[]{:S(2)}, u32[]{:S(2)}) collective-permute-start(s16[1,464,128]{2,1,0:T(8,128)(2,1)S(1)} %get-tuple-element.64), channel_id=1, source_target_pairs={{0,1},{1,0},{2,3},{3,2},{4,5},{5,4},{6,7},{7,6},{8,9},{9,8},{10,11... | collective-permute-start | bytes 356360 | tf_op jit(solution)/shard_map/ppermute | solution.py:426
  16.6 9.7 %collective-permute-start.8 = (s16[2,464,128]{2,1,0:T(8,128)(2,1)S(1)}, s16[2,464,128]{2,1,0:T(8,128)(2,1)S(1)}, u32[]{:S(2)}, u32[]{:S(2)}) collective-permute-start(s16[2,464,128]{2,1,0:T(8,128)(2,1)S(1)} %get-tuple-element.67), channel_id=1, source_target_pairs={{0,1},{1,0},{2,3},{3,2},{4,5},{5,4},{6,7},{7,6},{8,9},{9,8},{10,11... | collective-permute-start | bytes 712712 | tf_op jit(solution)/shard_map/ppermute | solution.py:426
  22.2 4.9 %collective-permute-start.9 = (s16[1,480,128]{2,1,0:T(8,128)(2,1)S(1)}, s16[1,480,128]{2,1,0:T(8,128)(2,1)S(1)}, u32[]{:S(2)}, u32[]{:S(2)}) collective-permute-start(s16[1,480,128]{2,1,0:T(8,128)(2,1)S(1)} %pass_sums.2), channel_id=1, source_target_pairs={{0,2},{1,3},{2,0},{3,1},{4,6},{5,7},{6,4},{7,5},{8,10},{9,11},{10,... | collective-permute-start | bytes 368648 | tf_op jit(solution)/shard_map/ppermute | solution.py:426
  24.3 6.2 %collective-permute-start.7 = (s16[1,464,128]{2,1,0:T(8,128)(2,1)S(1)}, s16[1,464,128]{2,1,0:T(8,128)(2,1)S(1)}, u32[]{:S(2)}, u32[]{:S(2)}) collective-permute-start(s16[1,464,128]{2,1,0:T(8,128)(2,1)S(1)} %get-tuple-element.87), channel_id=1, source_target_pairs={{0,1},{1,0},{2,3},{3,2},{4,5},{5,4},{6,7},{7,6},{8,9},{9,8},{10,11... | collective-permute-start | bytes 356360 | tf_op jit(solution)/shard_map/ppermute | solution.py:426
  25.8 10.7 %collective-permute-start.6 = (s16[2,464,128]{2,1,0:T(8,128)(2,1)S(1)}, s16[2,464,128]{2,1,0:T(8,128)(2,1)S(1)}, u32[]{:S(2)}, u32[]{:S(2)}) collective-permute-start(s16[2,464,128]{2,1,0:T(8,128)(2,1)S(1)} %get-tuple-element.85), channel_id=1, source_target_pairs={{0,1},{1,0},{2,3},{3,2},{4,5},{5,4},{6,7},{7,6},{8,9},{9,8},{10,11... | collective-permute-start | bytes 712712 | tf_op jit(solution)/shard_map/ppermute | solution.py:426
  27.3 9.2 %collective-permute-start.11 = (s16[1,496,128]{2,1,0:T(8,128)(2,1)S(1)}, s16[1,496,128]{2,1,0:T(8,128)(2,1)S(1)}, u32[]{:S(2)}, u32[]{:S(2)}) collective-permute-start(s16[1,496,128]{2,1,0:T(8,128)(2,1)S(1)} %get-tuple-element.90), channel_id=1, source_target_pairs={{0,4},{1,5},{2,6},{3,7},{4,0},{5,1},{6,2},{7,3},{8,12},{9,13},{10,... | collective-permute-start | bytes 380936 | tf_op jit(solution)/shard_map/ppermute | solution.py:426
  30.5 5.9 %collective-permute-start.10 = (s16[1,480,128]{2,1,0:T(8,128)(2,1)S(1)}, s16[1,480,128]{2,1,0:T(8,128)(2,1)S(1)}, u32[]{:S(2)}, u32[]{:S(2)}) collective-permute-start(s16[1,480,128]{2,1,0:T(8,128)(2,1)S(1)} %pass_sums.3), channel_id=1, source_target_pairs={{0,2},{1,3},{2,0},{3,1},{4,6},{5,7},{6,4},{7,5},{8,10},{9,11},{10,... | collective-permute-start | bytes 368648 | tf_op jit(solution)/shard_map/ppermute | solution.py:426
  32.2 6.7 %collective-permute-start.12 = (s16[1,464,128]{2,1,0:T(8,128)(2,1)S(1)}, s16[1,464,128]{2,1,0:T(8,128)(2,1)S(1)}, u32[]{:S(2)}, u32[]{:S(2)}) collective-permute-start(s16[1,464,128]{2,1,0:T(8,128)(2,1)S(1)} %get-tuple-element.94), channel_id=1, source_target_pairs={{0,2},{1,3},{2,0},{3,1},{4,6},{5,7},{6,4},{7,5},{8,10},{9,11},{10,... | collective-permute-start | bytes 356360 | tf_op jit(solution)/shard_map/ppermute | solution.py:426
  32.6 8.0 %collective-permute-start.5 = (s16[2,464,128]{2,1,0:T(8,128)(2,1)S(1)}, s16[2,464,128]{2,1,0:T(8,128)(2,1)S(1)}, u32[]{:S(2)}, u32[]{:S(2)}) collective-permute-start(s16[2,464,128]{2,1,0:T(8,128)(2,1)S(1)} %get-tuple-element.83), channel_id=1, source_target_pairs={{0,1},{1,0},{2,3},{3,2},{4,5},{5,4},{6,7},{7,6},{8,9},{9,8},{10,11... | collective-permute-start | bytes 712712 | tf_op jit(solution)/shard_map/ppermute | solution.py:426
  36.7 7.2 %collective-permute-start.14 = (s16[1,480,128]{2,1,0:T(8,128)(2,1)S(1)}, s16[1,480,128]{2,1,0:T(8,128)(2,1)S(1)}, u32[]{:S(2)}, u32[]{:S(2)}) collective-permute-start(s16[1,480,128]{2,1,0:T(8,128)(2,1)S(1)} %get-tuple-element.96), channel_id=1, source_target_pairs={{0,4},{1,5},{2,6},{3,7},{4,0},{5,1},{6,2},{7,3},{8,12},{9,13},{10,... | collective-permute-start | bytes 368648 | tf_op jit(solution)/shard_map/ppermute | solution.py:426
  38.9 4.8 %collective-permute-start.13 = (s16[1,464,128]{2,1,0:T(8,128)(2,1)S(1)}, s16[1,464,128]{2,1,0:T(8,128)(2,1)S(1)}, u32[]{:S(2)}, u32[]{:S(2)}) collective-permute-start(s16[1,464,128]{2,1,0:T(8,128)(2,1)S(1)} %get-tuple-element.95), channel_id=1, source_target_pairs={{0,2},{1,3},{2,0},{3,1},{4,6},{5,7},{6,4},{7,5},{8,10},{9,11},{10,... | collective-permute-start | bytes 356360 | tf_op jit(solution)/shard_map/ppermute | solution.py:426
